TPU v7x, 32 devices: a whole 2x2x4 slice. The times are simulated.
32 devices in a mesh: dp: 4 (over y, x), expert: 8 (over z, core).
Axes of the slice: x: 2, y: 2, z: 4, core: 2. Of those that a mesh axis runs over, the one named last changes fastest.
Arguments:
- tokens: bfloat16 [49152, 2048], P(('dp', 'expert')), may hold values from -6 to 6
- upstream: bfloat16 [49152, 2048], P(('dp', 'expert')), may hold values from -6 to 6
- counts: int32 [512], P(('dp', 'expert')), may hold values from 1 to 96, 30720 in all
- assign: int32 [2, 8], replicated, may hold values from 0 to 15
- gate_weight: bfloat16 [16, 512, 2048], P(None, 'expert', 'dp'), may hold values from -0.125 to 0.125
- up_weight: bfloat16 [16, 512, 2048], P(None, 'expert', 'dp'), may hold values from -0.125 to 0.125
- down_weight: bfloat16 [16, 512, 2048], P(None, 'expert', 'dp'), may hold values from -0.25 to 0.25
Outputs:
- token_grad: bfloat16 [49152, 2048], P(('dp', 'expert'))
- gate_weight_grad: float32 [16, 512, 2048], P(None, 'expert', 'dp')
- up_weight_grad: float32 [16, 512, 2048], P(None, 'expert', 'dp')
- down_weight_grad: float32 [16, 512, 2048], P(None, 'expert', 'dp')
Inputs may be any that keep to these rules, and one draw needn't show every extreme that they name: assign[s, i] is the expert used by copy slot i in microstep s; several slots may use the same expert. counts[j] live leading rows in micro-batch j of 96 slots; some micro-batch is full in every draw.
All inputs are finite; a program needn't handle non-finite values. No bound on the sum of `counts` on one device may be relied on, other than what follows from the above.
Results may differ from a plain program's by a relative error of at most 0.012.
Values may be sent and summed in bfloat16 or wider, within the bound.
No kernel may reach another device: no remote copies, remote signals or barrier semaphores. Data moves between devices by JAX's collectives and lax.ppermute only.
A program may use at most 128 MiB of HBM per device.

v0:
```python
import jax
import jax.numpy as jnp
from jax import lax
from jax.sharding import PartitionSpec as P


def expert_backward(
    token_rows, upstream_rows, live_rows, gate_full, up_full, down_full, grad_scale
):
    contract_last = (((1,), (1,)), ((), ()))
    contract_first = (((0,), (0,)), ((), ()))
    gate_pre = lax.dot_general(
        token_rows, gate_full, contract_last, preferred_element_type=jnp.float32
    )
    up_pre = lax.dot_general(token_rows, up_full, contract_last, preferred_element_type=jnp.float32)
    sigmoid = jax.nn.sigmoid(gate_pre)
    active = gate_pre * sigmoid
    hidden = (active * up_pre).astype(jnp.bfloat16)
    masked = jnp.where(live_rows[:, None], upstream_rows, jnp.zeros_like(upstream_rows))
    hidden_grad = lax.dot_general(
        masked, down_full, contract_last, preferred_element_type=jnp.float32
    )
    gate_grad = (hidden_grad * up_pre * sigmoid * (1.0 + gate_pre * (1.0 - sigmoid))).astype(
        jnp.bfloat16
    )
    up_grad = (hidden_grad * active).astype(jnp.bfloat16)
    input_grad = jnp.dot(gate_grad, gate_full, preferred_element_type=jnp.float32) + jnp.dot(
        up_grad, up_full, preferred_element_type=jnp.float32
    )
    gate_term = (
        lax.dot_general(gate_grad, token_rows, contract_first, preferred_element_type=jnp.float32)
        * grad_scale
    )
    up_term = (
        lax.dot_general(up_grad, token_rows, contract_first, preferred_element_type=jnp.float32)
        * grad_scale
    )
    down_term = (
        lax.dot_general(hidden, masked, contract_first, preferred_element_type=jnp.float32)
        * grad_scale
    )
    return (input_grad.astype(jnp.bfloat16), gate_term, up_term, down_term)


def flatten_slots(stacked):
    return stacked.reshape(stacked.shape[0] * stacked.shape[1], stacked.shape[2])


def fetch_expert(gate_weight, up_weight, down_weight, chosen):
    gate_picked = jnp.take(gate_weight, chosen, axis=0)
    up_picked = jnp.take(up_weight, chosen, axis=0)
    down_picked = jnp.take(down_weight, chosen, axis=0)
    received = (
        lax.all_to_all(
            flatten_slots(gate_picked), "expert", split_axis=0, concat_axis=0, tiled=True
        ),
        lax.all_to_all(flatten_slots(up_picked), "expert", split_axis=0, concat_axis=0, tiled=True),
        lax.all_to_all(
            flatten_slots(down_picked), "expert", split_axis=0, concat_axis=0, tiled=True
        ),
    )
    return (
        lax.all_gather(received[0], "dp", axis=1, tiled=True),
        lax.all_gather(received[1], "dp", axis=1, tiled=True),
        lax.all_gather(received[2], "dp", axis=1, tiled=True),
    )


def local(tokens, upstream, counts, assign, gate_weight, up_weight, down_weight):
    step_count = assign.shape[0]
    batch_count = counts.shape[0] // step_count
    block_rows = tokens.shape[0] // step_count
    batch_rows = block_rows // batch_count
    grad_scale = 1.0 / block_rows
    expert_count = gate_weight.shape[0]
    group_count = lax.axis_size("expert")
    catalog = jnp.arange(expert_count, dtype=jnp.int32)
    position = jnp.arange(batch_rows, dtype=jnp.int32)
    gate_total = jnp.zeros(gate_weight.shape, jnp.float32)
    up_total = jnp.zeros(up_weight.shape, jnp.float32)
    down_total = jnp.zeros(down_weight.shape, jnp.float32)
    produced = []
    for micro_step in range(step_count):
        current = fetch_expert(gate_weight, up_weight, down_weight, assign[micro_step])
        lower = micro_step * block_rows
        step_counts = counts[micro_step * batch_count : (micro_step + 1) * batch_count]
        live_rows = (position[None, :] < step_counts[:, None]).reshape(block_rows)
        input_grad, gate_term, up_term, down_term = expert_backward(
            tokens[lower : lower + block_rows],
            upstream[lower : lower + block_rows],
            live_rows,
            current[0],
            current[1],
            current[2],
            grad_scale,
        )
        produced.append(input_grad)
        reduced = (
            lax.psum_scatter(
                gate_term.astype(jnp.bfloat16), "dp", scatter_dimension=1, tiled=True
            ).astype(jnp.float32),
            lax.psum_scatter(
                up_term.astype(jnp.bfloat16), "dp", scatter_dimension=1, tiled=True
            ).astype(jnp.float32),
            lax.psum_scatter(
                down_term.astype(jnp.bfloat16), "dp", scatter_dimension=1, tiled=True
            ).astype(jnp.float32),
        )
        returned = (
            lax.all_to_all(
                reduced[0].astype(jnp.bfloat16), "expert", split_axis=0, concat_axis=0, tiled=True
            ).astype(jnp.float32),
            lax.all_to_all(
                reduced[1].astype(jnp.bfloat16), "expert", split_axis=0, concat_axis=0, tiled=True
            ).astype(jnp.float32),
            lax.all_to_all(
                reduced[2].astype(jnp.bfloat16), "expert", split_axis=0, concat_axis=0, tiled=True
            ).astype(jnp.float32),
        )
        selector = (assign[micro_step][:, None] == catalog[None, :]).astype(jnp.float32)

        def place_home(shard_grad):
            slotted = shard_grad.reshape(
                group_count, shard_grad.shape[0] // group_count, shard_grad.shape[1]
            )
            return jnp.einsum("ie,ifd->efd", selector, slotted, precision=lax.Precision.HIGHEST)

        gate_total = gate_total + place_home(returned[0])
        up_total = up_total + place_home(returned[1])
        down_total = down_total + place_home(returned[2])
    return (jnp.concatenate(produced, axis=0), gate_total, up_total, down_total)


def solution(mesh):
    placed = (
        P(("dp", "expert"), None),
        P(("dp", "expert"), None),
        P(("dp", "expert")),
        P(),
        P(None, "expert", "dp"),
        P(None, "expert", "dp"),
        P(None, "expert", "dp"),
    )
    return jax.shard_map(
        local,
        mesh=mesh,
        in_specs=placed,
        out_specs=(
            P(("dp", "expert"), None),
            P(None, "expert", "dp"),
            P(None, "expert", "dp"),
            P(None, "expert", "dp"),
        ),
        check_vma=False,
    )
```

profile of v0, /device:TPU:0, one launch (start us, length us, event | category | flops | bytes accessed | tf_op | source)
XLA Modules:
  0.0 518.1 jit_solution(11307466971279509695)
XLA Ops:
  13.1 21.6 %all_to_all.108 = bf16[8,64,512]{2,1,0:T(8,128)(2,1)} all-to-all(bf16[8,64,512]{2,1,0:T(8,128)(2,1)S(1)} %get-tuple-element.25), channel_id=1, replica_groups=mesh['dp'=4,'expert'=8] {'expert'}, dimensions={0} | all-to-all | bytes 1048576 | tf_op jit(solution)/shard_map/all_to_all | solution.py:57
  34.8 18.6 %all_to_all.109 = bf16[8,64,512]{2,1,0:T(8,128)(2,1)} all-to-all(bf16[8,64,512]{2,1,0:T(8,128)(2,1)S(1)} %get-tuple-element.26), channel_id=1, replica_groups=mesh['dp'=4,'expert'=8] {'expert'}, dimensions={0} | all-to-all | bytes 1048576 | tf_op jit(solution)/shard_map/all_to_all | solution.py:54
  53.5 18.4 %all_to_all.110 = bf16[8,64,512]{2,1,0:T(8,128)(2,1)} all-to-all(bf16[8,64,512]{2,1,0:T(8,128)(2,1)S(1)} %get-tuple-element.27), channel_id=1, replica_groups=mesh['dp'=4,'expert'=8] {'expert'}, dimensions={0} | all-to-all | bytes 1048576 | tf_op jit(solution)/shard_map/all_to_all | solution.py:58
  75.2 18.4 %all_to_all.111 = bf16[8,64,512]{2,1,0:T(8,128)(2,1)} all-to-all(bf16[8,64,512]{2,1,0:T(8,128)(2,1)S(1)} %get-tuple-element.31), channel_id=1, replica_groups=mesh['dp'=4,'expert'=8] {'expert'}, dimensions={0} | all-to-all | bytes 1048576 | tf_op jit(solution)/shard_map/all_to_all | solution.py:54
  93.7 18.4 %all_to_all.112 = bf16[8,64,512]{2,1,0:T(8,128)(2,1)} all-to-all(bf16[8,64,512]{2,1,0:T(8,128)(2,1)S(1)} %get-tuple-element.30), channel_id=1, replica_groups=mesh['dp'=4,'expert'=8] {'expert'}, dimensions={0} | all-to-all | bytes 1048576 | tf_op jit(solution)/shard_map/all_to_all | solution.py:57
  112.3 18.4 %all_to_all.113 = bf16[8,64,512]{2,1,0:T(8,128)(2,1)} all-to-all(bf16[8,64,512]{2,1,0:T(8,128)(2,1)S(1)} %get-tuple-element.32), channel_id=1, replica_groups=mesh['dp'=4,'expert'=8] {'expert'}, dimensions={0} | all-to-all | bytes 1048576 | tf_op jit(solution)/shard_map/all_to_all | solution.py:58
  131.0 5.6 %fusion.10 = f32[512,768]{0,1:T(8,128)} fusion(bf16[512,2048]{1,0:T(8,128)(2,1)} %all-gather.9.cloned.1.call-done, bf16[1536,2048]{1,0:T(8,128)(2,1)} %param.9), kind=kOutput, calls=%fused_computation.27 | convolution fusion | flops 1610612736 | bytes 6815744 | tf_op jit(solution)/shard_map/dot_general | solution.py:15
  143.1 5.7 %multiply_convert_fusion.7 = (bf16[768,512]{1,0:T(8,128)(2,1)S(1)}, bf16[768,512]{1,0:T(8,128)(2,1)S(1)}) fusion(f32[512,768]{0,1:T(8,128)} %fusion.8, f32[512,768]{0,1:T(8,128)} %fusion.10, bf16[512,2048]{1,0:T(8,128)(2,1)} %all-gather.7.cloned.1.call-done, bf16[1536,2048]{1,0:T(8,128)(2,1)} %param.10, pred[768]{0:T(1024)(128)(4,1)S(1)} %lt.46), kind=kOutput, calls=%fused_computation.59 | convolution fusion | flops 1617297408 | bytes 9962240 | tf_op jit(solution)/shard_map/dot_general | solution.py:20
  154.5 25.5 %all-gather.17.cloned.1.call-done = bf16[512,2048]{1,0:T(8,128)(2,1)} async-done(((bf16[512,512]{1,0:T(8,128)(2,1)}), bf16[512,2048]{1,0:T(8,128)(2,1)}) %all-gather.17.cloned.1.call-update) | async-done | bytes 2097168 | tf_op jit(solution)/shard_map/all_gather | solution.py:63
  180.0 5.5 %fusion.2 = f32[512,768]{0,1:T(8,128)} fusion(bf16[512,2048]{1,0:T(8,128)(2,1)} %all-gather.17.cloned.1.call-done, bf16[1536,2048]{1,0:T(8,128)(2,1)} %param.9), kind=kOutput, calls=%fused_computation.19 | convolution fusion | flops 1610612736 | bytes 6815744 | tf_op jit(solution)/shard_map/dot_general | solution.py:12
  185.5 31.4 %all-gather.15.cloned.1.call-done = bf16[512,2048]{1,0:T(8,128)(2,1)} async-done(((bf16[512,512]{1,0:T(8,128)(2,1)}), bf16[512,2048]{1,0:T(8,128)(2,1)}) %all-gather.15.cloned.1.call-update) | async-done | bytes 2097168 | tf_op jit(solution)/shard_map/all_gather | solution.py:64
  216.9 5.5 %fusion.4 = f32[512,768]{0,1:T(8,128)} fusion(bf16[512,2048]{1,0:T(8,128)(2,1)} %all-gather.15.cloned.1.call-done, bf16[1536,2048]{1,0:T(8,128)(2,1)} %param.9), kind=kOutput, calls=%fused_computation.21 | convolution fusion | flops 1610612736 | bytes 6815744 | tf_op jit(solution)/shard_map/dot_general | solution.py:15
  222.4 31.4 %all-gather.13.cloned.1.call-done = bf16[512,2048]{1,0:T(8,128)(2,1)} async-done(((bf16[512,512]{1,0:T(8,128)(2,1)}), bf16[512,2048]{1,0:T(8,128)(2,1)}) %all-gather.13.cloned.1.call-update) | async-done | bytes 2097168 | tf_op jit(solution)/shard_map/all_gather | solution.py:65
  253.7 5.7 %multiply_convert_fusion.6 = (bf16[768,512]{1,0:T(8,128)(2,1)S(1)}, bf16[768,512]{1,0:T(8,128)(2,1)S(1)}) fusion(f32[512,768]{0,1:T(8,128)} %fusion.2, f32[512,768]{0,1:T(8,128)} %fusion.4, bf16[512,2048]{1,0:T(8,128)(2,1)} %all-gather.13.cloned.1.call-done, bf16[1536,2048]{1,0:T(8,128)(2,1)} %param.10, pred[768]{0:T(1024)(128)(4,1)S(1)} %lt.50), kind=kOutput, calls=%fused_computation.58 | convolution fusion | flops 1617297408 | bytes 9962240 | tf_op jit(solution)/shard_map/dot_general | solution.py:20
  277.3 5.8 %multiply_convert_fusion.1 = bf16[512,2048]{1,0:T(8,128)(2,1)} fusion(bf16[1536,2048]{1,0:T(8,128)(2,1)} %param.10, pred[768]{0:T(1024)(128)(4,1)S(1)} %lt.46, f32[512,768]{0,1:T(8,128)S(1)} %copy-done.19, f32[512,768]{0,1:T(8,128)} %fusion.8), kind=kOutput, calls=%fused_computation.10 | convolution fusion | flops 1616642048 | bytes 8389376 | tf_op jit(solution)/shard_map/dot_general | solution.py:39
  283.1 9.4 %reduce-scatter.7.cloned.1.call-done = bf16[512,512]{1,0:T(8,128)(2,1)} async-done(((bf16[512,2048]{1,0:T(8,128)(2,1)}), bf16[512,512]{1,0:T(8,128)(2,1)}) %reduce-scatter.7.cloned.1.call-update) | async-done | bytes 524304 | tf_op jit(solution)/shard_map/reduce_scatter | solution.py:99
  297.3 34.2 %reduce-scatter.9.cloned.1.call-done = bf16[512,512]{1,0:T(8,128)(2,1)} async-done(((bf16[512,2048]{1,0:T(8,128)(2,1)}), bf16[512,512]{1,0:T(8,128)(2,1)}) %reduce-scatter.9.cloned.1.call-update) | async-done | bytes 524304 | tf_op jit(solution)/shard_map/reduce_scatter | solution.py:99
  337.0 5.7 %multiply_convert_fusion = bf16[512,2048]{1,0:T(8,128)(2,1)} fusion(bf16[1536,2048]{1,0:T(8,128)(2,1)} %param.10, pred[768]{0:T(1024)(128)(4,1)S(1)} %lt.50, f32[512,768]{0,1:T(8,128)} %fusion.4, f32[512,768]{0,1:T(8,128)S(1)} %copy-done.18), kind=kOutput, calls=%fused_computation.9 | convolution fusion | flops 1616642048 | bytes 8389376 | tf_op jit(solution)/shard_map/dot_general | solution.py:39
  343.4 26.9 %reduce-scatter.11.cloned.1.call-done = bf16[512,512]{1,0:T(8,128)(2,1)} async-done(((bf16[512,2048]{1,0:T(8,128)(2,1)}), bf16[512,512]{1,0:T(8,128)(2,1)}) %reduce-scatter.11.cloned.1.call-update) | async-done | bytes 524304 | tf_op jit(solution)/shard_map/reduce_scatter | solution.py:102
  378.6 30.6 %reduce-scatter.13.cloned.1.call-done = bf16[512,512]{1,0:T(8,128)(2,1)} async-done(((bf16[512,2048]{1,0:T(8,128)(2,1)}), bf16[512,512]{1,0:T(8,128)(2,1)}) %reduce-scatter.13.cloned.1.call-update) | async-done | bytes 524304 | tf_op jit(solution)/shard_map/reduce_scatter | solution.py:102
  421.0 26.4 %reduce-scatter.15.cloned.1.call-done = bf16[512,512]{1,0:T(8,128)(2,1)} async-done(((bf16[512,2048]{1,0:T(8,128)(2,1)}), bf16[512,512]{1,0:T(8,128)(2,1)}) %reduce-scatter.15.cloned.1.call-update) | async-done | bytes 524304 | tf_op jit(solution)/shard_map/reduce_scatter | solution.py:105
  452.0 5.6 %pad_maximum_fusion = bf16[1536,2048]{1,0:T(8,128)(2,1)} fusion(bf16[768,2048]{1,0:T(8,128)(2,1)} %add_convert_fusion, bf16[768,2048]{1,0:T(8,128)(2,1)S(1)} %add_convert_fusion.1), kind=kLoop, calls=%fused_computation.6 | loop fusion | flops 12582912 | bytes 12582912 | tf_op jit(solution)/shard_map/concatenate | solution.py:131
  461.8 24.5 %reduce-scatter.17.cloned.1.call-done = bf16[512,512]{1,0:T(8,128)(2,1)} async-done(((bf16[512,2048]{1,0:T(8,128)(2,1)}), bf16[512,512]{1,0:T(8,128)(2,1)}) %reduce-scatter.17.cloned.1.call-update) | async-done | bytes 524304 | tf_op jit(solution)/shard_map/reduce_scatter | solution.py:105
  498.6 8.0 %all-to-all-done.11 = bf16[8,64,512]{2,1,0:T(8,128)(2,1)} async-done(((bf16[8,64,512]{2,1,0:T(8,128)(2,1)}), bf16[8,64,512]{2,1,0:T(8,128)(2,1)}, u32[]{:S(2)}, u32[]{:S(2)}) %all-to-all-start.11) | async-done | bytes 524320 | tf_op jit(solution)/shard_map/all_to_all | solution.py:116
  (113 shorter events, 95.9 us)
Async XLA Ops:
  7.2 123.8 %all-gather.9.cloned.1.call-start = ((), (), s32[]{:S(2)}) async-start(), calls=%async_computation.19 | async-start | bytes 2621440 | tf_op jit(solution)/shard_map/all_gather | solution.py:64
  34.7 101.8 %all-gather.11.cloned.1.call-start = ((), (), s32[]{:S(2)}) async-start(), calls=%async_computation.20 | async-start | bytes 2621440 | tf_op jit(solution)/shard_map/all_gather | solution.py:63
  34.8 37.8 %copy-start.8 = (bf16[16,64,512]{2,1,0:T(8,128)(2,1)S(1)}, bf16[16,64,512]{2,1,0:T(8,128)(2,1)}, u32[]{:S(2)}) copy-start(bf16[16,64,512]{2,1,0:T(8,128)(2,1)} %param.13) | copy-start | bytes 3145732
  53.4 89.6 %all-gather.7.cloned.1.call-start = ((), (), s32[]{:S(2)}) async-start(), calls=%async_computation.18 | async-start | bytes 2621440 | tf_op jit(solution)/shard_map/all_gather | solution.py:65
  71.9 108.0 %all-gather.17.cloned.1.call-start = ((), (), s32[]{:S(2)}) async-start(), calls=%async_computation.23 | async-start | bytes 2621440 | tf_op jit(solution)/shard_map/all_gather | solution.py:63
  93.7 37.1 %copy-start.11 = (s32[16]{0:T(128)S(1)}, s32[16]{0:T(128)}, u32[]{:S(2)}) copy-start(s32[16]{0:T(128)} %param.11) | copy-start | bytes 196
  93.7 123.2 %all-gather.15.cloned.1.call-start = ((), (), s32[]{:S(2)}) async-start(), calls=%async_computation.22 | async-start | bytes 2621440 | tf_op jit(solution)/shard_map/all_gather | solution.py:64
  112.2 141.5 %all-gather.13.cloned.1.call-start = ((), (), s32[]{:S(2)}) async-start(), calls=%async_computation.21 | async-start | bytes 2621440 | tf_op jit(solution)/shard_map/all_gather | solution.py:65
  130.7 161.8 %reduce-scatter.7.cloned.1.call-start = ((), (), s32[]{:S(2)}) async-start(), calls=%async_computation.24 | async-start | bytes 2621440 | tf_op jit(solution)/shard_map/reduce_scatter | solution.py:99
  148.8 116.7 %copy-start.14 = (bf16[768,512]{1,0:T(8,128)(2,1)}, bf16[768,512]{1,0:T(8,128)(2,1)S(1)}, u32[]{:S(2)}) copy-start(bf16[768,512]{1,0:T(8,128)(2,1)S(1)} %get-tuple-element.17) | copy-start | bytes 2359300
  154.1 177.4 %reduce-scatter.9.cloned.1.call-start = ((), (), s32[]{:S(2)}) async-start(), calls=%async_computation.25 | async-start | bytes 2621440 | tf_op jit(solution)/shard_map/reduce_scatter | solution.py:99
  259.5 11.2 %copy-start.16 = (bf16[768,512]{1,0:T(8,128)(2,1)}, bf16[768,512]{1,0:T(8,128)(2,1)S(1)}, u32[]{:S(2)}) copy-start(bf16[768,512]{1,0:T(8,128)(2,1)S(1)} %get-tuple-element.19) | copy-start | bytes 2359300
  265.5 104.8 %reduce-scatter.11.cloned.1.call-start = ((), (), s32[]{:S(2)}) async-start(), calls=%async_computation.26 | async-start | bytes 2621440 | tf_op jit(solution)/shard_map/reduce_scatter | solution.py:102
  270.6 138.6 %reduce-scatter.13.cloned.1.call-start = ((), (), s32[]{:S(2)}) async-start(), calls=%async_computation.27 | async-start | bytes 2621440 | tf_op jit(solution)/shard_map/reduce_scatter | solution.py:102
  275.9 171.4 %reduce-scatter.15.cloned.1.call-start = ((), (), s32[]{:S(2)}) async-start(), calls=%async_computation.28 | async-start | bytes 2621440 | tf_op jit(solution)/shard_map/reduce_scatter | solution.py:105
  283.1 53.9 %copy-start.18 = (f32[512,768]{0,1:T(8,128)S(1)}, f32[512,768]{0,1:T(8,128)}, u32[]{:S(2)}) copy-start(f32[512,768]{0,1:T(8,128)} %fusion.2) | copy-start | bytes 4718596
  292.5 39.0 %all-to-all-start.6 = ((bf16[8,64,512]{2,1,0:T(8,128)(2,1)}), bf16[8,64,512]{2,1,0:T(8,128)(2,1)S(1)}, u32[]{:S(2)}, u32[]{:S(2)}) async-start(bf16[8,64,512]{2,1,0:T(8,128)(2,1)} %bitcast.130), calls=%async_computation.7 | async-start | bytes 1048576 | tf_op jit(solution)/shard_map/all_to_all | solution.py:110
  332.4 38.0 %all-to-all-start.7 = ((bf16[8,64,512]{2,1,0:T(8,128)(2,1)}), bf16[8,64,512]{2,1,0:T(8,128)(2,1)S(1)}, u32[]{:S(2)}, u32[]{:S(2)}) async-start(bf16[8,64,512]{2,1,0:T(8,128)(2,1)} %bitcast.131), calls=%async_computation.9 | async-start | bytes 1048576 | tf_op jit(solution)/shard_map/all_to_all | solution.py:110
  337.0 149.3 %reduce-scatter.17.cloned.1.call-start = ((), (), s32[]{:S(2)}) async-start(), calls=%async_computation.29 | async-start | bytes 2621440 | tf_op jit(solution)/shard_map/reduce_scatter | solution.py:105
  342.7 32.2 %copy-start.6 = (bf16[512,2048]{1,0:T(8,128)(2,1)S(1)}, bf16[512,2048]{1,0:T(8,128)(2,1)}, u32[]{:S(2)}) copy-start(bf16[512,2048]{1,0:T(8,128)(2,1)} %all-gather.11.cloned.1.call-done) | copy-start | bytes 6291460
  370.3 38.9 %all-to-all-start.8 = ((bf16[8,64,512]{2,1,0:T(8,128)(2,1)}), bf16[8,64,512]{2,1,0:T(8,128)(2,1)}, u32[]{:S(2)}, u32[]{:S(2)}) async-start(bf16[8,64,512]{2,1,0:T(8,128)(2,1)} %bitcast.129), calls=%async_computation.11 | async-start | bytes 1048576 | tf_op jit(solution)/shard_map/all_to_all | solution.py:113
  409.2 38.2 %all-to-all-start.9 = ((bf16[8,64,512]{2,1,0:T(8,128)(2,1)}), bf16[8,64,512]{2,1,0:T(8,128)(2,1)}, u32[]{:S(2)}, u32[]{:S(2)}) async-start(bf16[8,64,512]{2,1,0:T(8,128)(2,1)} %bitcast.127), calls=%async_computation.13 | async-start | bytes 1048576 | tf_op jit(solution)/shard_map/all_to_all | solution.py:113
  447.4 38.9 %all-to-all-start.10 = ((bf16[8,64,512]{2,1,0:T(8,128)(2,1)}), bf16[8,64,512]{2,1,0:T(8,128)(2,1)}, u32[]{:S(2)}, u32[]{:S(2)}) async-start(bf16[8,64,512]{2,1,0:T(8,128)(2,1)} %bitcast.126), calls=%async_computation.15 | async-start | bytes 1048576 | tf_op jit(solution)/shard_map/all_to_all | solution.py:116
  486.3 20.3 %all-to-all-start.11 = ((bf16[8,64,512]{2,1,0:T(8,128)(2,1)}), bf16[8,64,512]{2,1,0:T(8,128)(2,1)}, u32[]{:S(2)}, u32[]{:S(2)}) async-start(bf16[8,64,512]{2,1,0:T(8,128)(2,1)} %bitcast.128), calls=%async_computation.17 | async-start | bytes 1048576 | tf_op jit(solution)/shard_map/all_to_all | solution.py:116
  (14 other events, 36.6 us)
Sparse Core Ops, SparseCore 0:
  34.9 34.0 all-gather.8
  70.8 35.1 all-gather.10
  107.8 35.1 all-gather.6
  144.7 35.2 all-gather.16
  181.7 35.1 all-gather.14
  218.5 35.1 all-gather.12
  257.3 35.1 reduce-scatter.6
  296.3 35.1 reduce-scatter.8
  335.1 35.1 reduce-scatter.10
  374.0 35.1 reduce-scatter.12
  412.2 35.1 reduce-scatter.14
  451.0 35.1 reduce-scatter.16
where the time goes:
time: 526 us; the launch traced here: 518 us
  waiting for transfers between devices  249 us (47%)
  blocking collectives  114 us (22%)
  matrix products  84.2 us (16%)
  starting transfers between devices  28.8 us (5%)
  local copies, waits for them, and re-layouts  18.8 us (4%)
  between operations  15 us (3%)
  other arithmetic  8.07 us (2%)
    reduce_scatter x2, waiting for transfers between devices, local(): lax.psum_scatter(up_term.astype(jnp.bfloat16), 'dp', scatter_dimension=1,...  57.5 us
    reduce_scatter x2, waiting for transfers between devices, local(): lax.psum_scatter(down_term.astype(jnp.bfloat16), 'dp', scatter_dimension=...  50.8 us
    reduce_scatter x2, waiting for transfers between devices, local(): lax.psum_scatter(gate_term.astype(jnp.bfloat16), 'dp', scatter_dimension=...  43.6 us
    all_to_all x2, blocking collectives, fetch_expert(): lax.all_to_all(flatten_slots(up_picked), 'expert', split_axis=0, concat_a...  40 us
    all_to_all x2, blocking collectives, fetch_expert(): lax.all_to_all(flatten_slots(gate_picked), 'expert', split_axis=0, concat...  37 us
    all_to_all x2, blocking collectives, fetch_expert(): lax.all_to_all(flatten_slots(down_picked), 'expert', split_axis=0, concat...  36.9 us
    all_gather x2, waiting for transfers between devices, fetch_expert(): lax.all_gather(received[2], 'dp', axis=1, tiled=True)  32.4 us
    all_gather x2, waiting for transfers between devices, fetch_expert(): lax.all_gather(received[1], 'dp', axis=1, tiled=True)  31.4 us
  transfers between devices with their start and end apart: 18, of which 11 were waited for; matrix products, arithmetic and copies ran while one was open for 19% of the time, Pallas kernels for 0%

commit v1 on v0

v1 whole, which is shorter than its diff:
```python
import functools

import jax
import jax.numpy as jnp
from jax import lax
from jax.experimental import pallas as pl
from jax.experimental.pallas import tpu as pltpu
from jax.sharding import PartitionSpec as P

VMEM_BYTES = 56 * 1024 * 1024
ANY = pl.BlockSpec(memory_space=pl.ANY)
SMEM = pl.BlockSpec(memory_space=pltpu.SMEM)
VMEM = pl.BlockSpec(memory_space=pltpu.VMEM)


def exchange(value, axis, mask):
    size = lax.axis_size(axis)
    return lax.ppermute(value, axis, [(i, i ^ mask) for i in range(size)])


def axis_bits(size):
    return [1 << b for b in range(size.bit_length() - 1)]


def params(**extra):
    return pltpu.CompilerParams(vmem_limit_bytes=VMEM_BYTES, **extra)


def cost(flops, nbytes, trans=0):
    return pl.CostEstimate(flops=flops, bytes_accessed=nbytes, transcendentals=trans)


def pick_kernel(assign, gate, up, down, *rest):
    outs, sems = rest[:-1], rest[-1]
    steps, slots = assign.shape
    me = lax.axis_index("expert")
    copies = []
    for s in range(steps):
        for k in range(slots):
            chosen = assign[s, jnp.bitwise_xor(me, k)]
            for w, ref in enumerate((gate, up, down)):
                n = s * slots + k
                copy = pltpu.make_async_copy(ref.at[chosen], outs[n].at[w], sems.at[n, w])
                copy.start()
                copies.append(copy)
    for copy in copies:
        copy.wait()


def pick(assign, gate, up, down):
    steps, slots = assign.shape
    piece = jax.ShapeDtypeStruct((3,) + gate.shape[1:], gate.dtype)
    flat = pl.pallas_call(
        pick_kernel,
        out_shape=[piece] * (steps * slots),
        in_specs=[SMEM, ANY, ANY, ANY],
        out_specs=[ANY] * (steps * slots),
        scratch_shapes=[pltpu.SemaphoreType.DMA((steps * slots, 3))],
        compiler_params=params(),
        name="pick",
    )(assign, gate, up, down)
    return [flat[s * slots : (s + 1) * slots] for s in range(steps)]


def spread(own, order):
    have = {0: own}
    for bit in order:
        for j in list(have):
            have[j ^ bit] = exchange(have[j], "dp", bit)
    return have


def gather_rows(pieces, me, target, sems, first):
    copies = []
    kept = target.shape[0]
    for n, (j, row, ref) in enumerate(pieces):
        rows, columns = ref.shape[1], ref.shape[2]
        at = pl.multiple_of(jnp.bitwise_xor(me, j) * columns, columns)
        copies.append(
            pltpu.make_async_copy(
                ref.at[pl.ds(0, kept)],
                target.at[:, pl.ds(row, rows), pl.ds(at, columns)],
                sems.at[first + n],
            )
        )
    return copies


CONTRACT_LAST = (((1,), (1,)), ((), ()))
CONTRACT_FIRST = (((0,), (0,)), ((), ()))


def act_kernel(step, batches, places, counts, tokens, upstream, *rest):
    refs = rest[: len(places)]
    hidden, gate_grad, up_grad, weights, x, g, pre, sems = rest[len(places) :]
    me = lax.axis_index("dp")
    rows = x.shape[0]
    pieces = [(j, row, ref) for (j, row), ref in zip(places, refs)]
    loads = [
        pltpu.make_async_copy(tokens.at[pl.ds(step * rows, rows)], x, sems.at[0]),
        pltpu.make_async_copy(upstream.at[pl.ds(step * rows, rows)], g, sems.at[1]),
    ] + gather_rows(pieces, me, weights, sems, 2)
    for load in loads:
        load.start()
    for load in loads:
        load.wait()
    width = pre.shape[2]
    batch_rows = rows // batches
    for at in range(0, hidden.shape[1], width):
        cols = pl.ds(at, width)
        for w, left in enumerate((x, x, g)):
            pre[w] = lax.dot_general(
                left[...], weights[w, cols, :], CONTRACT_LAST, preferred_element_type=jnp.float32
            )
        for b in range(batches):
            span = pl.ds(b * batch_rows, batch_rows)
            live = (
                lax.broadcasted_iota(jnp.int32, (batch_rows, width), 0)
                < counts[step * batches + b]
            )
            gate_pre, up_pre, hidden_grad = pre[0, span, :], pre[1, span, :], pre[2, span, :]
            sigmoid = jax.nn.sigmoid(gate_pre)
            active = gate_pre * sigmoid
            kept = jnp.where(live, hidden_grad, 0.0)
            hidden[span, cols] = jnp.where(live, active * up_pre, 0.0).astype(hidden.dtype)
            gate_grad[span, cols] = (
                kept * up_pre * sigmoid * (1.0 + gate_pre * (1.0 - sigmoid))
            ).astype(gate_grad.dtype)
            up_grad[span, cols] = (kept * active).astype(up_grad.dtype)


def act(step, rows, batches, counts, tokens, upstream, placed):
    features = tokens.shape[1]
    places = tuple((j, row) for j, row, _ in placed)
    arrays = [a for _, _, a in placed]
    units = sum(a.shape[1] * a.shape[2] for a in arrays) // features
    out = jax.ShapeDtypeStruct((rows, units), tokens.dtype)
    width = min(units, 256)
    return pl.pallas_call(
        functools.partial(act_kernel, step, batches, places),
        out_shape=[out] * 3,
        in_specs=[SMEM, ANY, ANY] + [ANY] * len(arrays),
        out_specs=[VMEM] * 3,
        scratch_shapes=[
            pltpu.VMEM((3, units, features), tokens.dtype),
            pltpu.VMEM((rows, features), tokens.dtype),
            pltpu.VMEM((rows, features), tokens.dtype),
            pltpu.VMEM((3, rows, width), jnp.float32),
            pltpu.SemaphoreType.DMA((2 + len(arrays),)),
        ],
        compiler_params=params(),
        cost_estimate=cost(
            6 * rows * units * features, 2 * (2 * rows + 3 * units) * features, rows * units
        ),
        name="act",
    )(counts, tokens, upstream, *arrays)


def weight_grads_kernel(step, scale, layout, tokens, upstream, hidden, gate_grad, up_grad, *rest):
    outs = rest[: len(layout)]
    x, g, turned, stage, sems = rest[len(layout) :]
    parts, rows, width = x.shape
    me = lax.axis_index("dp")
    order = list(range(parts))[::-1]
    loads = {}
    for j in order:
        at = pl.multiple_of(jnp.bitwise_xor(me, j) * width, width)
        for n, (whole, local) in enumerate(((tokens, x), (upstream, g))):
            loads[j, n] = pltpu.make_async_copy(
                whole.at[pl.ds(step * rows, rows), pl.ds(at, width)],
                local.at[j],
                sems.at[2 * j + n],
            )
            loads[j, n].start()
    for w, ref in enumerate((gate_grad, up_grad, hidden)):
        turned[w] = ref[...].T
    stores = []
    for j in order:
        for w in range(3):
            if w == 0:
                loads[j, 0].wait()
            if w == 2:
                loads[j, 1].wait()
            right = (x, x, g)[w]
            stage[j, w] = (
                jnp.dot(turned[w], right[j], preferred_element_type=jnp.float32) * scale
            ).astype(stage.dtype)
        for n, (jj, row) in enumerate(layout):
            if jj == j:
                store = pltpu.make_async_copy(
                    stage.at[j, :, pl.ds(row, outs[n].shape[1]), :],
                    outs[n],
                    sems.at[2 * parts + n],
                )
                store.start()
                stores.append(store)
    for store in stores:
        store.wait()


def weight_grads(step, parts, scale, tokens, upstream, hidden, gate_grad, up_grad, layout, sizes):
    rows, units = hidden.shape
    features = tokens.shape[1]
    width = features // parts
    return pl.pallas_call(
        functools.partial(weight_grads_kernel, step, scale, layout),
        out_shape=[jax.ShapeDtypeStruct((3, size, width), tokens.dtype) for size in sizes],
        in_specs=[ANY, ANY, VMEM, VMEM, VMEM],
        out_specs=[ANY] * len(sizes),
        scratch_shapes=[
            pltpu.VMEM((parts, rows, width), tokens.dtype),
            pltpu.VMEM((parts, rows, width), tokens.dtype),
            pltpu.VMEM((3, units, rows), tokens.dtype),
            pltpu.VMEM((parts, 3, units, width), tokens.dtype),
            pltpu.SemaphoreType.DMA((2 * parts + len(sizes),)),
        ],
        compiler_params=params(),
        cost_estimate=cost(
            6 * rows * units * features, 2 * (2 * rows + 3 * units) * features
        ),
        name="weight_grads",
    )(tokens, upstream, hidden, gate_grad, up_grad)


def input_grad_kernel(step, places, has_base, gate_grad, up_grad, *rest):
    refs = rest[: len(places)]
    out, weights, stage, sems = rest[len(places) + has_base :]
    me = lax.axis_index("dp")
    pieces = [(j, row, ref) for (j, row), ref in zip(places, refs)]
    loads = gather_rows(pieces, me, weights, sems, 0)
    for load in loads:
        load.start()
    for load in loads:
        load.wait()
    parts, rows, width = stage.shape
    stores = []
    for n in range(parts):
        cols = pl.ds(n * width, width)
        stage[n] = (
            jnp.dot(gate_grad[...], weights[0, :, cols], preferred_element_type=jnp.float32)
            + jnp.dot(up_grad[...], weights[1, :, cols], preferred_element_type=jnp.float32)
        ).astype(stage.dtype)
        store = pltpu.make_async_copy(
            stage.at[n], out.at[pl.ds(step * rows, rows), cols], sems.at[len(places) + n]
        )
        store.start()
        stores.append(store)
    for store in stores:
        store.wait()


def input_grad(step, steps, gate_grad, up_grad, placed, features, base):
    rows, units = gate_grad.shape
    places = tuple((j, row) for j, row, _ in placed)
    arrays = [a for _, _, a in placed]
    parts = max(1, features // 512)
    more = [] if base is None else [base]
    return pl.pallas_call(
        functools.partial(input_grad_kernel, step, places, len(more)),
        out_shape=jax.ShapeDtypeStruct((steps * rows, features), gate_grad.dtype),
        in_specs=[VMEM, VMEM] + [ANY] * (len(arrays) + len(more)),
        out_specs=ANY,
        scratch_shapes=[
            pltpu.VMEM((2, units, features), gate_grad.dtype),
            pltpu.VMEM((parts, rows, features // parts), gate_grad.dtype),
            pltpu.SemaphoreType.DMA((len(arrays) + parts,)),
        ],
        input_output_aliases={2 + len(arrays): 0} if more else {},
        compiler_params=params(),
        cost_estimate=cost(4 * rows * units * features, 2 * (rows + 2 * units) * features),
        name="input_grad",
    )(gate_grad, up_grad, *arrays, *more)


def collect(parts, order):
    have = dict(parts)
    for bit in order:
        for j in [j for j in have if j & bit]:
            got = exchange(have.pop(j), "dp", bit)
            mine = have[j ^ bit]
            have[j ^ bit] = (mine.astype(jnp.float32) + got.astype(jnp.float32)).astype(mine.dtype)
    return have[0]


def place_kernel(assign, *rest):
    steps, slots = assign.shape
    pieces = rest[: steps * slots]
    outs = rest[steps * slots :]
    me = lax.axis_index("expert")
    expert = pl.program_id(0)
    for out in outs:
        out[...] = jnp.zeros_like(out)
    for s in range(steps):
        for k in range(slots):

            @pl.when(assign[s, jnp.bitwise_xor(me, k)] == expert)
            def _():
                for w, out in enumerate(outs):
                    out[0] += pieces[s * slots + k][w].astype(jnp.float32)


def place(assign, home, experts):
    _, units, width = home[0].shape
    out = jax.ShapeDtypeStruct((experts, units, width), jnp.float32)
    return pl.pallas_call(
        place_kernel,
        grid=(experts,),
        out_shape=[out] * 3,
        in_specs=[SMEM] + [VMEM] * len(home),
        out_specs=[pl.BlockSpec((1, units, width), lambda e: (e, 0, 0))] * 3,
        compiler_params=params(),
        name="place",
    )(assign, *home)


def local(tokens, upstream, counts, assign, gate_weight, up_weight, down_weight):
    steps, slots = assign.shape
    rows = tokens.shape[0] // steps
    batches = counts.shape[0] // steps
    features = tokens.shape[1]
    experts, chunk, _ = gate_weight.shape
    parts = lax.axis_size("dp")
    bits = axis_bits(parts)
    orders = (bits, bits[::-1])
    even = list(range(0, slots, 2))
    near = [k for k in even if k not in (0, slots // 2)]
    staged = [g for g in ([0], near, [slots // 2]) if g]
    half_units = slots // 2 * chunk

    picked = pick(assign, gate_weight, up_weight, down_weight)
    token_grad = None
    home = [[None] * slots for _ in range(steps)]
    for s in range(steps):
        groups = staged if s == 0 else [even]
        received = [
            picked[s][k] if k == 0 else exchange(picked[s][k], "expert", k) for k in range(slots)
        ]
        placed = []
        for half in range(2):
            for group in groups:
                row = half * half_units + sum(
                    len(before) for before in groups[: groups.index(group)]
                ) * chunk
                mine = [received[k ^ half] for k in group]
                own = mine[0] if len(mine) == 1 else jnp.concatenate(mine, axis=1)
                placed += [(j, row, a) for j, a in spread(own, orders[half]).items()]
        hidden, gate_grad, up_grad = act(s, rows, batches, counts, tokens, upstream, placed)
        kept = [k for group in groups for k in group]
        groups_back = [kept] if s == 0 else [[k] for k in kept]
        if s > 0:
            groups_back = [[k] for k in kept if k == slots // 2] + [
                [k] for k in kept if k not in (0, slots // 2)
            ] + [[0]]
        layout, sizes, names = [], [], []
        for group in groups_back:
            for half in range(2):
                for j in range(parts):
                    layout.append((j, half * half_units + kept.index(group[0]) * chunk))
                    sizes.append(len(group) * chunk)
                    names.append((tuple(group), half, j))
        produced = weight_grads(
            s, parts, 1.0 / rows, tokens, upstream, hidden, gate_grad, up_grad,
            tuple(layout), tuple(sizes),
        )
        by_name = dict(zip(names, produced))
        token_grad = input_grad(s, steps, gate_grad, up_grad, placed, features, token_grad)
        for group in groups_back:
            for half in range(2):
                total = collect(
                    {j: by_name[tuple(group), half, j] for j in range(parts)}, orders[half]
                )
                for n, k in enumerate(group):
                    back = total[:, n * chunk : (n + 1) * chunk]
                    k = k ^ half
                    home[s][k] = back if k == 0 else exchange(back, "expert", k)
    totals = place(assign, [piece for step in home for piece in step], experts)
    return (token_grad, *totals)


def solution(mesh):
    placed = (
        P(("dp", "expert"), None),
        P(("dp", "expert"), None),
        P(("dp", "expert")),
        P(),
        P(None, "expert", "dp"),
        P(None, "expert", "dp"),
        P(None, "expert", "dp"),
    )
    return jax.shard_map(
        local,
        mesh=mesh,
        in_specs=placed,
        out_specs=(
            P(("dp", "expert"), None),
            P(None, "expert", "dp"),
            P(None, "expert", "dp"),
            P(None, "expert", "dp"),
        ),
        check_vma=False,
    )
```

time: 526 us -> 520 us (0.989); the launches traced: 518 us -> 520 us
  Pallas kernels: 0 us -> 169 us
  blocking collectives: 114 us -> 0 us
  matrix products: 84.2 us -> 0 us
  starting transfers between devices: 28.8 us -> 112 us
  waiting for transfers between devices: 249 us -> 226 us
  local copies, waits for them, and re-layouts: 18.8 us -> 5.26 us
  between operations: 15 us -> 1.79 us
    ppermute x0 -> x82, waiting for transfers between devices: none -> 226 us  [exchange(): return lax.ppermute(value, axis, [(i, i ^ mask) for i in range(size)])]
    pallas_call x0 -> x8, Pallas kernels: none -> 169 us  [the longest x1 97.5 us: pick(): pl.pallas_call(pick_kernel, out_shape=[piece] * (steps * slots), in_specs...]
    reduce_scatter x6 -> x0, waiting for transfers between devices: 152 us -> none  [the longest x2 57.5 us: local(): lax.psum_scatter(up_term.astype(jnp.bfloat16), 'dp', scatter_dimension=1,...]
    all_to_all x6 -> x0, blocking collectives: 114 us -> none  [the longest x2 40 us: fetch_expert(): lax.all_to_all(flatten_slots(up_picked), 'expert', split_axis=0, concat_a...]
    ppermute x0 -> x82, starting transfers between devices: none -> 112 us  [exchange(): return lax.ppermute(value, axis, [(i, i ^ mask) for i in range(size)])]
    all_gather x6 -> x0, waiting for transfers between devices: 89.2 us -> none  [the longest x2 32.4 us: fetch_expert(): lax.all_gather(received[2], 'dp', axis=1, tiled=True)]
    dot_general x22 -> x0, matrix products: 84.2 us -> none  [the longest x2 11.5 us: expert_backward(): lax.dot_general(hidden, masked, contract_first, preferred_element_type=jn...]
    all_to_all x6 -> x0, starting transfers between devices: 28.1 us -> none  [the longest x2 9.5 us: local(): lax.all_to_all(reduced[2].astype(jnp.bfloat16), 'expert', split_axis=0, c...]
  transfers between devices with their start and end apart: 18 -> 82, of which waited for: 11 -> 36; matrix products, arithmetic and copies ran while one was open for 19% -> 1% of each run, Pallas kernels for 0% -> 12%
where the time goes in v1:
time: 520 us
  waiting for transfers between devices  226 us (43%)
  Pallas kernels  169 us (32%)
  starting transfers between devices  112 us (22%)
  other arithmetic  5.36 us (1%)
  local copies, waits for them, and re-layouts  5.26 us (1%)
    ppermute x82, waiting for transfers between devices, exchange(): return lax.ppermute(value, axis, [(i, i ^ mask) for i in range(size)])  226 us
    ppermute x82, starting transfers between devices, exchange(): return lax.ppermute(value, axis, [(i, i ^ mask) for i in range(size)])  112 us
    pallas_call x1, Pallas kernels, pick(): pl.pallas_call(pick_kernel, out_shape=[piece] * (steps * slots), in_specs...  97.5 us
    pallas_call x2, Pallas kernels, act(): pl.pallas_call(functools.partial(act_kernel, step, batches, places), out_...  24.4 us
    pallas_call x2, Pallas kernels, weight_grads(): pl.pallas_call(functools.partial(weight_grads_kernel, step, scale, layout...  20.9 us
    pallas_call x2, Pallas kernels, input_grad(): pl.pallas_call(functools.partial(input_grad_kernel, step, places, len(mor...  16.3 us
  transfers between devices with their start and end apart: 82, of which 36 were waited for; matrix products, arithmetic and copies ran while one was open for 1% of the time, Pallas kernels for 12%

profile of v1, /device:TPU:0, one launch (start us, length us, event | category | flops | bytes accessed | tf_op | source)
XLA Modules:
  0.0 519.6 jit_solution(11910941012172590230)
XLA Ops:
  0.6 97.5 %pick.1 = (bf16[3,64,512]{2,1,0:T(8,128)(2,1)}, bf16[3,64,512]{2,1,0:T(8,128)(2,1)}, bf16[3,64,512]{2,1,0:T(8,128)(2,1)}, bf16[3,64,512]{2,1,0:T(8,128)(2,1)}, b...) custom-call(s32[2,8]{1,0:T(2,128)} %assign.3, ...), custom_call_target="tpu_custom_call" | custom-call | tf_op jit(solution)/shard_map/pick/pallas_call | solution.py:53
  110.7 8.0 %collective-permute-done.1 = bf16[3,64,512]{2,1,0:T(8,128)(2,1)S(1)} collective-permute-done((bf16[3,64,512]{2,1,0:T(8,128)(2,1)}, bf16[3,64,512]{2,1,0:T(8,128)(2,1)S(1)}, u32[]{:S(2)}, u32[]{:S(2)}) %collective-permute-start.1) | collective-permute-done | bytes 196640 | tf_op jit(solution)/shard_map/ppermute | solution.py:18
  120.3 9.5 %collective-permute-start.9 = (bf16[3,64,512]{2,1,0:T(8,128)(2,1)}, bf16[3,64,512]{2,1,0:T(8,128)(2,1)S(1)}, u32[]{:S(2)}, u32[]{:S(2)}) collective-permute-start(bf16[3,64,512]{2,1,0:T(8,128)(2,1)} %get-tuple-element.76), channel_id=1, source_target_pairs={{0,7},{1,6},{2,5},{3,4},{4,3},{5,2},{6,1},{7,0},{8,15},{9,14},{10,... | collective-permute-start | bytes 589832 | tf_op jit(solution)/shard_map/ppermute | solution.py:18
  143.1 16.9 %collective-permute-done.21.rest_8_ = bf16[3,64,512]{2,1,0:T(8,128)(2,1)S(1)} collective-permute-done((bf16[3,64,512]{2,1,0:T(8,128)(2,1)}, bf16[3,64,512]{2,1,0:T(8,128)(2,1)S(1)}, u32[]{:S(2)}, u32[]{:S(2)}) %collective-permute-start.21) | collective-permute-done | bytes 196640 | tf_op jit(solution)/shard_map/ppermute | solution.py:18
  163.1 9.2 %collective-permute-done.34.rest_20_ = bf16[3,64,512]{2,1,0:T(8,128)(2,1)S(1)} collective-permute-done((bf16[3,64,512]{2,1,0:T(8,128)(2,1)}, bf16[3,64,512]{2,1,0:T(8,128)(2,1)S(1)}, u32[]{:S(2)}, u32[]{:S(2)}) %collective-permute-start.34) | collective-permute-done | bytes 196640 | tf_op jit(solution)/shard_map/ppermute | solution.py:18
  177.9 12.1 %collective-permute-done.27.rest_14_ = bf16[3,64,512]{2,1,0:T(8,128)(2,1)S(1)} collective-permute-done((bf16[3,64,512]{2,1,0:T(8,128)(2,1)S(1)}, bf16[3,64,512]{2,1,0:T(8,128)(2,1)S(1)}, u32[]{:S(2)}, u32[]{:S(2)}) %collective-permute-start.27) | collective-permute-done | bytes 196640 | tf_op jit(solution)/shard_map/ppermute | solution.py:18
  215.8 8.2 %collective-permute-done.37.rest_23_ = bf16[3,64,512]{2,1,0:T(8,128)(2,1)S(1)} collective-permute-done((bf16[3,64,512]{2,1,0:T(8,128)(2,1)S(1)}, bf16[3,64,512]{2,1,0:T(8,128)(2,1)S(1)}, u32[]{:S(2)}, u32[]{:S(2)}) %collective-permute-start.37) | collective-permute-done | bytes 196640 | tf_op jit(solution)/shard_map/ppermute | solution.py:18
  227.7 12.3 %act.3 = (bf16[768,512]{1,0:T(8,128)(2,1)}, bf16[768,512]{1,0:T(8,128)(2,1)}, bf16[768,512]{1,0:T(8,128)(2,1)}) custom-call(s32[16]{0:T(128)} %counts.3, bf16[1536,2048]{1,0:T(8,128)(2,1)} %tokens.7, bf16[1536,2048]{1,0:T(8,128)(2,1)} %upstream.7, bf16[3,64,512]{2,1,0:T(8,128)(2,1)} %get-tuple-element.79.rest_0_, bf16[3,64,512]{2,1,0:T(8,128)(2,1)} %copy-done.19, ...), custom_call_target="tpu_custom_call" | custom-call | flops 4831838208 | bytes 12582912 | tf_op jit(solution)/shard_map/act/pallas_call | solution.py:139
  240.0 10.3 %weight_grads.2 = (bf16[3,256,512]{2,1,0:T(8,128)(2,1)}, bf16[3,256,512]{2,1,0:T(8,128)(2,1)}, bf16[3,256,512]{2,1,0:T(8,128)(2,1)}, bf16[3,256,512]{2,1,0:T(8,1...) custom-call(bf16[1536,2048]{1,0:T(8,128)(2,1)} %tokens.7, ...), custom_call_target="tpu_custom_call" | custom-call | flops 4831838208 | bytes 12582912 | tf_op jit(solution)/shard_map/weight_grads/pallas_call | solution.py:205
  254.9 8.1 %input_grad.2.rest_8_ = bf16[1536,2048]{1,0:T(8,128)(2,1)} custom-call(bf16[768,512]{1,0:T(8,128)(2,1)} %get-tuple-element.87.gate_grad, bf16[768,512]{1,0:T(8,128)(2,1)} %get-tuple-element.88.up_grad, bf16[3,64,512]{2,1,0:T(8,128)(2,1)} %get-tuple-element.79.rest_0_, bf16[3,64,512]{2,1,0:T(8,128)(2,1)} %copy-done.19, bf16[3,64,512]{2,1,0:T(8,128)(2,1)} %copy-done.18, ...), custom_call_target="tpu_custom_call" | custom-call | flops 3221225472 | bytes 7340032 | tf_op jit(solution)/shard_map/input_grad/pallas_call | solution.py:258
  263.1 7.9 %collective-permute-done.39 = bf16[3,256,512]{2,1,0:T(8,128)(2,1)S(1)} collective-permute-done((bf16[3,256,512]{2,1,0:T(8,128)(2,1)}, bf16[3,256,512]{2,1,0:T(8,128)(2,1)S(1)}, u32[]{:S(2)}, u32[]{:S(2)}) %collective-permute-start.39) | collective-permute-done | bytes 786464 | tf_op jit(solution)/shard_map/ppermute | solution.py:18
  275.6 12.2 %collective-permute-done.11.rest_6_ = bf16[3,256,512]{2,1,0:T(8,128)(2,1)S(1)} collective-permute-done((bf16[3,256,512]{2,1,0:T(8,128)(2,1)S(1)}, bf16[3,256,512]{2,1,0:T(8,128)(2,1)S(1)}, u32[]{:S(2)}, u32[]{:S(2)}) %collective-permute-start.11) | collective-permute-done | bytes 786464 | tf_op jit(solution)/shard_map/ppermute | solution.py:18
  289.4 15.3 %collective-permute-done.12.rest_7_ = bf16[3,256,512]{2,1,0:T(8,128)(2,1)S(1)} collective-permute-done((bf16[3,256,512]{2,1,0:T(8,128)(2,1)S(1)}, bf16[3,256,512]{2,1,0:T(8,128)(2,1)S(1)}, u32[]{:S(2)}, u32[]{:S(2)}) %collective-permute-start.12) | collective-permute-done | bytes 786464 | tf_op jit(solution)/shard_map/ppermute | solution.py:18
  305.6 12.1 %act.2 = (bf16[768,512]{1,0:T(8,128)(2,1)}, bf16[768,512]{1,0:T(8,128)(2,1)}, bf16[768,512]{1,0:T(8,128)(2,1)}) custom-call(s32[16]{0:T(128)} %counts.3, bf16[1536,2048]{1,0:T(8,128)(2,1)} %tokens.7, bf16[1536,2048]{1,0:T(8,128)(2,1)} %upstream.7, bf16[3,256,512]{2,1,0:T(8,128)(2,1)} %copy-done, bf16[3,256,512]{2,1,0:T(8,128)(2,1)} %copy-done.2, ...), custom_call_target="tpu_custom_call" | custom-call | flops 4831838208 | bytes 12582912 | tf_op jit(solution)/shard_map/act/pallas_call | solution.py:139
  317.7 10.6 %weight_grads.3 = (bf16[3,64,512]{2,1,0:T(8,128)(2,1)}, bf16[3,64,512]{2,1,0:T(8,128)(2,1)}, bf16[3,64,512]{2,1,0:T(8,128)(2,1)}, bf16[3,64,512]{2,1,0:T(8,128)(...) custom-call(bf16[1536,2048]{1,0:T(8,128)(2,1)} %tokens.7, ...), custom_call_target="tpu_custom_call" | custom-call | flops 4831838208 | bytes 12582912 | tf_op jit(solution)/shard_map/weight_grads/pallas_call | solution.py:205
  330.5 8.1 %input_grad.3 = bf16[1536,2048]{1,0:T(8,128)(2,1)} custom-call(bf16[768,512]{1,0:T(8,128)(2,1)} %get-tuple-element.77.gate_grad, bf16[768,512]{1,0:T(8,128)(2,1)} %get-tuple-element.78.up_grad, bf16[3,256,512]{2,1,0:T(8,128)(2,1)} %copy-done, bf16[3,256,512]{2,1,0:T(8,128)(2,1)} %copy-done.2, ...), custom_call_target="tpu_custom_call", output_to_operand_aliasing={{}: (10, {})} | custom-call | flops 3221225472 | bytes 7340032 | tf_op jit(solution)/shard_map/input_grad/pallas_call | solution.py:258
  362.7 6.6 %collective-permute-done.71 = bf16[3,64,512]{2,1,0:T(8,128)(2,1)S(1)} collective-permute-done((bf16[3,64,512]{2,1,0:T(8,128)(2,1)S(1)}, bf16[3,64,512]{2,1,0:T(8,128)(2,1)S(1)}, u32[]{:S(2)}, u32[]{:S(2)}) %collective-permute-start.71) | collective-permute-done | bytes 196640 | tf_op jit(solution)/shard_map/ppermute | solution.py:18
  370.2 6.1 %collective-permute-done.75 = bf16[3,64,512]{2,1,0:T(8,128)(2,1)S(1)} collective-permute-done((bf16[3,64,512]{2,1,0:T(8,128)(2,1)S(1)}, bf16[3,64,512]{2,1,0:T(8,128)(2,1)S(1)}, u32[]{:S(2)}, u32[]{:S(2)}) %collective-permute-start.75) | collective-permute-done | bytes 196640 | tf_op jit(solution)/shard_map/ppermute | solution.py:18
  424.4 8.5 %collective-permute-done.80 = bf16[3,64,512]{2,1,0:T(8,128)(2,1)S(1)} collective-permute-done((bf16[3,64,512]{2,1,0:T(8,128)(2,1)S(1)}, bf16[3,64,512]{2,1,0:T(8,128)(2,1)S(1)}, u32[]{:S(2)}, u32[]{:S(2)}) %collective-permute-start.80) | collective-permute-done | bytes 196640 | tf_op jit(solution)/shard_map/ppermute | solution.py:18
  456.0 16.9 %collective-permute-done.73.rest_13_ = bf16[3,64,512]{2,1,0:T(8,128)(2,1)S(1)} collective-permute-done((bf16[3,64,512]{2,1,0:T(8,128)(2,1)S(1)}, bf16[3,64,512]{2,1,0:T(8,128)(2,1)S(1)}, u32[]{:S(2)}, u32[]{:S(2)}) %collective-permute-start.73) | collective-permute-done | bytes 196640 | tf_op jit(solution)/shard_map/ppermute | solution.py:18
  480.0 11.7 %collective-permute-start.48 = (bf16[3,64,512]{2,1,0:T(8,128)(2,1)S(1)}, bf16[3,64,512]{2,1,0:T(8,128)(2,1)S(1)}, u32[]{:S(2)}, u32[]{:S(2)}) collective-permute-start(bf16[3,64,512]{2,1,0:T(8,128)(2,1)S(1)} %get-tuple-element.135), channel_id=1, source_target_pairs={{0,5},{1,4},{2,7},{3,6},{4,1},{5,0},{6,3},{7,2},{8,13},{9,12},{10,... | collective-permute-start | bytes 589832 | tf_op jit(solution)/shard_map/ppermute | solution.py:18
  492.1 9.7 %collective-permute-done.47.rest_4_ = bf16[3,64,512]{2,1,0:T(8,128)(2,1)S(1)} collective-permute-done((bf16[3,64,512]{2,1,0:T(8,128)(2,1)S(1)}, bf16[3,64,512]{2,1,0:T(8,128)(2,1)S(1)}, u32[]{:S(2)}, u32[]{:S(2)}) %collective-permute-start.47) | collective-permute-done | bytes 196640 | tf_op jit(solution)/shard_map/ppermute | solution.py:18
  502.6 6.1 %collective-permute-done.48.rest_5_ = bf16[3,64,512]{2,1,0:T(8,128)(2,1)S(1)} collective-permute-done((bf16[3,64,512]{2,1,0:T(8,128)(2,1)S(1)}, bf16[3,64,512]{2,1,0:T(8,128)(2,1)S(1)}, u32[]{:S(2)}, u32[]{:S(2)}) %collective-permute-start.48) | collective-permute-done | bytes 196640 | tf_op jit(solution)/shard_map/ppermute | solution.py:18
  509.5 9.9 %place.1 = (f32[16,64,512]{2,1,0:T(8,128)}, f32[16,64,512]{2,1,0:T(8,128)}, f32[16,64,512]{2,1,0:T(8,128)}) custom-call(s32[2,8]{1,0:T(2,128)} %assign.3, bf16[3,64,512]{2,1,0:T(8,128)(2,1)} %get-tuple-element.141.rest_0_, bf16[3,64,512]{2,1,0:T(8,128)(2,1)} %copy-done.48, bf16[3,64,512]{2,1,0:T(8,128)(2,1)} %copy-done.44, bf16[3,64,512]{2,1,0:T(8,128)(2,1)} %copy-done.47, ...), custom_call_target="tpu_custom_call" | custom-call | tf_op jit(solution)/shard_map/place/pallas_call | solution.py:305
  (344 shorter events, 183.9 us)
Async XLA Ops:
  131.2 28.7 %collective-permute-start.21 = (bf16[3,64,512]{2,1,0:T(8,128)(2,1)}, bf16[3,64,512]{2,1,0:T(8,128)(2,1)S(1)}, u32[]{:S(2)}, u32[]{:S(2)}) collective-permute-start(bf16[3,64,512]{2,1,0:T(8,128)(2,1)} %get-tuple-element.82), channel_id=1, source_target_pairs={{0,4},{1,5},{2,6},{3,7},{4,0},{5,1},{6,2},{7,3},{8,12},{9,13},{10,... | collective-permute-start | bytes 589832 | tf_op jit(solution)/shard_map/ppermute | solution.py:18
  131.2 28.7 %collective-permute-start.25 = (bf16[3,64,512]{2,1,0:T(8,128)(2,1)}, bf16[3,64,512]{2,1,0:T(8,128)(2,1)S(1)}, u32[]{:S(2)}, u32[]{:S(2)}) collective-permute-start(bf16[3,64,512]{2,1,0:T(8,128)(2,1)} %get-tuple-element.83), channel_id=1, source_target_pairs={{0,1},{1,0},{2,3},{3,2},{4,5},{5,4},{6,7},{7,6},{8,9},{9,8},{10,11... | collective-permute-start | bytes 589832 | tf_op jit(solution)/shard_map/ppermute | solution.py:18
  131.3 30.2 %collective-permute-start.30 = (bf16[3,64,512]{2,1,0:T(8,128)(2,1)}, bf16[3,64,512]{2,1,0:T(8,128)(2,1)S(1)}, u32[]{:S(2)}, u32[]{:S(2)}) collective-permute-start(bf16[3,64,512]{2,1,0:T(8,128)(2,1)} %get-tuple-element.85), channel_id=1, source_target_pairs={{0,7},{1,6},{2,5},{3,4},{4,3},{5,2},{6,1},{7,0},{8,15},{9,14},{10,... | collective-permute-start | bytes 589832 | tf_op jit(solution)/shard_map/ppermute | solution.py:18
  139.2 34.6 %collective-permute-start.14 = (bf16[3,64,512]{2,1,0:T(8,128)(2,1)}, bf16[3,64,512]{2,1,0:T(8,128)(2,1)S(1)}, u32[]{:S(2)}, u32[]{:S(2)}) collective-permute-start(bf16[3,64,512]{2,1,0:T(8,128)(2,1)} %get-tuple-element.79.rest_0_), channel_id=1, source_target_pairs={{0,16},{8,24},{16,0},{24,8},{1,17},{9,25},{17,1},{25,9},{2,18},{10... | collective-permute-start | bytes 589832 | tf_op jit(solution)/shard_map/ppermute | solution.py:18
  141.6 33.8 %collective-permute-start.13 = (bf16[3,64,512]{2,1,0:T(8,128)(2,1)}, bf16[3,64,512]{2,1,0:T(8,128)(2,1)S(1)}, u32[]{:S(2)}, u32[]{:S(2)}) collective-permute-start(bf16[3,64,512]{2,1,0:T(8,128)(2,1)} %get-tuple-element.79.rest_0_), channel_id=1, source_target_pairs={{0,8},{8,0},{16,24},{24,16},{1,9},{9,1},{17,25},{25,17},{2,10},{10... | collective-permute-start | bytes 589832 | tf_op jit(solution)/shard_map/ppermute | solution.py:18
  172.3 35.5 %collective-permute-start.31 = (bf16[3,128,512]{2,1,0:T(8,128)(2,1)S(1)}, bf16[3,128,512]{2,1,0:T(8,128)(2,1)S(1)}, u32[]{:S(2)}, u32[]{:S(2)}) collective-permute-start(bf16[3,128,512]{2,1,0:T(8,128)(2,1)S(1)} %constant_dynamic-update-slice_fusion.10.rest_16_), channel_id=1, source_target_pairs={{0,16},{8,24},{16,0},{24,8},{1,17},{9,25},{17,1},{25,9},{2,18},{10... | collective-permute-start | bytes 1179656 | tf_op jit(solution)/shard_map/ppermute | solution.py:18
  173.8 34.7 %collective-permute-start.18 = (bf16[3,128,512]{2,1,0:T(8,128)(2,1)S(1)}, bf16[3,128,512]{2,1,0:T(8,128)(2,1)S(1)}, u32[]{:S(2)}, u32[]{:S(2)}) collective-permute-start(bf16[3,128,512]{2,1,0:T(8,128)(2,1)S(1)} %constant_dynamic-update-slice_fusion.8.rest_4_), channel_id=1, source_target_pairs={{0,8},{8,0},{16,24},{24,16},{1,9},{9,1},{17,25},{25,17},{2,10},{10... | collective-permute-start | bytes 1179656 | tf_op jit(solution)/shard_map/ppermute | solution.py:18
  224.0 29.8 %collective-permute-start.3 = (bf16[3,256,512]{2,1,0:T(8,128)(2,1)S(1)}, bf16[3,256,512]{2,1,0:T(8,128)(2,1)S(1)}, u32[]{:S(2)}, u32[]{:S(2)}) collective-permute-start(bf16[3,256,512]{2,1,0:T(8,128)(2,1)S(1)} %constant_dynamic-update-slice_fusion.rest_0_), channel_id=1, source_target_pairs={{0,8},{8,0},{16,24},{24,16},{1,9},{9,1},{17,25},{25,17},{2,10},{10... | collective-permute-start | bytes 2359304 | tf_op jit(solution)/shard_map/ppermute | solution.py:18
  225.5 28.9 %collective-permute-start.10 = (bf16[3,256,512]{2,1,0:T(8,128)(2,1)S(1)}, bf16[3,256,512]{2,1,0:T(8,128)(2,1)S(1)}, u32[]{:S(2)}, u32[]{:S(2)}) collective-permute-start(bf16[3,256,512]{2,1,0:T(8,128)(2,1)S(1)} %constant_dynamic-update-slice_fusion.4.rest_4_), channel_id=1, source_target_pairs={{0,16},{8,24},{16,0},{24,8},{1,17},{9,25},{17,1},{25,9},{2,18},{10... | collective-permute-start | bytes 2359304 | tf_op jit(solution)/shard_map/ppermute | solution.py:18
  252.4 35.5 %collective-permute-start.11 = (bf16[3,256,512]{2,1,0:T(8,128)(2,1)S(1)}, bf16[3,256,512]{2,1,0:T(8,128)(2,1)S(1)}, u32[]{:S(2)}, u32[]{:S(2)}) collective-permute-start(bf16[3,256,512]{2,1,0:T(8,128)(2,1)S(1)} %constant_dynamic-update-slice_fusion.4.rest_4_), channel_id=1, source_target_pairs={{0,8},{8,0},{16,24},{24,16},{1,9},{9,1},{17,25},{25,17},{2,10},{10... | collective-permute-start | bytes 2359304 | tf_op jit(solution)/shard_map/ppermute | solution.py:18
  253.9 35.5 %collective-permute-start.5 = (bf16[3,256,512]{2,1,0:T(8,128)(2,1)S(1)}, bf16[3,256,512]{2,1,0:T(8,128)(2,1)S(1)}, u32[]{:S(2)}, u32[]{:S(2)}) collective-permute-start(bf16[3,256,512]{2,1,0:T(8,128)(2,1)S(1)} %collective-permute-done.3.rest_1_), channel_id=1, source_target_pairs={{0,16},{8,24},{16,0},{24,8},{1,17},{9,25},{17,1},{25,9},{2,18},{10... | collective-permute-start | bytes 2359304 | tf_op jit(solution)/shard_map/ppermute | solution.py:18
  254.4 50.3 %collective-permute-start.12 = (bf16[3,256,512]{2,1,0:T(8,128)(2,1)S(1)}, bf16[3,256,512]{2,1,0:T(8,128)(2,1)S(1)}, u32[]{:S(2)}, u32[]{:S(2)}) collective-permute-start(bf16[3,256,512]{2,1,0:T(8,128)(2,1)S(1)} %collective-permute-done.10.rest_5_), channel_id=1, source_target_pairs={{0,8},{8,0},{16,24},{24,16},{1,9},{9,1},{17,25},{25,17},{2,10},{10... | collective-permute-start | bytes 2359304 | tf_op jit(solution)/shard_map/ppermute | solution.py:18
  271.9 163.1 %collective-permute-start.38 = (bf16[3,256,512]{2,1,0:T(8,128)(2,1)}, bf16[3,256,512]{2,1,0:T(8,128)(2,1)S(1)}, u32[]{:S(2)}, u32[]{:S(2)}) collective-permute-start(bf16[3,256,512]{2,1,0:T(8,128)(2,1)} %get-tuple-element.91), channel_id=1, source_target_pairs={{0,8},{8,0},{16,24},{24,16},{1,9},{9,1},{17,25},{25,17},{2,10},{10... | collective-permute-start | bytes 2359304 | tf_op jit(solution)/shard_map/ppermute | solution.py:18
  274.0 64.6 %collective-permute-start.42 = (bf16[3,256,512]{2,1,0:T(8,128)(2,1)}, bf16[3,256,512]{2,1,0:T(8,128)(2,1)}, u32[]{:S(2)}, u32[]{:S(2)}) collective-permute-start(bf16[3,256,512]{2,1,0:T(8,128)(2,1)} %get-tuple-element.97), channel_id=1, source_target_pairs={{0,16},{8,24},{16,0},{24,8},{1,17},{9,25},{17,1},{25,9},{2,18},{10... | collective-permute-start | bytes 2359304 | tf_op jit(solution)/shard_map/ppermute | solution.py:18
  287.9 147.6 %collective-permute-start.40 = (bf16[3,256,512]{2,1,0:T(8,128)(2,1)S(1)}, bf16[3,256,512]{2,1,0:T(8,128)(2,1)S(1)}, u32[]{:S(2)}, u32[]{:S(2)}) collective-permute-start(bf16[3,256,512]{2,1,0:T(8,128)(2,1)S(1)} %add_convert_fusion.4), channel_id=1, source_target_pairs={{0,16},{8,24},{16,0},{24,8},{1,17},{9,25},{17,1},{25,9},{2,18},{10... | collective-permute-start | bytes 2359304 | tf_op jit(solution)/shard_map/ppermute | solution.py:18
  328.9 55.2 %collective-permute-start.54 = (bf16[3,64,512]{2,1,0:T(8,128)(2,1)}, bf16[3,64,512]{2,1,0:T(8,128)(2,1)S(1)}, u32[]{:S(2)}, u32[]{:S(2)}) collective-permute-start(bf16[3,64,512]{2,1,0:T(8,128)(2,1)} %get-tuple-element.104), channel_id=1, source_target_pairs={{0,16},{8,24},{16,0},{24,8},{1,17},{9,25},{17,1},{25,9},{2,18},{10... | collective-permute-start | bytes 589832 | tf_op jit(solution)/shard_map/ppermute | solution.py:18
  340.7 48.1 %collective-permute-start.58 = (bf16[3,64,512]{2,1,0:T(8,128)(2,1)S(1)}, bf16[3,64,512]{2,1,0:T(8,128)(2,1)S(1)}, u32[]{:S(2)}, u32[]{:S(2)}) collective-permute-start(bf16[3,64,512]{2,1,0:T(8,128)(2,1)S(1)} %copy-done.73), channel_id=1, source_target_pairs={{0,8},{8,0},{16,24},{24,16},{1,9},{9,1},{17,25},{25,17},{2,10},{10... | collective-permute-start | bytes 589832 | tf_op jit(solution)/shard_map/ppermute | solution.py:18
  441.5 31.3 %collective-permute-start.73 = (bf16[3,64,512]{2,1,0:T(8,128)(2,1)S(1)}, bf16[3,64,512]{2,1,0:T(8,128)(2,1)S(1)}, u32[]{:S(2)}, u32[]{:S(2)}) collective-permute-start(bf16[3,64,512]{2,1,0:T(8,128)(2,1)S(1)} %add_convert_fusion.12), channel_id=1, source_target_pairs={{0,5},{1,4},{2,7},{3,6},{4,1},{5,0},{6,3},{7,2},{8,13},{9,12},{10,... | collective-permute-start | bytes 589832 | tf_op jit(solution)/shard_map/ppermute | solution.py:18
  441.5 36.1 %collective-permute-start.77 = (bf16[3,64,512]{2,1,0:T(8,128)(2,1)S(1)}, bf16[3,64,512]{2,1,0:T(8,128)(2,1)S(1)}, u32[]{:S(2)}, u32[]{:S(2)}) collective-permute-start(bf16[3,64,512]{2,1,0:T(8,128)(2,1)S(1)} %add_convert_fusion.9), channel_id=1, source_target_pairs={{0,6},{1,7},{2,4},{3,5},{4,2},{5,3},{6,0},{7,1},{8,14},{9,15},{10,... | collective-permute-start | bytes 589832 | tf_op jit(solution)/shard_map/ppermute | solution.py:18
  451.1 28.9 %collective-permute-start.81 = (bf16[3,64,512]{2,1,0:T(8,128)(2,1)S(1)}, bf16[3,64,512]{2,1,0:T(8,128)(2,1)S(1)}, u32[]{:S(2)}, u32[]{:S(2)}) collective-permute-start(bf16[3,64,512]{2,1,0:T(8,128)(2,1)S(1)} %add_convert_fusion.6), channel_id=1, source_target_pairs={{0,7},{1,6},{2,5},{3,4},{4,3},{5,2},{6,1},{7,0},{8,15},{9,14},{10,... | collective-permute-start | bytes 589832 | tf_op jit(solution)/shard_map/ppermute | solution.py:18
  454.5 37.1 %collective-permute-start.49 = (bf16[3,64,512]{2,1,0:T(8,128)(2,1)S(1)}, bf16[3,64,512]{2,1,0:T(8,128)(2,1)S(1)}, u32[]{:S(2)}, u32[]{:S(2)}) collective-permute-start(bf16[3,64,512]{2,1,0:T(8,128)(2,1)S(1)} %get-tuple-element.138), channel_id=1, source_target_pairs={{0,6},{1,7},{2,4},{3,5},{4,2},{5,3},{6,0},{7,1},{8,14},{9,15},{10,... | collective-permute-start | bytes 589832 | tf_op jit(solution)/shard_map/ppermute | solution.py:18
  454.7 47.1 %collective-permute-start.47 = (bf16[3,64,512]{2,1,0:T(8,128)(2,1)S(1)}, bf16[3,64,512]{2,1,0:T(8,128)(2,1)S(1)}, u32[]{:S(2)}, u32[]{:S(2)}) collective-permute-start(bf16[3,64,512]{2,1,0:T(8,128)(2,1)S(1)} %get-tuple-element.139), channel_id=1, source_target_pairs={{0,4},{1,5},{2,6},{3,7},{4,0},{5,1},{6,2},{7,3},{8,12},{9,13},{10,... | collective-permute-start | bytes 589832 | tf_op jit(solution)/shard_map/ppermute | solution.py:18
  472.9 29.7 %collective-permute-start.45 = (bf16[3,64,512]{2,1,0:T(8,128)(2,1)S(1)}, bf16[3,64,512]{2,1,0:T(8,128)(2,1)S(1)}, u32[]{:S(2)}, u32[]{:S(2)}) collective-permute-start(bf16[3,64,512]{2,1,0:T(8,128)(2,1)S(1)} %get-tuple-element.140), channel_id=1, source_target_pairs={{0,2},{1,3},{2,0},{3,1},{4,6},{5,7},{6,4},{7,5},{8,10},{9,11},{10,... | collective-permute-start | bytes 589832 | tf_op jit(solution)/shard_map/ppermute | solution.py:18
  480.0 28.7 %collective-permute-start.48 = (bf16[3,64,512]{2,1,0:T(8,128)(2,1)S(1)}, bf16[3,64,512]{2,1,0:T(8,128)(2,1)S(1)}, u32[]{:S(2)}, u32[]{:S(2)}) collective-permute-start(bf16[3,64,512]{2,1,0:T(8,128)(2,1)S(1)} %get-tuple-element.135), channel_id=1, source_target_pairs={{0,5},{1,4},{2,7},{3,6},{4,1},{5,0},{6,3},{7,2},{8,13},{9,12},{10,... | collective-permute-start | bytes 589832 | tf_op jit(solution)/shard_map/ppermute | solution.py:18
  (139 other events, 2761.1 us)

commit v2 on v1

v2 whole, which is shorter than its diff:
```python
import functools

import jax
import jax.numpy as jnp
from jax import lax
from jax.experimental import pallas as pl
from jax.experimental.pallas import tpu as pltpu
from jax.sharding import PartitionSpec as P

VMEM_BYTES = 56 * 1024 * 1024
ANY = pl.BlockSpec(memory_space=pl.ANY)
SMEM = pl.BlockSpec(memory_space=pltpu.SMEM)
VMEM = pl.BlockSpec(memory_space=pltpu.VMEM)
CONTRACT_LAST = (((1,), (1,)), ((), ()))
KINDS = 3


def xor(a, b):
    return jnp.bitwise_xor(a, b)


def swap(value, mask):
    size = lax.axis_size("expert")
    return lax.ppermute(value, "expert", [(i, i ^ mask) for i in range(size)])


def axis_bits(size):
    return [1 << b for b in range(size.bit_length() - 1)]


def hop(value, turn):
    parts, slots = lax.axis_size("dp"), lax.axis_size("expert")
    bits = axis_bits(parts)
    pairs = []
    for d in range(parts):
        for e in range(slots):
            bit = (bits if e % 2 == 0 else bits[::-1])[turn]
            pairs.append((d * slots + e, (d ^ bit) * slots + e))
    return lax.ppermute(value, ("dp", "expert"), pairs)


def feature_block(parts, j):
    bits = axis_bits(parts)
    even = sum(b for t, b in enumerate(bits) if j >> t & 1)
    odd = sum(b for t, b in enumerate(bits[::-1]) if j >> t & 1)
    mask = jnp.where(lax.axis_index("expert") % 2 == 0, even, odd)
    return xor(lax.axis_index("dp"), mask)


def params():
    return pltpu.CompilerParams(vmem_limit_bytes=VMEM_BYTES)


def cost(flops, nbytes, trans=0):
    return pl.CostEstimate(flops=flops, bytes_accessed=nbytes, transcendentals=trans)


def run(copies):
    for copy in copies:
        copy.start()
    for copy in copies:
        copy.wait()


def pick_kernel(wanted, extra, assign, *rest):
    weights, rest = rest[:KINDS], rest[KINDS:]
    given, outs, sems = rest[:extra], rest[extra:-1], rest[-1]
    me = lax.axis_index("expert")
    copies = []
    for out, chunks in zip(outs, wanted):
        for n, (s, k) in enumerate(chunks):
            if s is None:
                copies.append(pltpu.make_async_copy(given[0].at[k], out.at[n], sems.at[len(copies)]))
                continue
            chosen = assign[s, xor(me, k)]
            for w, ref in enumerate(weights):
                copies.append(
                    pltpu.make_async_copy(ref.at[chosen], out.at[n, w], sems.at[len(copies)])
                )
    run(copies)


def pick(wanted, assign, weights, given=()):
    chunk = (KINDS,) + weights[0].shape[1:]
    dtype = weights[0].dtype
    count = sum(KINDS if s is not None else 1 for chunks in wanted for s, _ in chunks)
    return pl.pallas_call(
        functools.partial(pick_kernel, wanted, len(given)),
        out_shape=[jax.ShapeDtypeStruct((len(chunks),) + chunk, dtype) for chunks in wanted],
        in_specs=[SMEM] + [ANY] * (KINDS + len(given)),
        out_specs=[VMEM] * len(wanted),
        scratch_shapes=[pltpu.SemaphoreType.DMA((count,))],
        compiler_params=params(),
        cost_estimate=cost(0, 4 * sum(map(len, wanted)) * chunk[0] * chunk[1] * chunk[2]),
        name="pick",
    )(assign, *weights, *given)


def weight_loads(pieces, kept, target, sems, first):
    parts = lax.axis_size("dp")
    copies = []
    for ref, n, j, position in pieces:
        units, width = ref.shape[2], ref.shape[3]
        at = pl.multiple_of(feature_block(parts, j) * width, width)
        copies.append(
            pltpu.make_async_copy(
                ref.at[n, pl.ds(0, kept)],
                target.at[:, pl.ds(position * units, units), pl.ds(at, width)],
                sems.at[first + len(copies)],
            )
        )
    return copies


def bind(table, refs):
    return [(refs[a], n, j, position) for a, n, j, position in table]


def act_kernel(step, batches, table, count, counts, tokens, upstream, *rest):
    pieces = bind(table, rest[:count])
    hidden, gate_grad, up_grad, weights, x, g, pre, sems = rest[count:]
    rows = x.shape[0]
    run(
        [
            pltpu.make_async_copy(tokens.at[pl.ds(step * rows, rows)], x, sems.at[0]),
            pltpu.make_async_copy(upstream.at[pl.ds(step * rows, rows)], g, sems.at[1]),
        ]
        + weight_loads(pieces, KINDS, weights, sems, 2)
    )
    width = pre.shape[2]
    batch_rows = rows // batches
    for at in range(0, hidden.shape[1], width):
        cols = pl.ds(at, width)
        for w, left in enumerate((x, x, g)):
            pre[w] = lax.dot_general(
                left[...], weights[w, cols, :], CONTRACT_LAST, preferred_element_type=jnp.float32
            )
        for b in range(batches):
            span = pl.ds(b * batch_rows, batch_rows)
            live = (
                lax.broadcasted_iota(jnp.int32, (batch_rows, width), 0)
                < counts[step * batches + b]
            )
            gate_pre, up_pre, hidden_grad = pre[0, span, :], pre[1, span, :], pre[2, span, :]
            sigmoid = jax.nn.sigmoid(gate_pre)
            active = gate_pre * sigmoid
            kept = jnp.where(live, hidden_grad, 0.0)
            hidden[span, cols] = jnp.where(live, active * up_pre, 0.0).astype(hidden.dtype)
            gate_grad[span, cols] = (
                kept * up_pre * sigmoid * (1.0 + gate_pre * (1.0 - sigmoid))
            ).astype(gate_grad.dtype)
            up_grad[span, cols] = (kept * active).astype(up_grad.dtype)


def act(step, rows, units, batches, counts, tokens, upstream, table, arrays):
    features = tokens.shape[1]
    out = jax.ShapeDtypeStruct((rows, units), tokens.dtype)
    width = min(units, 256)
    return pl.pallas_call(
        functools.partial(act_kernel, step, batches, table, len(arrays)),
        out_shape=[out] * 3,
        in_specs=[SMEM, ANY, ANY] + [ANY] * len(arrays),
        out_specs=[VMEM] * 3,
        scratch_shapes=[
            pltpu.VMEM((KINDS, units, features), tokens.dtype),
            pltpu.VMEM((rows, features), tokens.dtype),
            pltpu.VMEM((rows, features), tokens.dtype),
            pltpu.VMEM((3, rows, width), jnp.float32),
            pltpu.SemaphoreType.DMA((2 + len(table),)),
        ],
        compiler_params=params(),
        cost_estimate=cost(
            6 * rows * units * features, 2 * (2 * rows + 3 * units) * features, rows * units
        ),
        name="act",
    )(counts, tokens, upstream, *arrays)


def weight_grads_kernel(step, scale, groups, tokens, upstream, hidden, gate_grad, up_grad, *rest):
    x, g, turned, stage, sems = rest[-5:]
    outs = rest[:-5]
    parts, rows, width = x.shape
    chunk = outs[0].shape[2]
    order = list(range(parts))[::-1]
    loads = {}
    for j in order:
        at = pl.multiple_of(feature_block(parts, j) * width, width)
        for n, (whole, local) in enumerate(((tokens, x), (upstream, g))):
            loads[j, n] = pltpu.make_async_copy(
                whole.at[pl.ds(step * rows, rows), pl.ds(at, width)],
                local.at[j],
                sems.at[2 * j + n],
            )
            loads[j, n].start()
    for w, ref in enumerate((gate_grad, up_grad, hidden)):
        turned[w] = ref[...].T
    stores = []
    for j in order:
        for w in range(KINDS):
            if w == 0:
                loads[j, 0].wait()
            if w == 2:
                loads[j, 1].wait()
            right = (x, x, g)[w]
            stage[j, w] = (
                jnp.dot(turned[w], right[j], preferred_element_type=jnp.float32) * scale
            ).astype(stage.dtype)
        for n, positions in enumerate(groups):
            for i, position in enumerate(positions):
                store = pltpu.make_async_copy(
                    stage.at[j, :, pl.ds(position * chunk, chunk), :],
                    outs[n * parts + j].at[i],
                    sems.at[2 * parts + len(stores)],
                )
                store.start()
                stores.append(store)
    for store in stores:
        store.wait()


def weight_grads(step, parts, chunk, scale, tokens, upstream, hidden, gate_grad, up_grad, groups):
    rows, units = hidden.shape
    features = tokens.shape[1]
    width = features // parts
    shapes = [
        jax.ShapeDtypeStruct((len(positions), KINDS, chunk, width), tokens.dtype)
        for positions in groups
        for _ in range(parts)
    ]
    stores = sum(map(len, groups)) * parts
    flat = pl.pallas_call(
        functools.partial(weight_grads_kernel, step, scale, groups),
        out_shape=shapes,
        in_specs=[ANY, ANY, VMEM, VMEM, VMEM],
        out_specs=[ANY] * len(shapes),
        scratch_shapes=[
            pltpu.VMEM((parts, rows, width), tokens.dtype),
            pltpu.VMEM((parts, rows, width), tokens.dtype),
            pltpu.VMEM((KINDS, units, rows), tokens.dtype),
            pltpu.VMEM((parts, KINDS, units, width), tokens.dtype),
            pltpu.SemaphoreType.DMA((2 * parts + stores,)),
        ],
        compiler_params=params(),
        cost_estimate=cost(6 * rows * units * features, 2 * (2 * rows + 3 * units) * features),
        name="weight_grads",
    )(tokens, upstream, hidden, gate_grad, up_grad)
    return [
        {j: flat[n * parts + j] for j in range(parts)} for n in range(len(groups))
    ]


def input_grad_kernel(step, table, count, has_base, gate_grad, up_grad, *rest):
    pieces = bind(table, rest[:count])
    out, weights, stage, sems = rest[count + has_base :]
    run(weight_loads(pieces, 2, weights, sems, 0))
    parts, rows, width = stage.shape
    stores = []
    for n in range(parts):
        cols = pl.ds(n * width, width)
        stage[n] = (
            jnp.dot(gate_grad[...], weights[0, :, cols], preferred_element_type=jnp.float32)
            + jnp.dot(up_grad[...], weights[1, :, cols], preferred_element_type=jnp.float32)
        ).astype(stage.dtype)
        store = pltpu.make_async_copy(
            stage.at[n], out.at[pl.ds(step * rows, rows), cols], sems.at[len(table) + n]
        )
        store.start()
        stores.append(store)
    for store in stores:
        store.wait()


def input_grad(step, steps, gate_grad, up_grad, table, arrays, features, base):
    rows, units = gate_grad.shape
    parts = max(1, features // 512)
    more = [] if base is None else [base]
    return pl.pallas_call(
        functools.partial(input_grad_kernel, step, table, len(arrays), len(more)),
        out_shape=jax.ShapeDtypeStruct((steps * rows, features), gate_grad.dtype),
        in_specs=[VMEM, VMEM] + [ANY] * (len(arrays) + len(more)),
        out_specs=ANY,
        scratch_shapes=[
            pltpu.VMEM((2, units, features), gate_grad.dtype),
            pltpu.VMEM((parts, rows, features // parts), gate_grad.dtype),
            pltpu.SemaphoreType.DMA((len(table) + parts,)),
        ],
        input_output_aliases={2 + len(arrays): 0} if more else {},
        compiler_params=params(),
        cost_estimate=cost(4 * rows * units * features, 2 * (rows + 2 * units) * features),
        name="input_grad",
    )(gate_grad, up_grad, *arrays, *more)


def place_kernel(table, count, assign, *rest):
    pieces = rest[:count]
    outs = rest[count:]
    me = lax.axis_index("expert")
    expert = pl.program_id(0)
    for out in outs:
        out[...] = jnp.zeros_like(out)
    for a, n, s, k in table:

        @pl.when(assign[s, xor(me, k)] == expert)
        def _():
            for w, out in enumerate(outs):
                out[0] += pieces[a][n, w].astype(jnp.float32)


def place(assign, home, experts):
    arrays = list({id(a): a for a, _, _, _ in home}.values())
    index = {id(a): i for i, a in enumerate(arrays)}
    table = tuple((index[id(a)], n, s, k) for a, n, s, k in home)
    units, width = arrays[0].shape[2:]
    out = jax.ShapeDtypeStruct((experts, units, width), jnp.float32)
    return pl.pallas_call(
        functools.partial(place_kernel, table, len(arrays)),
        grid=(experts,),
        out_shape=[out] * KINDS,
        in_specs=[SMEM] + [VMEM] * len(arrays),
        out_specs=[pl.BlockSpec((1, units, width), lambda e: (e, 0, 0))] * KINDS,
        compiler_params=params(),
        name="place",
    )(assign, *arrays)


def finish_kernel(table, count, assign, *rest):
    pieces = rest[:count]
    outs = rest[count + KINDS : count + 2 * KINDS]
    held, sems = rest[count + 2 * KINDS :]
    me = lax.axis_index("expert")
    chosen = [assign[s, xor(me, k)] for _, _, s, k in table]
    first = []
    for m in range(len(table)):
        slot = jnp.int32(m)
        for o in range(m - 1, -1, -1):
            slot = jnp.where(chosen[o] == chosen[m], o, slot)
        first.append(slot)
    spots = [(m, w) for m in range(len(table)) for w in range(KINDS)]
    run([pltpu.make_async_copy(outs[w].at[chosen[m]], held.at[m, w], sems.at[m, w]) for m, w in spots])
    for m, (a, n, _, _) in enumerate(table):
        held[first[m]] += pieces[a][n].astype(jnp.float32)
    for wait in (False, True):
        for m in range(len(table)):

            @pl.when(first[m] == m)
            def _():
                for w in range(KINDS):
                    store = pltpu.make_async_copy(
                        held.at[m, w], outs[w].at[chosen[m]], sems.at[m, w]
                    )
                    store.wait() if wait else store.start()


def finish(assign, home, totals):
    arrays = list({id(a): a for a, _, _, _ in home}.values())
    index = {id(a): i for i, a in enumerate(arrays)}
    table = tuple((index[id(a)], n, s, k) for a, n, s, k in home)
    shape = totals[0].shape[1:]
    return pl.pallas_call(
        functools.partial(finish_kernel, table, len(arrays)),
        out_shape=[jax.ShapeDtypeStruct(t.shape, t.dtype) for t in totals],
        in_specs=[SMEM] + [VMEM] * len(arrays) + [ANY] * KINDS,
        out_specs=[ANY] * KINDS,
        scratch_shapes=[
            pltpu.VMEM((len(table), KINDS) + shape, jnp.float32),
            pltpu.SemaphoreType.DMA((len(table), KINDS)),
        ],
        input_output_aliases={1 + len(arrays) + w: w for w in range(KINDS)},
        compiler_params=params(),
        name="finish",
    )(assign, *arrays, *totals)


class Line:
    def __init__(self, depth):
        self.depth = depth
        self.sent = []
        self.gates = {}
        self.plans = []

    def send(self, move, value, *way, behind=()):
        behind = list(behind) + self.gates.get(len(self.sent), [])
        if len(self.sent) >= self.depth:
            behind.append(self.sent[-self.depth])
        if behind:
            value = after(value, *behind)
        self.sent.append(move(value, *way))
        result = self.sent[-1]
        self.settle()
        return result

    def settle(self, everything=False):
        while self.plans and (everything or self.plans[0][0] < len(self.sent)):
            number, plan = self.plans.pop(0)
            plan(self.sent[min(number, len(self.sent) - 1)])

    def plan(self, lag, what):
        self.plans.append((len(self.sent) - 1 + lag, what))
        self.plans.sort(key=lambda item: item[0])


def after(value, *others):
    return lax.optimization_barrier((value, *others))[0]


def overlap(jobs, sends):
    before = None
    for job in jobs:
        next(job)
        if before is not None:
            next(before)
            next(before, None)
        for _ in range(sends - 2):
            next(job)
        before = job
    next(before)
    next(before, None)


def spread(line, own, done):
    have = {0: own}
    for turn in range(len(axis_bits(lax.axis_size("dp")))):
        have[1 << turn] = line.send(hop, own, turn)
        yield True
    for turn in range(len(axis_bits(lax.axis_size("dp")))):
        for j in sorted(have):
            if j and j < 1 << turn:
                have[j | 1 << turn] = line.send(hop, have[j], turn)
                yield True
    done(have)


def collect(line, produced, done):
    terms = {j: [a] for j, a in produced.items()}

    def total(addends):
        if len(addends) == 1:
            return addends[0]
        return sum(a.astype(jnp.float32) for a in addends).astype(addends[0].dtype)

    for turn in range(len(axis_bits(len(produced)))):
        for j in sorted([j for j in terms if j >> turn & 1], reverse=True):
            terms[j ^ 1 << turn].append(line.send(hop, total(terms.pop(j)), turn))
            yield True
    done(total(terms[0]))


def local(tokens, upstream, counts, assign, gate_weight, up_weight, down_weight):
    steps, slots = assign.shape
    rows = tokens.shape[0] // steps
    batches = counts.shape[0] // steps
    features = tokens.shape[1]
    experts, chunk, _ = gate_weight.shape
    parts = lax.axis_size("dp")
    units = slots * chunk
    weights = (gate_weight, up_weight, down_weight)
    every = range(steps)
    far = slots // 2
    near = [k for k in range(2, slots, 2) if k != far]
    remote = near + [far]
    position = {k: 2 * i for i, k in enumerate([0] + remote)}
    wide, deep = Line(3), Line(2)

    own, mate_first, mate_rest = pick(
        (
            tuple((s, 0) for s in every),
            tuple((s, 1) for s in every),
            tuple((s, k ^ 1) for s in every for k in remote),
        ),
        assign,
        weights,
    )
    mate_first = swap(mate_first, 1)
    mate_rest = swap(mate_rest, 1)
    wanted = tuple(
        ((s, k), (None, s * len(remote) + i)) for s in every for i, k in enumerate(remote)
    )
    messages = pick(wanted, assign, weights, (mate_rest,))

    moves = [(s, k) for s in every for k in remote]
    arrived = {}

    def fetch(key):
        while key not in arrived:
            n = len(deep.sent)
            s, k = moves[n]
            at = 2 * n + 1 - len(near) % 2
            behind = wide.sent[min(at, len(wide.sent) - 1) :][:1] if n >= len(near) else ()
            arrived[s, k] = deep.send(swap, messages[n], k, behind=behind)

    def ahead(arrival):
        n = len(deep.sent)
        if n < len(moves) and 2 * n + 1 < len(wide.sent):
            fetch(moves[n])
        wide.plan(1, ahead)

    table = [[] for _ in every]

    def deliver(keys, array, places):
        for key in keys:
            fetch(key)
        if keys:
            pairs = [arrived[key] for key in keys]
            array = pairs[0] if len(pairs) == 1 else jnp.concatenate(pairs)

        def done(have):
            for j, a in have.items():
                for n, (s, p) in enumerate(places):
                    table[s].append((a, n, j, p))

        yield from spread(wide, array, done)

    jobs = [
        deliver([], own, [(s, 0) for s in every]),
        deliver([], mate_first, [(s, 1) for s in every]),
    ]
    for s in every:
        for group in (near, [far]):
            if group:
                places = [(s, position[k] + c) for k in group for c in range(2)]
                jobs.append(deliver([(s, k) for k in group], None, places))
    for k in near:
        fetch((0, k))
    wide.plan(1, ahead)
    overlap(jobs, parts - 1)
    wide.plans.clear()

    token_grad = None
    early, late = [], []
    jobs = []
    for s in every:
        arrays = list({id(a): a for a, _, _, _ in table[s]}.values())
        index = {id(a): i for i, a in enumerate(arrays)}
        places = tuple((index[id(a)], n, j, p) for a, n, j, p in table[s])
        hidden, gate_grad, up_grad = act(
            s, rows, units, batches, counts, tokens, upstream, places, arrays
        )
        groups = [g for g in ([far], near) if g]
        produced = weight_grads(
            s, parts, chunk, 1.0 / rows, tokens, upstream, hidden, gate_grad, up_grad,
            tuple(
                tuple(position[k] + c for k in group for c in range(2)) for group in groups + [[0]]
            ),
        )
        token_grad = input_grad(
            s, steps, gate_grad, up_grad, places, arrays, features, token_grad
        )
        counts = after(counts, token_grad)
        jobs.append([(s, group, terms) for group, terms in zip(groups + [[0]], produced)])

    def returned(s, group):
        home = late if group == [0] or (s == steps - 1 and group != [far]) else early

        def mates(pairs):
            def go(arrival):
                seconds = [pair[1:] for _, pair in pairs]
                seconds = seconds[0] if len(seconds) == 1 else jnp.concatenate(seconds)
                seconds = swap(seconds if arrival is None else after(seconds, arrival), 1)
                home.extend((seconds, n, s, k ^ 1) for n, (k, _) in enumerate(pairs))

            return go

        def done(total):
            pairs = []
            for i, k in enumerate(group):
                pair = total[2 * i : 2 * i + 2]
                if k:
                    pair = deep.send(swap, pair, k)
                home.append((pair, 0, s, k))
                pairs.append((k, pair))
            if group == [0]:
                mates(pairs)(None)
            else:
                wide.plan(parts - 1, mates(pairs))

        return done

    base = len(wide.sent)
    for n in range(parts - 1):
        wide.gates[base + n] = [wide.sent[-1]]
    wide.gates[base + 4 * parts - 6] = [token_grad]
    remote_jobs = [job for step in jobs for job in step[:-1]]
    own_jobs = [step[-1] for step in jobs]
    overlap(
        [
            collect(wide, terms, returned(s, group))
            for s, group, terms in remote_jobs + own_jobs
        ],
        parts - 1,
    )
    wide.settle(True)
    totals = place(after(assign, token_grad), early, experts)
    totals = finish(assign, late, totals)
    return (token_grad, *totals)


def solution(mesh):
    placed = (
        P(("dp", "expert"), None),
        P(("dp", "expert"), None),
        P(("dp", "expert")),
        P(),
        P(None, "expert", "dp"),
        P(None, "expert", "dp"),
        P(None, "expert", "dp"),
    )
    return jax.shard_map(
        local,
        mesh=mesh,
        in_specs=placed,
        out_specs=(
            P(("dp", "expert"), None),
            P(None, "expert", "dp"),
            P(None, "expert", "dp"),
            P(None, "expert", "dp"),
        ),
        check_vma=False,
    )
```

time: 520 us -> 299 us (0.57)
  Pallas kernels: 169 us -> 84.1 us
  waiting for transfers between devices: 226 us -> 150 us
  starting transfers between devices: 112 us -> 56.5 us
    pallas_call x8 -> x10, Pallas kernels: 169 us -> 84.1 us  [the longest x2 24.6 us: act(): pl.pallas_call(functools.partial(act_kernel, step, batches, table, len(ar...]
    ppermute x82 -> x56, waiting for transfers between devices: 226 us -> 150 us  [the longest x36 76.7 us: hop(): return lax.ppermute(value, ('dp', 'expert'), pairs)]
    ppermute x82 -> x56, starting transfers between devices: 112 us -> 56.5 us  [the longest x36 36.5 us: hop(): return lax.ppermute(value, ('dp', 'expert'), pairs)]
  transfers between devices with their start and end apart: 82 -> 56, of which waited for: 36 -> 20; matrix products, arithmetic and copies ran while one was open for 1% -> 1% of each run, Pallas kernels for 12% -> 25%
where the time goes in v2:
time: 299 us
  waiting for transfers between devices  150 us (50%)
  Pallas kernels  84.1 us (28%)
  starting transfers between devices  56.5 us (19%)
  local copies, waits for them, and re-layouts  3.87 us (1%)
    ppermute x36, waiting for transfers between devices, hop(): return lax.ppermute(value, ('dp', 'expert'), pairs)  76.7 us
    ppermute x20, waiting for transfers between devices, swap(): return lax.ppermute(value, 'expert', [(i, i ^ mask) for i in range(size)])  73.3 us
    ppermute x36, starting transfers between devices, hop(): return lax.ppermute(value, ('dp', 'expert'), pairs)  36.5 us
    pallas_call x2, Pallas kernels, act(): pl.pallas_call(functools.partial(act_kernel, step, batches, table, len(ar...  24.6 us
    pallas_call x2, Pallas kernels, weight_grads(): pl.pallas_call(functools.partial(weight_grads_kernel, step, scale, groups...  21.2 us
    ppermute x20, starting transfers between devices, swap(): return lax.ppermute(value, 'expert', [(i, i ^ mask) for i in range(size)])  20 us
    pallas_call x2, Pallas kernels, input_grad(): pl.pallas_call(functools.partial(input_grad_kernel, step, table, len(arra...  16.7 us
    pallas_call x1, Pallas kernels, place(): pl.pallas_call(functools.partial(place_kernel, table, len(arrays)), grid=...  8.57 us
  transfers between devices with their start and end apart: 56, of which 20 were waited for; matrix products, arithmetic and copies ran while one was open for 1% of the time, Pallas kernels for 25%

profile of v2, /device:TPU:0, one launch (start us, length us, event | category | flops | bytes accessed | tf_op | source)
XLA Modules:
  0.0 298.6 jit_solution(18404032215031336031)
XLA Ops:
  8.9 4.0 %pick.3 = (bf16[2,3,64,512]{3,2,1,0:T(8,128)(2,1)}, bf16[2,3,64,512]{3,2,1,0:T(8,128)(2,1)}, bf16[2,3,64,512]{3,2,1,0:T(8,128)(2,1)}, bf16[2,3,64,512]{3,2,1,0:T...) custom-call(s32[2,8]{1,0:T(2,128)} %assign.6, bf16[16,64,512]{2,1,0:T(8,128)(2,1)} %rest_0_.3, ...), custom_call_target="tpu_custom_call" | custom-call | bytes 4718592 | tf_op jit(solution)/shard_map/pick/pallas_call | solution.py:87
  21.7 3.8 %collective-permute-done.8 = bf16[2,3,64,512]{3,2,1,0:T(8,128)(2,1)S(1)} collective-permute-done((bf16[2,3,64,512]{3,2,1,0:T(8,128)(2,1)}, bf16[2,3,64,512]{3,2,1,0:T(8,128)(2,1)S(1)}, u32[]{:S(2)}, u32[]{:S(2)}) %collective-permute-start.8) | collective-permute-done | bytes 393248 | tf_op jit(solution)/shard_map/ppermute | solution.py:24
  25.5 10.5 %collective-permute-done.9 = bf16[2,3,64,512]{3,2,1,0:T(8,128)(2,1)S(1)} collective-permute-done((bf16[2,3,64,512]{3,2,1,0:T(8,128)(2,1)}, bf16[2,3,64,512]{3,2,1,0:T(8,128)(2,1)S(1)}, u32[]{:S(2)}, u32[]{:S(2)}) %collective-permute-start.9) | collective-permute-done | bytes 393248 | tf_op jit(solution)/shard_map/ppermute | solution.py:24
  39.7 10.0 %collective-permute-done.5.rest_6_ = bf16[2,3,64,512]{3,2,1,0:T(8,128)(2,1)S(1)} collective-permute-done((bf16[2,3,64,512]{3,2,1,0:T(8,128)(2,1)S(1)}, bf16[2,3,64,512]{3,2,1,0:T(8,128)(2,1)S(1)}, u32[]{:S(2)}, u32[]{:S(2)}) %collective-permute-start.5) | collective-permute-done | bytes 393248 | tf_op jit(solution)/shard_map/ppermute | solution.py:39
  63.3 12.8 %collective-permute-done.13.rest_12_ = bf16[2,3,64,512]{3,2,1,0:T(8,128)(2,1)S(1)} collective-permute-done((bf16[2,3,64,512]{3,2,1,0:T(8,128)(2,1)S(1)}, bf16[2,3,64,512]{3,2,1,0:T(8,128)(2,1)S(1)}, u32[]{:S(2)}, u32[]{:S(2)}) %collective-permute-start.13) | collective-permute-done | bytes 393248 | tf_op jit(solution)/shard_map/ppermute | solution.py:24
  79.3 12.4 %collective-permute-done.17 = bf16[2,3,64,512]{3,2,1,0:T(8,128)(2,1)S(1)} collective-permute-done((bf16[2,3,64,512]{3,2,1,0:T(8,128)(2,1)S(1)}, bf16[2,3,64,512]{3,2,1,0:T(8,128)(2,1)S(1)}, u32[]{:S(2)}, u32[]{:S(2)}) %collective-permute-start.17) | collective-permute-done | bytes 393248 | tf_op jit(solution)/shard_map/ppermute | solution.py:24
  95.5 16.1 %collective-permute-done.19.rest_9_ = bf16[4,3,64,512]{3,2,1,0:T(8,128)(2,1)S(1)} collective-permute-done((bf16[4,3,64,512]{3,2,1,0:T(8,128)(2,1)S(1)}, bf16[4,3,64,512]{3,2,1,0:T(8,128)(2,1)S(1)}, u32[]{:S(2)}, u32[]{:S(2)}) %collective-permute-start.19) | collective-permute-done | bytes 786464 | tf_op jit(solution)/shard_map/ppermute | solution.py:39
  116.0 12.7 %collective-permute-done.22.rest_12_ = bf16[2,3,64,512]{3,2,1,0:T(8,128)(2,1)} collective-permute-done((bf16[2,3,64,512]{3,2,1,0:T(8,128)(2,1)S(1)}, bf16[2,3,64,512]{3,2,1,0:T(8,128)(2,1)}, u32[]{:S(2)}, u32[]{:S(2)}) %collective-permute-start.22) | collective-permute-done | bytes 393248 | tf_op jit(solution)/shard_map/ppermute | solution.py:24
  130.1 12.3 %act.2 = (bf16[768,512]{1,0:T(8,128)(2,1)}, bf16[768,512]{1,0:T(8,128)(2,1)}, bf16[768,512]{1,0:T(8,128)(2,1)}) custom-call(s32[16]{0:T(128)} %counts.2, bf16[1536,2048]{1,0:T(8,128)(2,1)} %tokens.7, bf16[1536,2048]{1,0:T(8,128)(2,1)} %upstream.7, bf16[2,3,64,512]{3,2,1,0:T(8,128)(2,1)} %get-tuple-element.98.rest_0_, bf16[2,3,64,512]{3,2,1,0:T(8,128)(2,1)} %copy-done.2, ...), custom_call_target="tpu_custom_call" | custom-call | flops 4831838208 | bytes 12582912 | tf_op jit(solution)/shard_map/act/pallas_call | solution.py:159
  142.4 8.2 %input_grad.2.rest_16_ = bf16[1536,2048]{1,0:T(8,128)(2,1)} custom-call(bf16[768,512]{1,0:T(8,128)(2,1)} %get-tuple-element.114.gate_grad, bf16[768,512]{1,0:T(8,128)(2,1)} %get-tuple-element.115.up_grad, bf16[2,3,64,512]{3,2,1,0:T(8,128)(2,1)} %get-tuple-element.98.rest_0_, bf16[2,3,64,512]{3,2,1,0:T(8,128)(2,1)} %copy-done.2, ...), custom_call_target="tpu_custom_call" | custom-call | flops 3221225472 | bytes 7340032 | tf_op jit(solution)/shard_map/input_grad/pallas_call | solution.py:277
  152.7 10.7 %weight_grads.3 = (bf16[2,3,64,512]{3,2,1,0:T(8,128)(2,1)}, bf16[2,3,64,512]{3,2,1,0:T(8,128)(2,1)}, bf16[2,3,64,512]{3,2,1,0:T(8,128)(2,1)}, bf16[2,3,64,512]{3...) custom-call(bf16[1536,2048]{1,0:T(8,128)(2,1)} %tokens.7, ...), custom_call_target="tpu_custom_call" | custom-call | flops 4831838208 | bytes 12582912 | tf_op jit(solution)/shard_map/weight_grads/pallas_call | solution.py:231
  166.3 12.3 %act.3 = (bf16[768,512]{1,0:T(8,128)(2,1)}, bf16[768,512]{1,0:T(8,128)(2,1)}, bf16[768,512]{1,0:T(8,128)(2,1)}) custom-call(s32[16]{0:T(128)} %counts.2, bf16[1536,2048]{1,0:T(8,128)(2,1)} %tokens.7, bf16[1536,2048]{1,0:T(8,128)(2,1)} %upstream.7, bf16[2,3,64,512]{3,2,1,0:T(8,128)(2,1)} %get-tuple-element.98.rest_0_, bf16[2,3,64,512]{3,2,1,0:T(8,128)(2,1)} %copy-done.2, ...), custom_call_target="tpu_custom_call" | custom-call | flops 4831838208 | bytes 12582912 | tf_op jit(solution)/shard_map/act/pallas_call | solution.py:159
  180.2 10.6 %weight_grads.2 = (bf16[2,3,64,512]{3,2,1,0:T(8,128)(2,1)}, bf16[2,3,64,512]{3,2,1,0:T(8,128)(2,1)}, bf16[2,3,64,512]{3,2,1,0:T(8,128)(2,1)}, bf16[2,3,64,512]{3...) custom-call(bf16[1536,2048]{1,0:T(8,128)(2,1)} %tokens.7, ...), custom_call_target="tpu_custom_call" | custom-call | flops 4831838208 | bytes 12582912 | tf_op jit(solution)/shard_map/weight_grads/pallas_call | solution.py:231
  193.8 8.4 %input_grad.3 = bf16[1536,2048]{1,0:T(8,128)(2,1)} custom-call(bf16[768,512]{1,0:T(8,128)(2,1)} %get-tuple-element.129.gate_grad, bf16[768,512]{1,0:T(8,128)(2,1)} %get-tuple-element.130.up_grad, bf16[2,3,64,512]{3,2,1,0:T(8,128)(2,1)} %get-tuple-element.98.rest_0_, bf16[2,3,64,512]{3,2,1,0:T(8,128)(2,1)} %copy-done.2, ...), custom_call_target="tpu_custom_call", output_to_operand_aliasing={{}: (18, {})} | custom-call | flops 3221225472 | bytes 7340032 | tf_op jit(solution)/shard_map/input_grad/pallas_call | solution.py:277
  203.7 5.1 %collective-permute-done.31 = bf16[2,3,64,512]{3,2,1,0:T(8,128)(2,1)S(1)} collective-permute-done((bf16[2,3,64,512]{3,2,1,0:T(8,128)(2,1)}, bf16[2,3,64,512]{3,2,1,0:T(8,128)(2,1)S(1)}, u32[]{:S(2)}, u32[]{:S(2)}) %collective-permute-start.31) | collective-permute-done | bytes 393248 | tf_op jit(solution)/shard_map/ppermute | solution.py:39
  209.9 3.9 %collective-permute-done.28 = bf16[2,3,64,512]{3,2,1,0:T(8,128)(2,1)S(1)} collective-permute-done((bf16[2,3,64,512]{3,2,1,0:T(8,128)(2,1)S(1)}, bf16[2,3,64,512]{3,2,1,0:T(8,128)(2,1)S(1)}, u32[]{:S(2)}, u32[]{:S(2)}) %collective-permute-start.28) | collective-permute-done | bytes 393248 | tf_op jit(solution)/shard_map/ppermute | solution.py:39
  215.4 11.0 %collective-permute-done.32 = bf16[4,3,64,512]{3,2,1,0:T(8,128)(2,1)S(1)} collective-permute-done((bf16[4,3,64,512]{3,2,1,0:T(8,128)(2,1)S(1)}, bf16[4,3,64,512]{3,2,1,0:T(8,128)(2,1)S(1)}, u32[]{:S(2)}, u32[]{:S(2)}) %collective-permute-start.32) | collective-permute-done | bytes 786464 | tf_op jit(solution)/shard_map/ppermute | solution.py:39
  232.1 11.0 %collective-permute-done.29 = bf16[4,3,64,512]{3,2,1,0:T(8,128)(2,1)S(1)} collective-permute-done((bf16[4,3,64,512]{3,2,1,0:T(8,128)(2,1)S(1)}, bf16[4,3,64,512]{3,2,1,0:T(8,128)(2,1)S(1)}, u32[]{:S(2)}, u32[]{:S(2)}) %collective-permute-start.29) | collective-permute-done | bytes 786464 | tf_op jit(solution)/shard_map/ppermute | solution.py:39
  243.2 4.2 %collective-permute-done.44 = bf16[2,3,64,512]{3,2,1,0:T(8,128)(2,1)S(1)} collective-permute-done((bf16[2,3,64,512]{3,2,1,0:T(8,128)(2,1)S(1)}, bf16[2,3,64,512]{3,2,1,0:T(8,128)(2,1)S(1)}, u32[]{:S(2)}, u32[]{:S(2)}) %collective-permute-start.44) | collective-permute-done | bytes 393248 | tf_op jit(solution)/shard_map/ppermute | solution.py:39
  256.6 6.2 %collective-permute-done.42.rest_5_ = bf16[2,3,64,512]{3,2,1,0:T(8,128)(2,1)S(1)} collective-permute-done((bf16[2,3,64,512]{3,2,1,0:T(8,128)(2,1)S(1)}, bf16[2,3,64,512]{3,2,1,0:T(8,128)(2,1)S(1)}, u32[]{:S(2)}, u32[]{:S(2)}) %collective-permute-start.42) | collective-permute-done | bytes 393248 | tf_op jit(solution)/shard_map/ppermute | solution.py:24
  266.3 7.6 %collective-permute-done.40.rest_0_ = bf16[2,3,64,512]{3,2,1,0:T(8,128)(2,1)S(1)} collective-permute-done((bf16[2,3,64,512]{3,2,1,0:T(8,128)(2,1)S(1)}, bf16[2,3,64,512]{3,2,1,0:T(8,128)(2,1)S(1)}, u32[]{:S(2)}, u32[]{:S(2)}) %collective-permute-start.40) | collective-permute-done | bytes 393248 | tf_op jit(solution)/shard_map/ppermute | solution.py:24
  273.9 7.3 %collective-permute-done.43.rest_1_ = bf16[2,3,64,512]{3,2,1,0:T(8,128)(2,1)S(1)} collective-permute-done((bf16[2,3,64,512]{3,2,1,0:T(8,128)(2,1)S(1)}, bf16[2,3,64,512]{3,2,1,0:T(8,128)(2,1)S(1)}, u32[]{:S(2)}, u32[]{:S(2)}) %collective-permute-start.43) | collective-permute-done | bytes 393248 | tf_op jit(solution)/shard_map/ppermute | solution.py:24
  283.6 8.6 %place.1 = (f32[16,64,512]{2,1,0:T(8,128)}, f32[16,64,512]{2,1,0:T(8,128)}, f32[16,64,512]{2,1,0:T(8,128)}) custom-call(s32[2,8]{1,0:T(2,128)} %assign.6, bf16[2,3,64,512]{3,2,1,0:T(8,128)(2,1)} %copy-done.25, bf16[1,3,64,512]{3,2,1,0:T(8,128)(2,1)} %copy-done.43, bf16[2,3,64,512]{3,2,1,0:T(8,128)(2,1)} %copy-done.26, bf16[2,3,64,512]{3,2,1,0:T(8,128)(2,1)} %copy-done.27, ...), custom_call_target="tpu_custom_call" | custom-call | tf_op jit(solution)/shard_map/place/pallas_call | solution.py:315
  293.1 5.3 %finish.1 = (f32[16,64,512]{2,1,0:T(8,128)}, f32[16,64,512]{2,1,0:T(8,128)}, f32[16,64,512]{2,1,0:T(8,128)}) custom-call(s32[2,8]{1,0:T(2,128)} %assign.6, bf16[2,3,64,512]{3,2,1,0:T(8,128)(2,1)} %copy-done.23, bf16[2,3,64,512]{3,2,1,0:T(8,128)(2,1)} %copy-done.24, ...), custom_call_target="tpu_custom_call", output_to_operand_aliasing={{0}: (8, {}), {1}: (9, {}), {2}: (10, {})} | custom-call | tf_op jit(solution)/shard_map/finish/pallas_call | solution.py:359
  (244 shorter events, 81.7 us)
Async XLA Ops:
  15.7 20.3 %collective-permute-start.9 = (bf16[2,3,64,512]{3,2,1,0:T(8,128)(2,1)}, bf16[2,3,64,512]{3,2,1,0:T(8,128)(2,1)S(1)}, u32[]{:S(2)}, u32[]{:S(2)}) collective-permute-start(bf16[2,3,64,512]{3,2,1,0:T(8,128)(2,1)} %get-tuple-element.105), channel_id=1, source_target_pairs={{0,6},{1,7},{2,4},{3,5},{4,2},{5,3},{6,0},{7,1},{8,14},{9,15},{10,... | collective-permute-start | bytes 1179656 | tf_op jit(solution)/shard_map/ppermute | solution.py:24
  18.1 17.9 %collective-permute-start.4 = (bf16[2,3,64,512]{3,2,1,0:T(8,128)(2,1)S(1)}, bf16[2,3,64,512]{3,2,1,0:T(8,128)(2,1)S(1)}, u32[]{:S(2)}, u32[]{:S(2)}) collective-permute-start(bf16[2,3,64,512]{3,2,1,0:T(8,128)(2,1)S(1)} %collective-permute-done.3.rest_4_), channel_id=1, source_target_pairs={{0,8},{1,17},{2,10},{3,19},{4,12},{5,21},{6,14},{7,23},{8,0},{9,25... | collective-permute-start | bytes 1179656 | tf_op jit(solution)/shard_map/ppermute | solution.py:39
  19.6 18.0 %collective-permute-start.1 = (bf16[2,3,64,512]{3,2,1,0:T(8,128)(2,1)S(1)}, bf16[2,3,64,512]{3,2,1,0:T(8,128)(2,1)S(1)}, u32[]{:S(2)}, u32[]{:S(2)}) collective-permute-start(bf16[2,3,64,512]{3,2,1,0:T(8,128)(2,1)S(1)} %copy-done), channel_id=1, source_target_pairs={{0,16},{1,9},{2,18},{3,11},{4,20},{5,13},{6,22},{7,15},{8,24},{9,1... | collective-permute-start | bytes 1179656 | tf_op jit(solution)/shard_map/ppermute | solution.py:39
  21.2 18.0 %collective-permute-start.2 = (bf16[2,3,64,512]{3,2,1,0:T(8,128)(2,1)S(1)}, bf16[2,3,64,512]{3,2,1,0:T(8,128)(2,1)S(1)}, u32[]{:S(2)}, u32[]{:S(2)}) collective-permute-start(bf16[2,3,64,512]{3,2,1,0:T(8,128)(2,1)S(1)} %collective-permute-done.rest_1_), channel_id=1, source_target_pairs={{0,16},{1,9},{2,18},{3,11},{4,20},{5,13},{6,22},{7,15},{8,24},{9,1... | collective-permute-start | bytes 1179656 | tf_op jit(solution)/shard_map/ppermute | solution.py:39
  36.1 20.4 %collective-permute-start.10 = (bf16[4,3,64,512]{3,2,1,0:T(8,128)(2,1)S(1)}, bf16[4,3,64,512]{3,2,1,0:T(8,128)(2,1)S(1)}, u32[]{:S(2)}, u32[]{:S(2)}) collective-permute-start(bf16[4,3,64,512]{3,2,1,0:T(8,128)(2,1)S(1)} %constant_dynamic-update-slice_fusion.rest_8_), channel_id=1, source_target_pairs={{0,8},{1,17},{2,10},{3,19},{4,12},{5,21},{6,14},{7,23},{8,0},{9,25... | collective-permute-start | bytes 2359304 | tf_op jit(solution)/shard_map/ppermute | solution.py:39
  56.5 19.6 %collective-permute-start.12 = (bf16[4,3,64,512]{3,2,1,0:T(8,128)(2,1)S(1)}, bf16[4,3,64,512]{3,2,1,0:T(8,128)(2,1)S(1)}, u32[]{:S(2)}, u32[]{:S(2)}) collective-permute-start(bf16[4,3,64,512]{3,2,1,0:T(8,128)(2,1)S(1)} %collective-permute-done.10.rest_9_), channel_id=1, source_target_pairs={{0,16},{1,9},{2,18},{3,11},{4,20},{5,13},{6,22},{7,15},{8,24},{9,1... | collective-permute-start | bytes 2359304 | tf_op jit(solution)/shard_map/ppermute | solution.py:39
  63.3 28.4 %collective-permute-start.17 = (bf16[2,3,64,512]{3,2,1,0:T(8,128)(2,1)S(1)}, bf16[2,3,64,512]{3,2,1,0:T(8,128)(2,1)S(1)}, u32[]{:S(2)}, u32[]{:S(2)}) collective-permute-start(bf16[2,3,64,512]{3,2,1,0:T(8,128)(2,1)S(1)} %copy-done.56), channel_id=1, source_target_pairs={{0,2},{1,3},{2,0},{3,1},{4,6},{5,7},{6,4},{7,5},{8,10},{9,11},{10,... | collective-permute-start | bytes 1179656 | tf_op jit(solution)/shard_map/ppermute | solution.py:24
  91.8 19.7 %collective-permute-start.19 = (bf16[4,3,64,512]{3,2,1,0:T(8,128)(2,1)S(1)}, bf16[4,3,64,512]{3,2,1,0:T(8,128)(2,1)S(1)}, u32[]{:S(2)}, u32[]{:S(2)}) collective-permute-start(bf16[4,3,64,512]{3,2,1,0:T(8,128)(2,1)S(1)} %constant_dynamic-update-slice_fusion.2.rest_8_), channel_id=1, source_target_pairs={{0,8},{1,17},{2,10},{3,19},{4,12},{5,21},{6,14},{7,23},{8,0},{9,25... | collective-permute-start | bytes 2359304 | tf_op jit(solution)/shard_map/ppermute | solution.py:39
  93.4 20.5 %collective-permute-start.15 = (bf16[2,3,64,512]{3,2,1,0:T(8,128)(2,1)S(1)}, bf16[2,3,64,512]{3,2,1,0:T(8,128)(2,1)}, u32[]{:S(2)}, u32[]{:S(2)}) collective-permute-start(bf16[2,3,64,512]{3,2,1,0:T(8,128)(2,1)S(1)} %collective-permute-done.13.rest_12_), channel_id=1, source_target_pairs={{0,16},{1,9},{2,18},{3,11},{4,20},{5,13},{6,22},{7,15},{8,24},{9,1... | collective-permute-start | bytes 1179656 | tf_op jit(solution)/shard_map/ppermute | solution.py:39
  93.4 21.2 %collective-permute-start.16 = (bf16[2,3,64,512]{3,2,1,0:T(8,128)(2,1)S(1)}, bf16[2,3,64,512]{3,2,1,0:T(8,128)(2,1)}, u32[]{:S(2)}, u32[]{:S(2)}) collective-permute-start(bf16[2,3,64,512]{3,2,1,0:T(8,128)(2,1)S(1)} %collective-permute-done.14.rest_13_), channel_id=1, source_target_pairs={{0,16},{1,9},{2,18},{3,11},{4,20},{5,13},{6,22},{7,15},{8,24},{9,1... | collective-permute-start | bytes 1179656 | tf_op jit(solution)/shard_map/ppermute | solution.py:39
  113.9 36.7 %collective-permute-start.20 = (bf16[4,3,64,512]{3,2,1,0:T(8,128)(2,1)S(1)}, bf16[4,3,64,512]{3,2,1,0:T(8,128)(2,1)S(1)}, u32[]{:S(2)}, u32[]{:S(2)}) collective-permute-start(bf16[4,3,64,512]{3,2,1,0:T(8,128)(2,1)S(1)} %constant_dynamic-update-slice_fusion.2.rest_8_), channel_id=1, source_target_pairs={{0,16},{1,9},{2,18},{3,11},{4,20},{5,13},{6,22},{7,15},{8,24},{9,1... | collective-permute-start | bytes 2359304 | tf_op jit(solution)/shard_map/ppermute | solution.py:39
  114.6 48.8 %collective-permute-start.21 = (bf16[4,3,64,512]{3,2,1,0:T(8,128)(2,1)S(1)}, bf16[4,3,64,512]{3,2,1,0:T(8,128)(2,1)S(1)}, u32[]{:S(2)}, u32[]{:S(2)}) collective-permute-start(bf16[4,3,64,512]{3,2,1,0:T(8,128)(2,1)S(1)} %collective-permute-done.19.rest_9_), channel_id=1, source_target_pairs={{0,16},{1,9},{2,18},{3,11},{4,20},{5,13},{6,22},{7,15},{8,24},{9,1... | collective-permute-start | bytes 2359304 | tf_op jit(solution)/shard_map/ppermute | solution.py:39
  128.7 22.0 %collective-permute-start.23 = (bf16[2,3,64,512]{3,2,1,0:T(8,128)(2,1)}, bf16[2,3,64,512]{3,2,1,0:T(8,128)(2,1)}, u32[]{:S(2)}, u32[]{:S(2)}) collective-permute-start(bf16[2,3,64,512]{3,2,1,0:T(8,128)(2,1)} %collective-permute-done.22.rest_12_), channel_id=1, source_target_pairs={{0,8},{1,17},{2,10},{3,19},{4,12},{5,21},{6,14},{7,23},{8,0},{9,25... | collective-permute-start | bytes 1179656 | tf_op jit(solution)/shard_map/ppermute | solution.py:39
  165.6 25.2 %collective-permute-start.30 = (bf16[4,3,64,512]{3,2,1,0:T(8,128)(2,1)}, bf16[4,3,64,512]{3,2,1,0:T(8,128)(2,1)S(1)}, u32[]{:S(2)}, u32[]{:S(2)}) collective-permute-start(bf16[4,3,64,512]{3,2,1,0:T(8,128)(2,1)} %get-tuple-element.146), channel_id=1, source_target_pairs={{0,8},{1,17},{2,10},{3,19},{4,12},{5,21},{6,14},{7,23},{8,0},{9,25... | collective-permute-start | bytes 2359304 | tf_op jit(solution)/shard_map/ppermute | solution.py:39
  179.4 22.9 %collective-permute-start.27 = (bf16[4,3,64,512]{3,2,1,0:T(8,128)(2,1)S(1)}, bf16[4,3,64,512]{3,2,1,0:T(8,128)(2,1)S(1)}, u32[]{:S(2)}, u32[]{:S(2)}) collective-permute-start(bf16[4,3,64,512]{3,2,1,0:T(8,128)(2,1)S(1)} %copy-done.48), channel_id=1, source_target_pairs={{0,8},{1,17},{2,10},{3,19},{4,12},{5,21},{6,14},{7,23},{8,0},{9,25... | collective-permute-start | bytes 2359304 | tf_op jit(solution)/shard_map/ppermute | solution.py:39
  190.8 18.0 %collective-permute-start.31 = (bf16[2,3,64,512]{3,2,1,0:T(8,128)(2,1)}, bf16[2,3,64,512]{3,2,1,0:T(8,128)(2,1)S(1)}, u32[]{:S(2)}, u32[]{:S(2)}) collective-permute-start(bf16[2,3,64,512]{3,2,1,0:T(8,128)(2,1)} %get-tuple-element.147), channel_id=1, source_target_pairs={{0,8},{1,17},{2,10},{3,19},{4,12},{5,21},{6,14},{7,23},{8,0},{9,25... | collective-permute-start | bytes 1179656 | tf_op jit(solution)/shard_map/ppermute | solution.py:39
  192.3 22.1 %collective-permute-start.35 = (bf16[4,3,64,512]{3,2,1,0:T(8,128)(2,1)S(1)}, bf16[4,3,64,512]{3,2,1,0:T(8,128)(2,1)S(1)}, u32[]{:S(2)}, u32[]{:S(2)}) collective-permute-start(bf16[4,3,64,512]{3,2,1,0:T(8,128)(2,1)S(1)} %add_convert_fusion.2), channel_id=1, source_target_pairs={{0,16},{1,9},{2,18},{3,11},{4,20},{5,13},{6,22},{7,15},{8,24},{9,1... | collective-permute-start | bytes 2359304 | tf_op jit(solution)/shard_map/ppermute | solution.py:39
  209.7 18.3 %collective-permute-start.38 = (bf16[2,3,64,512]{3,2,1,0:T(8,128)(2,1)S(1)}, bf16[2,3,64,512]{3,2,1,0:T(8,128)(2,1)S(1)}, u32[]{:S(2)}, u32[]{:S(2)}) collective-permute-start(bf16[2,3,64,512]{3,2,1,0:T(8,128)(2,1)S(1)} %add_convert_fusion.9), channel_id=1, source_target_pairs={{0,4},{1,5},{2,6},{3,7},{4,0},{5,1},{6,2},{7,3},{8,12},{9,13},{10,... | collective-permute-start | bytes 1179656 | tf_op jit(solution)/shard_map/ppermute | solution.py:24
  213.8 29.3 %collective-permute-start.29 = (bf16[4,3,64,512]{3,2,1,0:T(8,128)(2,1)S(1)}, bf16[4,3,64,512]{3,2,1,0:T(8,128)(2,1)S(1)}, u32[]{:S(2)}, u32[]{:S(2)}) collective-permute-start(bf16[4,3,64,512]{3,2,1,0:T(8,128)(2,1)S(1)} %copy-done.47), channel_id=1, source_target_pairs={{0,8},{1,17},{2,10},{3,19},{4,12},{5,21},{6,14},{7,23},{8,0},{9,25... | collective-permute-start | bytes 2359304 | tf_op jit(solution)/shard_map/ppermute | solution.py:39
  226.3 21.1 %collective-permute-start.44 = (bf16[2,3,64,512]{3,2,1,0:T(8,128)(2,1)S(1)}, bf16[2,3,64,512]{3,2,1,0:T(8,128)(2,1)S(1)}, u32[]{:S(2)}, u32[]{:S(2)}) collective-permute-start(bf16[2,3,64,512]{3,2,1,0:T(8,128)(2,1)S(1)} %copy-done.52), channel_id=1, source_target_pairs={{0,8},{1,17},{2,10},{3,19},{4,12},{5,21},{6,14},{7,23},{8,0},{9,25... | collective-permute-start | bytes 1179656 | tf_op jit(solution)/shard_map/ppermute | solution.py:39
  227.3 28.8 %collective-permute-start.37 = (bf16[4,3,64,512]{3,2,1,0:T(8,128)(2,1)S(1)}, bf16[4,3,64,512]{3,2,1,0:T(8,128)(2,1)S(1)}, u32[]{:S(2)}, u32[]{:S(2)}) collective-permute-start(bf16[4,3,64,512]{3,2,1,0:T(8,128)(2,1)S(1)} %add_convert_fusion.3), channel_id=1, source_target_pairs={{0,16},{1,9},{2,18},{3,11},{4,20},{5,13},{6,22},{7,15},{8,24},{9,1... | collective-permute-start | bytes 2359304 | tf_op jit(solution)/shard_map/ppermute | solution.py:39
  228.1 20.2 %collective-permute-start.41 = (bf16[2,3,64,512]{3,2,1,0:T(8,128)(2,1)S(1)}, bf16[2,3,64,512]{3,2,1,0:T(8,128)(2,1)S(1)}, u32[]{:S(2)}, u32[]{:S(2)}) collective-permute-start(bf16[2,3,64,512]{3,2,1,0:T(8,128)(2,1)S(1)} %get-tuple-element.164), channel_id=1, source_target_pairs={{0,2},{1,3},{2,0},{3,1},{4,6},{5,7},{6,4},{7,5},{8,10},{9,11},{10,... | collective-permute-start | bytes 1179656 | tf_op jit(solution)/shard_map/ppermute | solution.py:24
  229.3 19.2 %collective-permute-start.39 = (bf16[2,3,64,512]{3,2,1,0:T(8,128)(2,1)S(1)}, bf16[2,3,64,512]{3,2,1,0:T(8,128)(2,1)S(1)}, u32[]{:S(2)}, u32[]{:S(2)}) collective-permute-start(bf16[2,3,64,512]{3,2,1,0:T(8,128)(2,1)S(1)} %get-tuple-element.161), channel_id=1, source_target_pairs={{0,6},{1,7},{2,4},{3,5},{4,2},{5,3},{6,0},{7,1},{8,14},{9,15},{10,... | collective-permute-start | bytes 1179656 | tf_op jit(solution)/shard_map/ppermute | solution.py:24
  262.8 18.3 %collective-permute-start.43 = (bf16[2,3,64,512]{3,2,1,0:T(8,128)(2,1)S(1)}, bf16[2,3,64,512]{3,2,1,0:T(8,128)(2,1)S(1)}, u32[]{:S(2)}, u32[]{:S(2)}) collective-permute-start(bf16[2,3,64,512]{3,2,1,0:T(8,128)(2,1)S(1)} %get-tuple-element.166), channel_id=1, source_target_pairs={{0,6},{1,7},{2,4},{3,5},{4,2},{5,3},{6,0},{7,1},{8,14},{9,15},{10,... | collective-permute-start | bytes 1179656 | tf_op jit(solution)/shard_map/ppermute | solution.py:24
  (91 other events, 2095.0 us)

commit v3 on v2

--- a/solution.py
+++ b/solution.py
@@ -62,38 +62,60 @@
         copy.wait()
 
 
-def pick_kernel(wanted, extra, assign, *rest):
-    weights, rest = rest[:KINDS], rest[KINDS:]
-    given, outs, sems = rest[:extra], rest[extra:-1], rest[-1]
+def pick_kernel(wanted, assign, *rest):
+    weights, outs = rest[:KINDS], rest[KINDS:-2]
+    stage, sems = rest[-2:]
     me = lax.axis_index("expert")
-    copies = []
+    loads, stores = [], []
     for out, chunks in zip(outs, wanted):
-        for n, (s, k) in enumerate(chunks):
-            if s is None:
-                copies.append(pltpu.make_async_copy(given[0].at[k], out.at[n], sems.at[len(copies)]))
-                continue
+        first = len(loads)
+        for s, k in chunks:
             chosen = assign[s, xor(me, k)]
-            for w, ref in enumerate(weights):
-                copies.append(
-                    pltpu.make_async_copy(ref.at[chosen], out.at[n, w], sems.at[len(copies)])
-                )
-    run(copies)
-
-
-def pick(wanted, assign, weights, given=()):
+            n = len(loads)
+            loads.append(
+                [
+                    pltpu.make_async_copy(ref.at[chosen], stage.at[n, w], sems.at[n, w])
+                    for w, ref in enumerate(weights)
+                ]
+            )
+        stores.append(
+            (
+                first,
+                len(chunks),
+                pltpu.make_async_copy(
+                    stage.at[pl.ds(first, len(chunks))], out, sems.at[first, KINDS]
+                ),
+            )
+        )
+    for load in loads:
+        for copy in load:
+            copy.start()
+    for first, count, store in stores:
+        for load in loads[first : first + count]:
+            for copy in load:
+                copy.wait()
+        store.start()
+    for _, _, store in stores:
+        store.wait()
+
+
+def pick(wanted, assign, weights):
     chunk = (KINDS,) + weights[0].shape[1:]
     dtype = weights[0].dtype
-    count = sum(KINDS if s is not None else 1 for chunks in wanted for s, _ in chunks)
+    count = sum(map(len, wanted))
     return pl.pallas_call(
-        functools.partial(pick_kernel, wanted, len(given)),
+        functools.partial(pick_kernel, wanted),
         out_shape=[jax.ShapeDtypeStruct((len(chunks),) + chunk, dtype) for chunks in wanted],
-        in_specs=[SMEM] + [ANY] * (KINDS + len(given)),
-        out_specs=[VMEM] * len(wanted),
-        scratch_shapes=[pltpu.SemaphoreType.DMA((count,))],
+        in_specs=[SMEM] + [ANY] * KINDS,
+        out_specs=[ANY] * len(wanted),
+        scratch_shapes=[
+            pltpu.VMEM((count,) + chunk, dtype),
+            pltpu.SemaphoreType.DMA((count, KINDS + 1)),
+        ],
         compiler_params=params(),
-        cost_estimate=cost(0, 4 * sum(map(len, wanted)) * chunk[0] * chunk[1] * chunk[2]),
+        cost_estimate=cost(0, 4 * count * chunk[0] * chunk[1] * chunk[2]),
         name="pick",
-    )(assign, *weights, *given)
+    )(assign, *weights)
 
 
 def weight_loads(pieces, kept, target, sems, first):
@@ -326,7 +348,7 @@
 def finish_kernel(table, count, assign, *rest):
     pieces = rest[:count]
     outs = rest[count + KINDS : count + 2 * KINDS]
-    held, sems = rest[count + 2 * KINDS :]
+    held, terms, sems = rest[count + 2 * KINDS :]
     me = lax.axis_index("expert")
     chosen = [assign[s, xor(me, k)] for _, _, s, k in table]
     first = []
@@ -335,10 +357,22 @@
         for o in range(m - 1, -1, -1):
             slot = jnp.where(chosen[o] == chosen[m], o, slot)
         first.append(slot)
-    spots = [(m, w) for m in range(len(table)) for w in range(KINDS)]
-    run([pltpu.make_async_copy(outs[w].at[chosen[m]], held.at[m, w], sems.at[m, w]) for m, w in spots])
-    for m, (a, n, _, _) in enumerate(table):
-        held[first[m]] += pieces[a][n].astype(jnp.float32)
+    loads = [
+        [pltpu.make_async_copy(pieces[a].at[n], terms.at[m], sems.at[m, KINDS])]
+        + [
+            pltpu.make_async_copy(outs[w].at[chosen[m]], held.at[m, w], sems.at[m, w])
+            for w in range(KINDS)
+        ]
+        for m, (a, n, _, _) in enumerate(table)
+    ]
+    for load in loads:
+        for copy in load:
+            copy.start()
+    for load in loads:
+        for copy in load:
+            copy.wait()
+    for m in range(len(table)):
+        held[first[m]] += terms[m].astype(jnp.float32)
     for wait in (False, True):
         for m in range(len(table)):
 
@@ -359,11 +393,12 @@
     return pl.pallas_call(
         functools.partial(finish_kernel, table, len(arrays)),
         out_shape=[jax.ShapeDtypeStruct(t.shape, t.dtype) for t in totals],
-        in_specs=[SMEM] + [VMEM] * len(arrays) + [ANY] * KINDS,
+        in_specs=[SMEM] + [ANY] * (len(arrays) + KINDS),
         out_specs=[ANY] * KINDS,
         scratch_shapes=[
             pltpu.VMEM((len(table), KINDS) + shape, jnp.float32),
-            pltpu.SemaphoreType.DMA((len(table), KINDS)),
+            pltpu.VMEM((len(table), KINDS) + shape, arrays[0].dtype),
+            pltpu.SemaphoreType.DMA((len(table), KINDS + 1)),
         ],
         input_output_aliases={1 + len(arrays) + w: w for w in range(KINDS)},
         compiler_params=params(),
@@ -379,9 +414,10 @@
         self.plans = []
 
     def send(self, move, value, *way, behind=()):
-        behind = list(behind) + self.gates.get(len(self.sent), [])
-        if len(self.sent) >= self.depth:
-            behind.append(self.sent[-self.depth])
+        gate = self.gates.get(len(self.sent), [])
+        behind = list(behind) + list(gate() if callable(gate) else gate)
+        depth = self.depth
+        behind += self.sent[:-depth][-1:] + self.sent[: 1 - depth][-1:]
         if behind:
             value = after(value, *behind)
         self.sent.append(move(value, *way))
@@ -456,44 +492,47 @@
     weights = (gate_weight, up_weight, down_weight)
     every = range(steps)
     far = slots // 2
-    near = [k for k in range(2, slots, 2) if k != far]
+    near = [k for k in range(2, slots, 2) if k != far][::-1]
     remote = near + [far]
     position = {k: 2 * i for i, k in enumerate([0] + remote)}
     wide, deep = Line(3), Line(2)
 
-    own, mate_first, mate_rest = pick(
-        (
-            tuple((s, 0) for s in every),
-            tuple((s, 1) for s in every),
-            tuple((s, k ^ 1) for s in every for k in remote),
-        ),
+    moves = [(s, k) for s in every for k in remote]
+    pairs = [((s, k), (s, k ^ 1)) for s, k in moves]
+    own, mate, *messages = pick(
+        (tuple((s, 0) for s in every), tuple((s, 1) for s in every), *pairs[: len(near)]),
         assign,
         weights,
     )
-    mate_first = swap(mate_first, 1)
-    mate_rest = swap(mate_rest, 1)
-    wanted = tuple(
-        ((s, k), (None, s * len(remote) + i)) for s in every for i, k in enumerate(remote)
+    mate = swap(mate, 1)
+    wide.plan(
+        1,
+        lambda arrival: messages.extend(
+            pick(tuple(pairs[len(near) :]), after(assign, arrival), weights)
+        ),
     )
-    messages = pick(wanted, assign, weights, (mate_rest,))
-
-    moves = [(s, k) for s in every for k in remote]
+
     arrived = {}
+
+    def beside(s, k):
+        return (3 + 6 * s if k == far else 5 * s) * (parts - 1) // 3
 
     def fetch(key):
         while key not in arrived:
-            n = len(deep.sent)
-            s, k = moves[n]
-            at = 2 * n + 1 - len(near) % 2
-            behind = wide.sent[min(at, len(wide.sent) - 1) :][:1] if n >= len(near) else ()
-            arrived[s, k] = deep.send(swap, messages[n], k, behind=behind)
+            s, k = moves[len(deep.sent)]
+            behind = []
+            if s or k == far:
+                behind = wide.sent[: beside(s, k) + 1][-3:]
+                behind += [arrived[s, near[0]] if k == far and near else arrived[s - 1, far]]
+            arrived[s, k] = deep.send(swap, messages[len(deep.sent)], k, behind=behind)
 
     def ahead(arrival):
         n = len(deep.sent)
-        if n < len(moves) and 2 * n + 1 < len(wide.sent):
+        if n < len(moves) and beside(*moves[n]) < len(wide.sent):
             fetch(moves[n])
         wide.plan(1, ahead)
 
+    ready = []
     table = [[] for _ in every]
 
     def deliver(keys, array, places):
@@ -501,7 +540,11 @@
             fetch(key)
         if keys:
             pairs = [arrived[key] for key in keys]
-            array = pairs[0] if len(pairs) == 1 else jnp.concatenate(pairs)
+            theirs = [pair[1:] for pair in pairs]
+            theirs = theirs[0] if len(theirs) == 1 else jnp.concatenate(theirs)
+            theirs = after(theirs, *wide.sent[-3:], *messages[len(near) :][:1])
+            array = jnp.concatenate([pair[:1] for pair in pairs] + [swap(theirs, 1)])
+            ready.append(array)
 
         def done(have):
             for j, a in have.items():
@@ -512,12 +555,12 @@
 
     jobs = [
         deliver([], own, [(s, 0) for s in every]),
-        deliver([], mate_first, [(s, 1) for s in every]),
+        deliver([], mate, [(s, 1) for s in every]),
     ]
     for s in every:
         for group in (near, [far]):
             if group:
-                places = [(s, position[k] + c) for k in group for c in range(2)]
+                places = [(s, position[k] + c) for c in range(2) for k in group]
                 jobs.append(deliver([(s, k) for k in group], None, places))
     for k in near:
         fetch((0, k))
@@ -525,8 +568,9 @@
     overlap(jobs, parts - 1)
     wide.plans.clear()
 
+    counts = after(counts, ready[-1])
     token_grad = None
-    early, late = [], []
+    early, late, totals = [], [], []
     jobs = []
     for s in every:
         arrays = list({id(a): a for a, _, _, _ in table[s]}.values())
@@ -535,6 +579,8 @@
         hidden, gate_grad, up_grad = act(
             s, rows, units, batches, counts, tokens, upstream, places, arrays
         )
+        if s == 0:
+            hidden = after(hidden, wide.sent[-parts])
         groups = [g for g in ([far], near) if g]
         produced = weight_grads(
             s, parts, chunk, 1.0 / rows, tokens, upstream, hidden, gate_grad, up_grad,
@@ -545,11 +591,10 @@
         token_grad = input_grad(
             s, steps, gate_grad, up_grad, places, arrays, features, token_grad
         )
-        counts = after(counts, token_grad)
         jobs.append([(s, group, terms) for group, terms in zip(groups + [[0]], produced)])
 
     def returned(s, group):
-        home = late if group == [0] or (s == steps - 1 and group != [far]) else early
+        home = late if s == steps - 1 or group == [0] else early
 
         def mates(pairs):
             def go(arrival):
@@ -576,20 +621,28 @@
         return done
 
     base = len(wide.sent)
-    for n in range(parts - 1):
-        wide.gates[base + n] = [wide.sent[-1]]
-    wide.gates[base + 4 * parts - 6] = [token_grad]
+    wide.gates[base + parts - 2] = [wide.sent[-1]]
+    wide.gates[base + parts] = [wide.sent[-1]]
     remote_jobs = [job for step in jobs for job in step[:-1]]
     own_jobs = [step[-1] for step in jobs]
-    overlap(
-        [
-            collect(wide, terms, returned(s, group))
-            for s, group, terms in remote_jobs + own_jobs
-        ],
-        parts - 1,
-    )
+    jobs = [
+        collect(wide, terms, returned(s, group)) for s, group, terms in remote_jobs + own_jobs
+    ]
+    def place_early():
+        totals.extend(place(assign, early, experts))
+        return totals
+
+    back = len(moves)
+    wide.gates[base + 2 * parts - 3] = lambda: [deep.sent[back], wide.sent[-1]]
+    wide.gates[base + 4 * parts - 6] = lambda: [
+        token_grad,
+        *deep.sent[back + 1 : back + 1 + len(near)],
+    ]
+    wide.gates[base + 4 * parts - 3] = lambda: [deep.sent[back + 1 + len(near)]]
+    wide.gates[base + 4 * parts - 2] = place_early
+    wide.gates[base + 4 * parts + 1] = lambda: deep.sent[back + 2 + len(near) :][:1]
+    overlap(jobs, parts - 1)
     wide.settle(True)
-    totals = place(after(assign, token_grad), early, experts)
     totals = finish(assign, late, totals)
     return (token_grad, *totals)
 

time: 299 us -> 269 us (0.90)
  waiting for transfers between devices: 150 us -> 115 us
  starting transfers between devices: 56.5 us -> 61.3 us
    ppermute x36, waiting for transfers between devices: 76.7 us -> 32.2 us  [hop(): return lax.ppermute(value, ('dp', 'expert'), pairs)]
    ppermute x20 -> x23, waiting for transfers between devices: 73.3 us -> 82.8 us  [swap(): return lax.ppermute(value, 'expert', [(i, i ^ mask) for i in range(size)])]
    ppermute x36, starting transfers between devices: 36.5 us -> 41.6 us  [hop(): return lax.ppermute(value, ('dp', 'expert'), pairs)]
    ppermute x20 -> x23, starting transfers between devices: 20 us -> 19.7 us  [swap(): return lax.ppermute(value, 'expert', [(i, i ^ mask) for i in range(size)])]
  transfers between devices with their start and end apart: 56 -> 59, of which waited for: 20 -> 30; matrix products, arithmetic and copies ran while one was open for 1% -> 1% of each run, Pallas kernels for 25% -> 28%
where the time goes in v3:
time: 269 us; the launch traced here: 267 us
  waiting for transfers between devices  115 us (43%)
  Pallas kernels  82.6 us (31%)
  starting transfers between devices  61.3 us (23%)
  other arithmetic  3.76 us (1%)
    ppermute x23, waiting for transfers between devices, swap(): return lax.ppermute(value, 'expert', [(i, i ^ mask) for i in range(size)])  82.8 us
    ppermute x36, starting transfers between devices, hop(): return lax.ppermute(value, ('dp', 'expert'), pairs)  41.6 us
    ppermute x36, waiting for transfers between devices, hop(): return lax.ppermute(value, ('dp', 'expert'), pairs)  32.2 us
    pallas_call x2, Pallas kernels, act(): pl.pallas_call(functools.partial(act_kernel, step, batches, table, len(ar...  24.5 us
    pallas_call x2, Pallas kernels, weight_grads(): pl.pallas_call(functools.partial(weight_grads_kernel, step, scale, groups...  21 us
    ppermute x23, starting transfers between devices, swap(): return lax.ppermute(value, 'expert', [(i, i ^ mask) for i in range(size)])  19.7 us
    pallas_call x2, Pallas kernels, input_grad(): pl.pallas_call(functools.partial(input_grad_kernel, step, table, len(arra...  16.4 us
    pallas_call x1, Pallas kernels, place(): pl.pallas_call(functools.partial(place_kernel, table, len(arrays)), grid=...  8.21 us
  transfers between devices with their start and end apart: 59, of which 30 were waited for; matrix products, arithmetic and copies ran while one was open for 1% of the time, Pallas kernels for 28%

profile of v3, /device:TPU:0, one launch (start us, length us, event | category | flops | bytes accessed | tf_op | source)
XLA Modules:
  0.0 266.6 jit_solution(10632285953971985507)
XLA Ops:
  0.6 3.4 %pick.2 = (bf16[2,3,64,512]{3,2,1,0:T(8,128)(2,1)}, bf16[2,3,64,512]{3,2,1,0:T(8,128)(2,1)}, bf16[2,3,64,512]{3,2,1,0:T(8,128)(2,1)}, bf16[2,3,64,512]{3,2,1,0:T(8,128)(2,1)}) custom-call(s32[2,8]{1,0:T(2,128)} %assign.6, bf16[16,64,512]{2,1,0:T(8,128)(2,1)} %rest_0_.3, bf16[16,64,512]{2,1,0:T(8,128)(2,1)} %rest_1_.3, bf16[16,64,512]{2,1,0:T(8,128)(2,1)} %rest_2_.3), custom_call_target="tpu_custom_call" | custom-call | bytes 3145728 | tf_op jit(solution)/shard_map/pick/pallas_call | solution.py:106
  8.7 3.5 %collective-permute-start.1 = (bf16[2,3,64,512]{3,2,1,0:T(8,128)(2,1)}, bf16[2,3,64,512]{3,2,1,0:T(8,128)(2,1)S(1)}, u32[]{:S(2)}, u32[]{:S(2)}) collective-permute-start(bf16[2,3,64,512]{3,2,1,0:T(8,128)(2,1)} %get-tuple-element.105), channel_id=1, source_target_pairs={{0,6},{1,7},{2,4},{3,5},{4,2},{5,3},{6,0},{7,1},{8,14},{9,15},{10,... | collective-permute-start | bytes 1179656 | tf_op jit(solution)/shard_map/ppermute | solution.py:24
  12.2 4.2 %collective-permute-done.6.rest_2_ = bf16[2,3,64,512]{3,2,1,0:T(8,128)(2,1)S(1)} collective-permute-done((bf16[2,3,64,512]{3,2,1,0:T(8,128)(2,1)}, bf16[2,3,64,512]{3,2,1,0:T(8,128)(2,1)S(1)}, u32[]{:S(2)}, u32[]{:S(2)}) %collective-permute-start.6) | collective-permute-done | bytes 393248 | tf_op jit(solution)/shard_map/ppermute | solution.py:39
  26.0 4.1 %collective-permute-done.2 = bf16[2,3,64,512]{3,2,1,0:T(8,128)(2,1)S(1)} collective-permute-done((bf16[2,3,64,512]{3,2,1,0:T(8,128)(2,1)}, bf16[2,3,64,512]{3,2,1,0:T(8,128)(2,1)S(1)}, u32[]{:S(2)}, u32[]{:S(2)}) %collective-permute-start.2) | collective-permute-done | bytes 393248 | tf_op jit(solution)/shard_map/ppermute | solution.py:24
  41.9 16.8 %collective-permute-done.10 = bf16[2,3,64,512]{3,2,1,0:T(8,128)(2,1)S(1)} collective-permute-done((bf16[2,3,64,512]{3,2,1,0:T(8,128)(2,1)S(1)}, bf16[2,3,64,512]{3,2,1,0:T(8,128)(2,1)S(1)}, u32[]{:S(2)}, u32[]{:S(2)}) %collective-permute-start.10) | collective-permute-done | bytes 393248 | tf_op jit(solution)/shard_map/ppermute | solution.py:24
  58.7 3.6 %collective-permute-start.16 = (bf16[2,3,64,512]{3,2,1,0:T(8,128)(2,1)S(1)}, bf16[2,3,64,512]{3,2,1,0:T(8,128)(2,1)S(1)}, u32[]{:S(2)}, u32[]{:S(2)}) collective-permute-start(bf16[2,3,64,512]{3,2,1,0:T(8,128)(2,1)S(1)} %copy-done.57), channel_id=1, source_target_pairs={{0,6},{1,7},{2,4},{3,5},{4,2},{5,3},{6,0},{7,1},{8,14},{9,15},{10,... | collective-permute-start | bytes 1179656 | tf_op jit(solution)/shard_map/ppermute | solution.py:24
  65.9 6.7 %collective-permute-done.16 = bf16[2,3,64,512]{3,2,1,0:T(8,128)(2,1)S(1)} collective-permute-done((bf16[2,3,64,512]{3,2,1,0:T(8,128)(2,1)S(1)}, bf16[2,3,64,512]{3,2,1,0:T(8,128)(2,1)S(1)}, u32[]{:S(2)}, u32[]{:S(2)}) %collective-permute-start.16) | collective-permute-done | bytes 393248 | tf_op jit(solution)/shard_map/ppermute | solution.py:24
  72.7 7.4 %collective-permute-done.18 = bf16[2,3,64,512]{3,2,1,0:T(8,128)(2,1)S(1)} collective-permute-done((bf16[2,3,64,512]{3,2,1,0:T(8,128)(2,1)S(1)}, bf16[2,3,64,512]{3,2,1,0:T(8,128)(2,1)S(1)}, u32[]{:S(2)}, u32[]{:S(2)}) %collective-permute-start.18) | collective-permute-done | bytes 393248 | tf_op jit(solution)/shard_map/ppermute | solution.py:24
  89.1 16.5 %collective-permute-done.17 = bf16[2,3,64,512]{3,2,1,0:T(8,128)(2,1)S(1)} collective-permute-done((bf16[2,3,64,512]{3,2,1,0:T(8,128)(2,1)S(1)}, bf16[2,3,64,512]{3,2,1,0:T(8,128)(2,1)S(1)}, u32[]{:S(2)}, u32[]{:S(2)}) %collective-permute-start.17) | collective-permute-done | bytes 393248 | tf_op jit(solution)/shard_map/ppermute | solution.py:24
  111.4 12.2 %act.3 = (bf16[768,512]{1,0:T(8,128)(2,1)}, bf16[768,512]{1,0:T(8,128)(2,1)}, bf16[768,512]{1,0:T(8,128)(2,1)}) custom-call(s32[16]{0:T(128)} %counts.1, bf16[1536,2048]{1,0:T(8,128)(2,1)} %tokens.7, bf16[1536,2048]{1,0:T(8,128)(2,1)} %upstream.7, bf16[2,3,64,512]{3,2,1,0:T(8,128)(2,1)} %get-tuple-element.102.rest_0_, bf16[2,3,64,512]{3,2,1,0:T(8,128)(2,1)} %copy-done.4, ...), custom_call_target="tpu_custom_call" | custom-call | flops 4831838208 | bytes 12582912 | tf_op jit(solution)/shard_map/act/pallas_call | solution.py:181
  125.0 10.5 %weight_grads.3 = (bf16[2,3,64,512]{3,2,1,0:T(8,128)(2,1)}, bf16[2,3,64,512]{3,2,1,0:T(8,128)(2,1)}, bf16[2,3,64,512]{3,2,1,0:T(8,128)(2,1)}, bf16[2,3,64,512]{3...) custom-call(bf16[1536,2048]{1,0:T(8,128)(2,1)} %tokens.7, ...), custom_call_target="tpu_custom_call" | custom-call | flops 4831838208 | bytes 12582912 | tf_op jit(solution)/shard_map/weight_grads/pallas_call | solution.py:253
  139.4 4.2 %collective-permute-done.29 = bf16[2,3,64,512]{3,2,1,0:T(8,128)(2,1)S(1)} collective-permute-done((bf16[2,3,64,512]{3,2,1,0:T(8,128)(2,1)}, bf16[2,3,64,512]{3,2,1,0:T(8,128)(2,1)S(1)}, u32[]{:S(2)}, u32[]{:S(2)}) %collective-permute-start.29) | collective-permute-done | bytes 393248 | tf_op jit(solution)/shard_map/ppermute | solution.py:39
  145.6 12.3 %act.2 = (bf16[768,512]{1,0:T(8,128)(2,1)}, bf16[768,512]{1,0:T(8,128)(2,1)}, bf16[768,512]{1,0:T(8,128)(2,1)}) custom-call(s32[16]{0:T(128)} %counts.1, bf16[1536,2048]{1,0:T(8,128)(2,1)} %tokens.7, bf16[1536,2048]{1,0:T(8,128)(2,1)} %upstream.7, bf16[2,3,64,512]{3,2,1,0:T(8,128)(2,1)} %get-tuple-element.102.rest_0_, bf16[2,3,64,512]{3,2,1,0:T(8,128)(2,1)} %copy-done.4, ...), custom_call_target="tpu_custom_call" | custom-call | flops 4831838208 | bytes 12582912 | tf_op jit(solution)/shard_map/act/pallas_call | solution.py:181
  162.1 10.5 %weight_grads.2 = (bf16[2,3,64,512]{3,2,1,0:T(8,128)(2,1)}, bf16[2,3,64,512]{3,2,1,0:T(8,128)(2,1)}, bf16[2,3,64,512]{3,2,1,0:T(8,128)(2,1)}, bf16[2,3,64,512]{3...) custom-call(bf16[1536,2048]{1,0:T(8,128)(2,1)} %tokens.7, ...), custom_call_target="tpu_custom_call" | custom-call | flops 4831838208 | bytes 12582912 | tf_op jit(solution)/shard_map/weight_grads/pallas_call | solution.py:253
  172.6 4.8 %collective-permute-done.32 = bf16[4,3,64,512]{3,2,1,0:T(8,128)(2,1)S(1)} collective-permute-done((bf16[4,3,64,512]{3,2,1,0:T(8,128)(2,1)S(1)}, bf16[4,3,64,512]{3,2,1,0:T(8,128)(2,1)S(1)}, u32[]{:S(2)}, u32[]{:S(2)}) %collective-permute-start.32) | collective-permute-done | bytes 786464 | tf_op jit(solution)/shard_map/ppermute | solution.py:39
  179.9 8.2 %input_grad.2.rest_16_ = bf16[1536,2048]{1,0:T(8,128)(2,1)} custom-call(bf16[768,512]{1,0:T(8,128)(2,1)} %get-tuple-element.137.gate_grad, bf16[768,512]{1,0:T(8,128)(2,1)} %get-tuple-element.138.up_grad, bf16[2,3,64,512]{3,2,1,0:T(8,128)(2,1)} %get-tuple-element.102.rest_0_, bf16[2,3,64,512]{3,2,1,0:T(8,128)(2,1)} %copy-done.4, ...), custom_call_target="tpu_custom_call" | custom-call | flops 3221225472 | bytes 7340032 | tf_op jit(solution)/shard_map/input_grad/pallas_call | solution.py:299
  193.7 8.2 %input_grad.3 = bf16[1536,2048]{1,0:T(8,128)(2,1)} custom-call(bf16[768,512]{1,0:T(8,128)(2,1)} %get-tuple-element.135.gate_grad, bf16[768,512]{1,0:T(8,128)(2,1)} %get-tuple-element.136.up_grad, bf16[2,3,64,512]{3,2,1,0:T(8,128)(2,1)} %get-tuple-element.102.rest_0_, bf16[2,3,64,512]{3,2,1,0:T(8,128)(2,1)} %copy-done.4, ...), custom_call_target="tpu_custom_call", output_to_operand_aliasing={{}: (18, {})} | custom-call | flops 3221225472 | bytes 7340032 | tf_op jit(solution)/shard_map/input_grad/pallas_call | solution.py:299
  204.8 5.5 %collective-permute-done.44.rest_3_ = bf16[2,3,64,512]{3,2,1,0:T(8,128)(2,1)S(1)} collective-permute-done((bf16[2,3,64,512]{3,2,1,0:T(8,128)(2,1)S(1)}, bf16[2,3,64,512]{3,2,1,0:T(8,128)(2,1)S(1)}, u32[]{:S(2)}, u32[]{:S(2)}) %collective-permute-start.44) | collective-permute-done | bytes 393248 | tf_op jit(solution)/shard_map/ppermute | solution.py:24
  216.2 8.2 %place.1 = (f32[16,64,512]{2,1,0:T(8,128)}, f32[16,64,512]{2,1,0:T(8,128)}, f32[16,64,512]{2,1,0:T(8,128)}) custom-call(s32[2,8]{1,0:T(2,128)} %assign.6, bf16[2,3,64,512]{3,2,1,0:T(8,128)(2,1)} %copy-done.28, bf16[1,3,64,512]{3,2,1,0:T(8,128)(2,1)} %copy-done.44, bf16[2,3,64,512]{3,2,1,0:T(8,128)(2,1)} %copy-done.29, bf16[2,3,64,512]{3,2,1,0:T(8,128)(2,1)} %copy-done.30, ...), custom_call_target="tpu_custom_call" | custom-call | tf_op jit(solution)/shard_map/place/pallas_call | solution.py:337
  224.4 9.5 %collective-permute-done.40.rest_0_ = bf16[2,3,64,512]{3,2,1,0:T(8,128)(2,1)S(1)} collective-permute-done((bf16[2,3,64,512]{3,2,1,0:T(8,128)(2,1)S(1)}, bf16[2,3,64,512]{3,2,1,0:T(8,128)(2,1)S(1)}, u32[]{:S(2)}, u32[]{:S(2)}) %collective-permute-start.40) | collective-permute-done | bytes 393248 | tf_op jit(solution)/shard_map/ppermute | solution.py:24
  239.6 3.4 %collective-permute-done.51 = bf16[2,3,64,512]{3,2,1,0:T(8,128)(2,1)S(1)} collective-permute-done((bf16[2,3,64,512]{3,2,1,0:T(8,128)(2,1)S(1)}, bf16[2,3,64,512]{3,2,1,0:T(8,128)(2,1)S(1)}, u32[]{:S(2)}, u32[]{:S(2)}) %collective-permute-start.51) | collective-permute-done | bytes 393248 | tf_op jit(solution)/shard_map/ppermute | solution.py:39
  244.8 5.3 %collective-permute-done.56 = bf16[2,3,64,512]{3,2,1,0:T(8,128)(2,1)S(1)} collective-permute-done((bf16[2,3,64,512]{3,2,1,0:T(8,128)(2,1)S(1)}, bf16[2,3,64,512]{3,2,1,0:T(8,128)(2,1)S(1)}, u32[]{:S(2)}, u32[]{:S(2)}) %collective-permute-start.56) | collective-permute-done | bytes 393248 | tf_op jit(solution)/shard_map/ppermute | solution.py:39
  252.2 5.1 %collective-permute-done.47.rest_3_ = bf16[2,3,64,512]{3,2,1,0:T(8,128)(2,1)S(1)} collective-permute-done((bf16[2,3,64,512]{3,2,1,0:T(8,128)(2,1)S(1)}, bf16[2,3,64,512]{3,2,1,0:T(8,128)(2,1)S(1)}, u32[]{:S(2)}, u32[]{:S(2)}) %collective-permute-start.47) | collective-permute-done | bytes 393248 | tf_op jit(solution)/shard_map/ppermute | solution.py:24
  260.6 5.8 %finish.1 = (f32[16,64,512]{2,1,0:T(8,128)}, f32[16,64,512]{2,1,0:T(8,128)}, f32[16,64,512]{2,1,0:T(8,128)}) custom-call(s32[2,8]{1,0:T(2,128)} %assign.6, bf16[2,3,64,512]{3,2,1,0:T(8,128)(2,1)} %copy-done.25, bf16[1,3,64,512]{3,2,1,0:T(8,128)(2,1)} %copy-done.45, ...), custom_call_target="tpu_custom_call", output_to_operand_aliasing={{0}: (10, {}), {1}: (11, {}), {2}: (12, {})} | custom-call | tf_op jit(solution)/shard_map/finish/pallas_call | solution.py:393
  (260 shorter events, 84.6 us)
Async XLA Ops:
  12.2 17.9 %collective-permute-start.2 = (bf16[2,3,64,512]{3,2,1,0:T(8,128)(2,1)}, bf16[2,3,64,512]{3,2,1,0:T(8,128)(2,1)S(1)}, u32[]{:S(2)}, u32[]{:S(2)}) collective-permute-start(bf16[2,3,64,512]{3,2,1,0:T(8,128)(2,1)} %get-tuple-element.106), channel_id=1, source_target_pairs={{0,2},{1,3},{2,0},{3,1},{4,6},{5,7},{6,4},{7,5},{8,10},{9,11},{10,... | collective-permute-start | bytes 1179656 | tf_op jit(solution)/shard_map/ppermute | solution.py:24
  35.1 23.6 %collective-permute-start.11 = (bf16[4,3,64,512]{3,2,1,0:T(8,128)(2,1)S(1)}, bf16[4,3,64,512]{3,2,1,0:T(8,128)(2,1)S(1)}, u32[]{:S(2)}, u32[]{:S(2)}) collective-permute-start(bf16[4,3,64,512]{3,2,1,0:T(8,128)(2,1)S(1)} %pad_maximum_fusion.rest_8_), channel_id=1, source_target_pairs={{0,8},{1,17},{2,10},{3,19},{4,12},{5,21},{6,14},{7,23},{8,0},{9,25... | collective-permute-start | bytes 2359304 | tf_op jit(solution)/shard_map/ppermute | solution.py:39
  37.0 25.3 %collective-permute-start.9 = (bf16[4,3,64,512]{3,2,1,0:T(8,128)(2,1)S(1)}, bf16[4,3,64,512]{3,2,1,0:T(8,128)(2,1)S(1)}, u32[]{:S(2)}, u32[]{:S(2)}) collective-permute-start(bf16[4,3,64,512]{3,2,1,0:T(8,128)(2,1)S(1)} %pad_maximum_fusion.rest_8_), channel_id=1, source_target_pairs={{0,16},{1,9},{2,18},{3,11},{4,20},{5,13},{6,22},{7,15},{8,24},{9,1... | collective-permute-start | bytes 2359304 | tf_op jit(solution)/shard_map/ppermute | solution.py:39
  38.8 19.9 %collective-permute-start.10 = (bf16[2,3,64,512]{3,2,1,0:T(8,128)(2,1)S(1)}, bf16[2,3,64,512]{3,2,1,0:T(8,128)(2,1)S(1)}, u32[]{:S(2)}, u32[]{:S(2)}) collective-permute-start(bf16[2,3,64,512]{3,2,1,0:T(8,128)(2,1)S(1)} %copy-done.59), channel_id=1, source_target_pairs={{0,4},{1,5},{2,6},{3,7},{4,0},{5,1},{6,2},{7,3},{8,12},{9,13},{10,... | collective-permute-start | bytes 1179656 | tf_op jit(solution)/shard_map/ppermute | solution.py:24
  41.4 20.9 %collective-permute-start.12 = (bf16[2,3,64,512]{3,2,1,0:T(8,128)(2,1)S(1)}, bf16[2,3,64,512]{3,2,1,0:T(8,128)(2,1)S(1)}, u32[]{:S(2)}, u32[]{:S(2)}) collective-permute-start(bf16[2,3,64,512]{3,2,1,0:T(8,128)(2,1)S(1)} %collective-permute-done.4.rest_5_), channel_id=1, source_target_pairs={{0,16},{1,9},{2,18},{3,11},{4,20},{5,13},{6,22},{7,15},{8,24},{9,1... | collective-permute-start | bytes 1179656 | tf_op jit(solution)/shard_map/ppermute | solution.py:39
  62.4 20.5 %collective-permute-start.15 = (bf16[4,3,64,512]{3,2,1,0:T(8,128)(2,1)S(1)}, bf16[4,3,64,512]{3,2,1,0:T(8,128)(2,1)S(1)}, u32[]{:S(2)}, u32[]{:S(2)}) collective-permute-start(bf16[4,3,64,512]{3,2,1,0:T(8,128)(2,1)S(1)} %collective-permute-done.11.rest_9_), channel_id=1, source_target_pairs={{0,16},{1,9},{2,18},{3,11},{4,20},{5,13},{6,22},{7,15},{8,24},{9,1... | collective-permute-start | bytes 2359304 | tf_op jit(solution)/shard_map/ppermute | solution.py:39
  64.8 18.1 %collective-permute-start.19 = (bf16[2,3,64,512]{3,2,1,0:T(8,128)(2,1)S(1)}, bf16[2,3,64,512]{3,2,1,0:T(8,128)(2,1)S(1)}, u32[]{:S(2)}, u32[]{:S(2)}) collective-permute-start(bf16[2,3,64,512]{3,2,1,0:T(8,128)(2,1)S(1)} %pad_maximum_fusion.3.rest_12_), channel_id=1, source_target_pairs={{0,16},{1,9},{2,18},{3,11},{4,20},{5,13},{6,22},{7,15},{8,24},{9,1... | collective-permute-start | bytes 1179656 | tf_op jit(solution)/shard_map/ppermute | solution.py:39
  84.8 23.9 %collective-permute-start.21 = (bf16[4,3,64,512]{3,2,1,0:T(8,128)(2,1)S(1)}, bf16[4,3,64,512]{3,2,1,0:T(8,128)(2,1)S(1)}, u32[]{:S(2)}, u32[]{:S(2)}) collective-permute-start(bf16[4,3,64,512]{3,2,1,0:T(8,128)(2,1)S(1)} %pad_maximum_fusion.1.rest_8_), channel_id=1, source_target_pairs={{0,8},{1,17},{2,10},{3,19},{4,12},{5,21},{6,14},{7,23},{8,0},{9,25... | collective-permute-start | bytes 2359304 | tf_op jit(solution)/shard_map/ppermute | solution.py:39
  85.2 23.5 %collective-permute-start.23 = (bf16[4,3,64,512]{3,2,1,0:T(8,128)(2,1)S(1)}, bf16[4,3,64,512]{3,2,1,0:T(8,128)(2,1)S(1)}, u32[]{:S(2)}, u32[]{:S(2)}) collective-permute-start(bf16[4,3,64,512]{3,2,1,0:T(8,128)(2,1)S(1)} %pad_maximum_fusion.1.rest_8_), channel_id=1, source_target_pairs={{0,16},{1,9},{2,18},{3,11},{4,20},{5,13},{6,22},{7,15},{8,24},{9,1... | collective-permute-start | bytes 2359304 | tf_op jit(solution)/shard_map/ppermute | solution.py:39
  85.7 19.9 %collective-permute-start.17 = (bf16[2,3,64,512]{3,2,1,0:T(8,128)(2,1)S(1)}, bf16[2,3,64,512]{3,2,1,0:T(8,128)(2,1)S(1)}, u32[]{:S(2)}, u32[]{:S(2)}) collective-permute-start(bf16[2,3,64,512]{3,2,1,0:T(8,128)(2,1)S(1)} %copy-done.55), channel_id=1, source_target_pairs={{0,4},{1,5},{2,6},{3,7},{4,0},{5,1},{6,2},{7,3},{8,12},{9,13},{10,... | collective-permute-start | bytes 1179656 | tf_op jit(solution)/shard_map/ppermute | solution.py:24
  88.0 20.7 %collective-permute-start.22 = (bf16[2,3,64,512]{3,2,1,0:T(8,128)(2,1)S(1)}, bf16[2,3,64,512]{3,2,1,0:T(8,128)(2,1)S(1)}, u32[]{:S(2)}, u32[]{:S(2)}) collective-permute-start(bf16[2,3,64,512]{3,2,1,0:T(8,128)(2,1)S(1)} %collective-permute-done.14.rest_13_), channel_id=1, source_target_pairs={{0,16},{1,9},{2,18},{3,11},{4,20},{5,13},{6,22},{7,15},{8,24},{9,1... | collective-permute-start | bytes 1179656 | tf_op jit(solution)/shard_map/ppermute | solution.py:39
  108.9 26.7 %collective-permute-start.25 = (bf16[4,3,64,512]{3,2,1,0:T(8,128)(2,1)S(1)}, bf16[4,3,64,512]{3,2,1,0:T(8,128)(2,1)S(1)}, u32[]{:S(2)}, u32[]{:S(2)}) collective-permute-start(bf16[4,3,64,512]{3,2,1,0:T(8,128)(2,1)S(1)} %collective-permute-done.21.rest_9_), channel_id=1, source_target_pairs={{0,16},{1,9},{2,18},{3,11},{4,20},{5,13},{6,22},{7,15},{8,24},{9,1... | collective-permute-start | bytes 2359304 | tf_op jit(solution)/shard_map/ppermute | solution.py:39
  110.6 26.8 %collective-permute-start.27 = (bf16[2,3,64,512]{3,2,1,0:T(8,128)(2,1)S(1)}, bf16[2,3,64,512]{3,2,1,0:T(8,128)(2,1)S(1)}, u32[]{:S(2)}, u32[]{:S(2)}) collective-permute-start(bf16[2,3,64,512]{3,2,1,0:T(8,128)(2,1)S(1)} %pad_maximum_fusion.5.rest_12_), channel_id=1, source_target_pairs={{0,16},{1,9},{2,18},{3,11},{4,20},{5,13},{6,22},{7,15},{8,24},{9,1... | collective-permute-start | bytes 1179656 | tf_op jit(solution)/shard_map/ppermute | solution.py:39
  137.4 20.5 %collective-permute-start.31 = (bf16[2,3,64,512]{3,2,1,0:T(8,128)(2,1)}, bf16[2,3,64,512]{3,2,1,0:T(8,128)(2,1)S(1)}, u32[]{:S(2)}, u32[]{:S(2)}) collective-permute-start(bf16[2,3,64,512]{3,2,1,0:T(8,128)(2,1)} %get-tuple-element.150), channel_id=1, source_target_pairs={{0,8},{1,17},{2,10},{3,19},{4,12},{5,21},{6,14},{7,23},{8,0},{9,25... | collective-permute-start | bytes 1179656 | tf_op jit(solution)/shard_map/ppermute | solution.py:39
  137.7 23.2 %collective-permute-start.35 = (bf16[4,3,64,512]{3,2,1,0:T(8,128)(2,1)}, bf16[4,3,64,512]{3,2,1,0:T(8,128)(2,1)S(1)}, u32[]{:S(2)}, u32[]{:S(2)}) collective-permute-start(bf16[4,3,64,512]{3,2,1,0:T(8,128)(2,1)} %get-tuple-element.158), channel_id=1, source_target_pairs={{0,8},{1,17},{2,10},{3,19},{4,12},{5,21},{6,14},{7,23},{8,0},{9,25... | collective-permute-start | bytes 2359304 | tf_op jit(solution)/shard_map/ppermute | solution.py:39
  158.0 19.5 %collective-permute-start.32 = (bf16[4,3,64,512]{3,2,1,0:T(8,128)(2,1)S(1)}, bf16[4,3,64,512]{3,2,1,0:T(8,128)(2,1)S(1)}, u32[]{:S(2)}, u32[]{:S(2)}) collective-permute-start(bf16[4,3,64,512]{3,2,1,0:T(8,128)(2,1)S(1)} %copy-done.50), channel_id=1, source_target_pairs={{0,8},{1,17},{2,10},{3,19},{4,12},{5,21},{6,14},{7,23},{8,0},{9,25... | collective-permute-start | bytes 2359304 | tf_op jit(solution)/shard_map/ppermute | solution.py:39
  159.9 18.2 %collective-permute-start.34 = (bf16[2,3,64,512]{3,2,1,0:T(8,128)(2,1)S(1)}, bf16[2,3,64,512]{3,2,1,0:T(8,128)(2,1)S(1)}, u32[]{:S(2)}, u32[]{:S(2)}) collective-permute-start(bf16[2,3,64,512]{3,2,1,0:T(8,128)(2,1)S(1)} %add_convert_fusion.10), channel_id=1, source_target_pairs={{0,4},{1,5},{2,6},{3,7},{4,0},{5,1},{6,2},{7,3},{8,12},{9,13},{10,... | collective-permute-start | bytes 1179656 | tf_op jit(solution)/shard_map/ppermute | solution.py:24
  161.1 29.1 %collective-permute-start.37 = (bf16[4,3,64,512]{3,2,1,0:T(8,128)(2,1)S(1)}, bf16[4,3,64,512]{3,2,1,0:T(8,128)(2,1)S(1)}, u32[]{:S(2)}, u32[]{:S(2)}) collective-permute-start(bf16[4,3,64,512]{3,2,1,0:T(8,128)(2,1)S(1)} %add_convert_fusion.3), channel_id=1, source_target_pairs={{0,16},{1,9},{2,18},{3,11},{4,20},{5,13},{6,22},{7,15},{8,24},{9,1... | collective-permute-start | bytes 2359304 | tf_op jit(solution)/shard_map/ppermute | solution.py:39
  188.8 22.5 %collective-permute-start.41 = (bf16[4,3,64,512]{3,2,1,0:T(8,128)(2,1)S(1)}, bf16[4,3,64,512]{3,2,1,0:T(8,128)(2,1)S(1)}, u32[]{:S(2)}, u32[]{:S(2)}) collective-permute-start(bf16[4,3,64,512]{3,2,1,0:T(8,128)(2,1)S(1)} %copy-done.49), channel_id=1, source_target_pairs={{0,8},{1,17},{2,10},{3,19},{4,12},{5,21},{6,14},{7,23},{8,0},{9,25... | collective-permute-start | bytes 2359304 | tf_op jit(solution)/shard_map/ppermute | solution.py:39
  192.6 18.9 %collective-permute-start.38 = (bf16[2,3,64,512]{3,2,1,0:T(8,128)(2,1)S(1)}, bf16[2,3,64,512]{3,2,1,0:T(8,128)(2,1)S(1)}, u32[]{:S(2)}, u32[]{:S(2)}) collective-permute-start(bf16[2,3,64,512]{3,2,1,0:T(8,128)(2,1)S(1)} %add_convert_fusion.9), channel_id=1, source_target_pairs={{0,16},{1,9},{2,18},{3,11},{4,20},{5,13},{6,22},{7,15},{8,24},{9,1... | collective-permute-start | bytes 1179656 | tf_op jit(solution)/shard_map/ppermute | solution.py:39
  210.3 23.5 %collective-permute-start.45 = (bf16[4,3,64,512]{3,2,1,0:T(8,128)(2,1)S(1)}, bf16[4,3,64,512]{3,2,1,0:T(8,128)(2,1)S(1)}, u32[]{:S(2)}, u32[]{:S(2)}) collective-permute-start(bf16[4,3,64,512]{3,2,1,0:T(8,128)(2,1)S(1)} %copy-done.48), channel_id=1, source_target_pairs={{0,8},{1,17},{2,10},{3,19},{4,12},{5,21},{6,14},{7,23},{8,0},{9,25... | collective-permute-start | bytes 2359304 | tf_op jit(solution)/shard_map/ppermute | solution.py:39
  211.6 24.4 %collective-permute-start.42 = (bf16[4,3,64,512]{3,2,1,0:T(8,128)(2,1)S(1)}, bf16[4,3,64,512]{3,2,1,0:T(8,128)(2,1)S(1)}, u32[]{:S(2)}, u32[]{:S(2)}) collective-permute-start(bf16[4,3,64,512]{3,2,1,0:T(8,128)(2,1)S(1)} %add_convert_fusion.1), channel_id=1, source_target_pairs={{0,16},{1,9},{2,18},{3,11},{4,20},{5,13},{6,22},{7,15},{8,24},{9,1... | collective-permute-start | bytes 2359304 | tf_op jit(solution)/shard_map/ppermute | solution.py:39
  213.7 20.2 %collective-permute-start.40 = (bf16[2,3,64,512]{3,2,1,0:T(8,128)(2,1)S(1)}, bf16[2,3,64,512]{3,2,1,0:T(8,128)(2,1)S(1)}, u32[]{:S(2)}, u32[]{:S(2)}) collective-permute-start(bf16[2,3,64,512]{3,2,1,0:T(8,128)(2,1)S(1)} %add_convert_fusion.8), channel_id=1, source_target_pairs={{0,4},{1,5},{2,6},{3,7},{4,0},{5,1},{6,2},{7,3},{8,12},{9,13},{10,... | collective-permute-start | bytes 1179656 | tf_op jit(solution)/shard_map/ppermute | solution.py:24
  214.4 20.8 %collective-permute-start.48 = (bf16[2,3,64,512]{3,2,1,0:T(8,128)(2,1)S(1)}, bf16[2,3,64,512]{3,2,1,0:T(8,128)(2,1)S(1)}, u32[]{:S(2)}, u32[]{:S(2)}) collective-permute-start(bf16[2,3,64,512]{3,2,1,0:T(8,128)(2,1)S(1)} %copy-done.53), channel_id=1, source_target_pairs={{0,8},{1,17},{2,10},{3,19},{4,12},{5,21},{6,14},{7,23},{8,0},{9,25... | collective-permute-start | bytes 1179656 | tf_op jit(solution)/shard_map/ppermute | solution.py:39
  (95 other events, 1218.2 us)

commit v4 on v3

--- a/solution.py
+++ b/solution.py
@@ -633,7 +633,10 @@
         return totals
 
     back = len(moves)
-    wide.gates[base + 2 * parts - 3] = lambda: [deep.sent[back], wide.sent[-1]]
+    wide.gates[base + 2 * parts - 3] = lambda: [wide.sent[-1]]
+    wide.gates[base + 2 * parts] = lambda: [deep.sent[back]]
+    wide.gates[base + parts - 1] = [hidden]
+    wide.gates[base + 2 * parts - 2] = [produced[0][0]]
     wide.gates[base + 4 * parts - 6] = lambda: [
         token_grad,
         *deep.sent[back + 1 : back + 1 + len(near)],

time: 269 us -> 265 us (0.985)
    ppermute x36, waiting for transfers between devices: 32.2 us -> 29.3 us  [hop(): return lax.ppermute(value, ('dp', 'expert'), pairs)]
  transfers between devices with their start and end apart: 59 -> 59, of which waited for: 30 -> 29; matrix products, arithmetic and copies ran while one was open for 1% -> 1% of each run, Pallas kernels for 28% -> 28%
where the time goes in v4:
time: 265 us; the launch traced here: 263 us
  waiting for transfers between devices  113 us (43%)
  Pallas kernels  82.5 us (31%)
  starting transfers between devices  60.8 us (23%)
  other arithmetic  2.76 us (1%)
    ppermute x23, waiting for transfers between devices, swap(): return lax.ppermute(value, 'expert', [(i, i ^ mask) for i in range(size)])  83.7 us
    ppermute x36, starting transfers between devices, hop(): return lax.ppermute(value, ('dp', 'expert'), pairs)  39.7 us
    ppermute x36, waiting for transfers between devices, hop(): return lax.ppermute(value, ('dp', 'expert'), pairs)  29.3 us
    pallas_call x2, Pallas kernels, act(): pl.pallas_call(functools.partial(act_kernel, step, batches, table, len(ar...  24.5 us
    ppermute x23, starting transfers between devices, swap(): return lax.ppermute(value, 'expert', [(i, i ^ mask) for i in range(size)])  21.1 us
    pallas_call x2, Pallas kernels, weight_grads(): pl.pallas_call(functools.partial(weight_grads_kernel, step, scale, groups...  21.1 us
    pallas_call x2, Pallas kernels, input_grad(): pl.pallas_call(functools.partial(input_grad_kernel, step, table, len(arra...  16.4 us
    pallas_call x1, Pallas kernels, place(): pl.pallas_call(functools.partial(place_kernel, table, len(arrays)), grid=...  8.24 us
  transfers between devices with their start and end apart: 59, of which 29 were waited for; matrix products, arithmetic and copies ran while one was open for 1% of the time, Pallas kernels for 28%

profile of v4, /device:TPU:0, one launch (start us, length us, event | category | flops | bytes accessed | tf_op | source)
XLA Modules:
  0.0 263.0 jit_solution(6575087579882025430)
XLA Ops:
  0.6 3.1 %pick.2 = (bf16[2,3,64,512]{3,2,1,0:T(8,128)(2,1)}, bf16[2,3,64,512]{3,2,1,0:T(8,128)(2,1)}, bf16[2,3,64,512]{3,2,1,0:T(8,128)(2,1)}, bf16[2,3,64,512]{3,2,1,0:T(8,128)(2,1)}) custom-call(s32[2,8]{1,0:T(2,128)} %assign.6, bf16[16,64,512]{2,1,0:T(8,128)(2,1)} %rest_0_.3, bf16[16,64,512]{2,1,0:T(8,128)(2,1)} %rest_1_.3, bf16[16,64,512]{2,1,0:T(8,128)(2,1)} %rest_2_.3), custom_call_target="tpu_custom_call" | custom-call | bytes 3145728 | tf_op jit(solution)/shard_map/pick/pallas_call | solution.py:106
  8.4 3.8 %collective-permute-start.1 = (bf16[2,3,64,512]{3,2,1,0:T(8,128)(2,1)}, bf16[2,3,64,512]{3,2,1,0:T(8,128)(2,1)S(1)}, u32[]{:S(2)}, u32[]{:S(2)}) collective-permute-start(bf16[2,3,64,512]{3,2,1,0:T(8,128)(2,1)} %get-tuple-element.105), channel_id=1, source_target_pairs={{0,6},{1,7},{2,4},{3,5},{4,2},{5,3},{6,0},{7,1},{8,14},{9,15},{10,... | collective-permute-start | bytes 1179656 | tf_op jit(solution)/shard_map/ppermute | solution.py:24
  12.2 3.9 %collective-permute-done.6.rest_2_ = bf16[2,3,64,512]{3,2,1,0:T(8,128)(2,1)S(1)} collective-permute-done((bf16[2,3,64,512]{3,2,1,0:T(8,128)(2,1)}, bf16[2,3,64,512]{3,2,1,0:T(8,128)(2,1)S(1)}, u32[]{:S(2)}, u32[]{:S(2)}) %collective-permute-start.6) | collective-permute-done | bytes 393248 | tf_op jit(solution)/shard_map/ppermute | solution.py:39
  22.5 3.3 %pick.3 = (bf16[2,3,64,512]{3,2,1,0:T(8,128)(2,1)}, bf16[2,3,64,512]{3,2,1,0:T(8,128)(2,1)}, bf16[2,3,64,512]{3,2,1,0:T(8,128)(2,1)}, bf16[2,3,64,512]{3,2,1,0:T(8,128)(2,1)}) custom-call(s32[2,8]{1,0:T(2,128)} %assign.6, bf16[16,64,512]{2,1,0:T(8,128)(2,1)} %rest_0_.3, bf16[16,64,512]{2,1,0:T(8,128)(2,1)} %rest_1_.3, bf16[16,64,512]{2,1,0:T(8,128)(2,1)} %rest_2_.3), custom_call_target="tpu_custom_call" | custom-call | bytes 3145728 | tf_op jit(solution)/shard_map/pick/pallas_call | solution.py:106
  25.9 4.2 %collective-permute-done.2 = bf16[2,3,64,512]{3,2,1,0:T(8,128)(2,1)S(1)} collective-permute-done((bf16[2,3,64,512]{3,2,1,0:T(8,128)(2,1)}, bf16[2,3,64,512]{3,2,1,0:T(8,128)(2,1)S(1)}, u32[]{:S(2)}, u32[]{:S(2)}) %collective-permute-start.2) | collective-permute-done | bytes 393248 | tf_op jit(solution)/shard_map/ppermute | solution.py:24
  41.8 16.8 %collective-permute-done.10 = bf16[2,3,64,512]{3,2,1,0:T(8,128)(2,1)S(1)} collective-permute-done((bf16[2,3,64,512]{3,2,1,0:T(8,128)(2,1)S(1)}, bf16[2,3,64,512]{3,2,1,0:T(8,128)(2,1)S(1)}, u32[]{:S(2)}, u32[]{:S(2)}) %collective-permute-start.10) | collective-permute-done | bytes 393248 | tf_op jit(solution)/shard_map/ppermute | solution.py:24
  58.6 3.6 %collective-permute-start.16 = (bf16[2,3,64,512]{3,2,1,0:T(8,128)(2,1)S(1)}, bf16[2,3,64,512]{3,2,1,0:T(8,128)(2,1)S(1)}, u32[]{:S(2)}, u32[]{:S(2)}) collective-permute-start(bf16[2,3,64,512]{3,2,1,0:T(8,128)(2,1)S(1)} %copy-done.59), channel_id=1, source_target_pairs={{0,6},{1,7},{2,4},{3,5},{4,2},{5,3},{6,0},{7,1},{8,14},{9,15},{10,... | collective-permute-start | bytes 1179656 | tf_op jit(solution)/shard_map/ppermute | solution.py:24
  65.8 6.7 %collective-permute-done.16 = bf16[2,3,64,512]{3,2,1,0:T(8,128)(2,1)S(1)} collective-permute-done((bf16[2,3,64,512]{3,2,1,0:T(8,128)(2,1)S(1)}, bf16[2,3,64,512]{3,2,1,0:T(8,128)(2,1)S(1)}, u32[]{:S(2)}, u32[]{:S(2)}) %collective-permute-start.16) | collective-permute-done | bytes 393248 | tf_op jit(solution)/shard_map/ppermute | solution.py:24
  72.5 7.5 %collective-permute-done.18 = bf16[2,3,64,512]{3,2,1,0:T(8,128)(2,1)S(1)} collective-permute-done((bf16[2,3,64,512]{3,2,1,0:T(8,128)(2,1)S(1)}, bf16[2,3,64,512]{3,2,1,0:T(8,128)(2,1)S(1)}, u32[]{:S(2)}, u32[]{:S(2)}) %collective-permute-start.18) | collective-permute-done | bytes 393248 | tf_op jit(solution)/shard_map/ppermute | solution.py:24
  89.0 16.5 %collective-permute-done.17 = bf16[2,3,64,512]{3,2,1,0:T(8,128)(2,1)S(1)} collective-permute-done((bf16[2,3,64,512]{3,2,1,0:T(8,128)(2,1)S(1)}, bf16[2,3,64,512]{3,2,1,0:T(8,128)(2,1)S(1)}, u32[]{:S(2)}, u32[]{:S(2)}) %collective-permute-start.17) | collective-permute-done | bytes 393248 | tf_op jit(solution)/shard_map/ppermute | solution.py:24
  111.3 12.2 %act.3 = (bf16[768,512]{1,0:T(8,128)(2,1)}, bf16[768,512]{1,0:T(8,128)(2,1)}, bf16[768,512]{1,0:T(8,128)(2,1)}) custom-call(s32[16]{0:T(128)} %counts.1, bf16[1536,2048]{1,0:T(8,128)(2,1)} %tokens.7, bf16[1536,2048]{1,0:T(8,128)(2,1)} %upstream.7, bf16[2,3,64,512]{3,2,1,0:T(8,128)(2,1)} %get-tuple-element.102.rest_0_, bf16[2,3,64,512]{3,2,1,0:T(8,128)(2,1)} %copy-done.4, ...), custom_call_target="tpu_custom_call" | custom-call | flops 4831838208 | bytes 12582912 | tf_op jit(solution)/shard_map/act/pallas_call | solution.py:181
  124.9 10.5 %weight_grads.3 = (bf16[2,3,64,512]{3,2,1,0:T(8,128)(2,1)}, bf16[2,3,64,512]{3,2,1,0:T(8,128)(2,1)}, bf16[2,3,64,512]{3,2,1,0:T(8,128)(2,1)}, bf16[2,3,64,512]{3...) custom-call(bf16[1536,2048]{1,0:T(8,128)(2,1)} %tokens.7, ...), custom_call_target="tpu_custom_call" | custom-call | flops 4831838208 | bytes 12582912 | tf_op jit(solution)/shard_map/weight_grads/pallas_call | solution.py:253
  139.4 12.3 %act.2 = (bf16[768,512]{1,0:T(8,128)(2,1)}, bf16[768,512]{1,0:T(8,128)(2,1)}, bf16[768,512]{1,0:T(8,128)(2,1)}) custom-call(s32[16]{0:T(128)} %counts.1, bf16[1536,2048]{1,0:T(8,128)(2,1)} %tokens.7, bf16[1536,2048]{1,0:T(8,128)(2,1)} %upstream.7, bf16[2,3,64,512]{3,2,1,0:T(8,128)(2,1)} %get-tuple-element.102.rest_0_, bf16[2,3,64,512]{3,2,1,0:T(8,128)(2,1)} %copy-done.4, ...), custom_call_target="tpu_custom_call" | custom-call | flops 4831838208 | bytes 12582912 | tf_op jit(solution)/shard_map/act/pallas_call | solution.py:181
  153.4 10.6 %weight_grads.2 = (bf16[2,3,64,512]{3,2,1,0:T(8,128)(2,1)}, bf16[2,3,64,512]{3,2,1,0:T(8,128)(2,1)}, bf16[2,3,64,512]{3,2,1,0:T(8,128)(2,1)}, bf16[2,3,64,512]{3...) custom-call(bf16[1536,2048]{1,0:T(8,128)(2,1)} %tokens.7, ...), custom_call_target="tpu_custom_call" | custom-call | flops 4831838208 | bytes 12582912 | tf_op jit(solution)/shard_map/weight_grads/pallas_call | solution.py:253
  167.4 5.3 %collective-permute-done.32 = bf16[4,3,64,512]{3,2,1,0:T(8,128)(2,1)S(1)} collective-permute-done((bf16[4,3,64,512]{3,2,1,0:T(8,128)(2,1)S(1)}, bf16[4,3,64,512]{3,2,1,0:T(8,128)(2,1)S(1)}, u32[]{:S(2)}, u32[]{:S(2)}) %collective-permute-start.32) | collective-permute-done | bytes 786464 | tf_op jit(solution)/shard_map/ppermute | solution.py:39
  174.8 8.2 %input_grad.2.rest_16_ = bf16[1536,2048]{1,0:T(8,128)(2,1)} custom-call(bf16[768,512]{1,0:T(8,128)(2,1)} %get-tuple-element.137.gate_grad, bf16[768,512]{1,0:T(8,128)(2,1)} %get-tuple-element.138.up_grad, bf16[2,3,64,512]{3,2,1,0:T(8,128)(2,1)} %get-tuple-element.102.rest_0_, bf16[2,3,64,512]{3,2,1,0:T(8,128)(2,1)} %copy-done.4, ...), custom_call_target="tpu_custom_call" | custom-call | flops 3221225472 | bytes 7340032 | tf_op jit(solution)/shard_map/input_grad/pallas_call | solution.py:299
  189.3 8.2 %input_grad.3 = bf16[1536,2048]{1,0:T(8,128)(2,1)} custom-call(bf16[768,512]{1,0:T(8,128)(2,1)} %get-tuple-element.135.gate_grad, bf16[768,512]{1,0:T(8,128)(2,1)} %get-tuple-element.136.up_grad, bf16[2,3,64,512]{3,2,1,0:T(8,128)(2,1)} %get-tuple-element.102.rest_0_, bf16[2,3,64,512]{3,2,1,0:T(8,128)(2,1)} %copy-done.4, ...), custom_call_target="tpu_custom_call", output_to_operand_aliasing={{}: (18, {})} | custom-call | flops 3221225472 | bytes 7340032 | tf_op jit(solution)/shard_map/input_grad/pallas_call | solution.py:299
  199.8 6.9 %collective-permute-done.44.rest_3_ = bf16[2,3,64,512]{3,2,1,0:T(8,128)(2,1)S(1)} collective-permute-done((bf16[2,3,64,512]{3,2,1,0:T(8,128)(2,1)S(1)}, bf16[2,3,64,512]{3,2,1,0:T(8,128)(2,1)S(1)}, u32[]{:S(2)}, u32[]{:S(2)}) %collective-permute-start.44) | collective-permute-done | bytes 393248 | tf_op jit(solution)/shard_map/ppermute | solution.py:24
  212.6 8.2 %place.1 = (f32[16,64,512]{2,1,0:T(8,128)}, f32[16,64,512]{2,1,0:T(8,128)}, f32[16,64,512]{2,1,0:T(8,128)}) custom-call(s32[2,8]{1,0:T(2,128)} %assign.6, bf16[2,3,64,512]{3,2,1,0:T(8,128)(2,1)} %copy-done.28, bf16[1,3,64,512]{3,2,1,0:T(8,128)(2,1)} %copy-done.45, bf16[2,3,64,512]{3,2,1,0:T(8,128)(2,1)} %copy-done.29, bf16[2,3,64,512]{3,2,1,0:T(8,128)(2,1)} %copy-done.30, ...), custom_call_target="tpu_custom_call" | custom-call | tf_op jit(solution)/shard_map/place/pallas_call | solution.py:337
  220.8 9.5 %collective-permute-done.40.rest_0_ = bf16[2,3,64,512]{3,2,1,0:T(8,128)(2,1)S(1)} collective-permute-done((bf16[2,3,64,512]{3,2,1,0:T(8,128)(2,1)S(1)}, bf16[2,3,64,512]{3,2,1,0:T(8,128)(2,1)S(1)}, u32[]{:S(2)}, u32[]{:S(2)}) %collective-permute-start.40) | collective-permute-done | bytes 393248 | tf_op jit(solution)/shard_map/ppermute | solution.py:24
  235.8 4.0 %collective-permute-done.51 = bf16[2,3,64,512]{3,2,1,0:T(8,128)(2,1)S(1)} collective-permute-done((bf16[2,3,64,512]{3,2,1,0:T(8,128)(2,1)S(1)}, bf16[2,3,64,512]{3,2,1,0:T(8,128)(2,1)S(1)}, u32[]{:S(2)}, u32[]{:S(2)}) %collective-permute-start.51) | collective-permute-done | bytes 393248 | tf_op jit(solution)/shard_map/ppermute | solution.py:39
  240.4 6.1 %collective-permute-done.56 = bf16[2,3,64,512]{3,2,1,0:T(8,128)(2,1)S(1)} collective-permute-done((bf16[2,3,64,512]{3,2,1,0:T(8,128)(2,1)S(1)}, bf16[2,3,64,512]{3,2,1,0:T(8,128)(2,1)S(1)}, u32[]{:S(2)}, u32[]{:S(2)}) %collective-permute-start.56) | collective-permute-done | bytes 393248 | tf_op jit(solution)/shard_map/ppermute | solution.py:39
  248.7 5.1 %collective-permute-done.47.rest_3_ = bf16[2,3,64,512]{3,2,1,0:T(8,128)(2,1)S(1)} collective-permute-done((bf16[2,3,64,512]{3,2,1,0:T(8,128)(2,1)S(1)}, bf16[2,3,64,512]{3,2,1,0:T(8,128)(2,1)S(1)}, u32[]{:S(2)}, u32[]{:S(2)}) %collective-permute-start.47) | collective-permute-done | bytes 393248 | tf_op jit(solution)/shard_map/ppermute | solution.py:24
  257.0 5.8 %finish.1 = (f32[16,64,512]{2,1,0:T(8,128)}, f32[16,64,512]{2,1,0:T(8,128)}, f32[16,64,512]{2,1,0:T(8,128)}) custom-call(s32[2,8]{1,0:T(2,128)} %assign.6, bf16[2,3,64,512]{3,2,1,0:T(8,128)(2,1)} %copy-done.25, bf16[1,3,64,512]{3,2,1,0:T(8,128)(2,1)} %copy-done.46, ...), custom_call_target="tpu_custom_call", output_to_operand_aliasing={{0}: (10, {}), {1}: (11, {}), {2}: (12, {})} | custom-call | tf_op jit(solution)/shard_map/finish/pallas_call | solution.py:393
  (264 shorter events, 78.9 us)
Async XLA Ops:
  34.8 23.7 %collective-permute-start.11 = (bf16[4,3,64,512]{3,2,1,0:T(8,128)(2,1)S(1)}, bf16[4,3,64,512]{3,2,1,0:T(8,128)(2,1)S(1)}, u32[]{:S(2)}, u32[]{:S(2)}) collective-permute-start(bf16[4,3,64,512]{3,2,1,0:T(8,128)(2,1)S(1)} %pad_maximum_fusion.rest_8_), channel_id=1, source_target_pairs={{0,8},{1,17},{2,10},{3,19},{4,12},{5,21},{6,14},{7,23},{8,0},{9,25... | collective-permute-start | bytes 2359304 | tf_op jit(solution)/shard_map/ppermute | solution.py:39
  36.7 25.5 %collective-permute-start.9 = (bf16[4,3,64,512]{3,2,1,0:T(8,128)(2,1)S(1)}, bf16[4,3,64,512]{3,2,1,0:T(8,128)(2,1)S(1)}, u32[]{:S(2)}, u32[]{:S(2)}) collective-permute-start(bf16[4,3,64,512]{3,2,1,0:T(8,128)(2,1)S(1)} %pad_maximum_fusion.rest_8_), channel_id=1, source_target_pairs={{0,16},{1,9},{2,18},{3,11},{4,20},{5,13},{6,22},{7,15},{8,24},{9,1... | collective-permute-start | bytes 2359304 | tf_op jit(solution)/shard_map/ppermute | solution.py:39
  38.5 20.1 %collective-permute-start.10 = (bf16[2,3,64,512]{3,2,1,0:T(8,128)(2,1)S(1)}, bf16[2,3,64,512]{3,2,1,0:T(8,128)(2,1)S(1)}, u32[]{:S(2)}, u32[]{:S(2)}) collective-permute-start(bf16[2,3,64,512]{3,2,1,0:T(8,128)(2,1)S(1)} %copy-done.61), channel_id=1, source_target_pairs={{0,4},{1,5},{2,6},{3,7},{4,0},{5,1},{6,2},{7,3},{8,12},{9,13},{10,... | collective-permute-start | bytes 1179656 | tf_op jit(solution)/shard_map/ppermute | solution.py:24
  41.3 20.9 %collective-permute-start.12 = (bf16[2,3,64,512]{3,2,1,0:T(8,128)(2,1)S(1)}, bf16[2,3,64,512]{3,2,1,0:T(8,128)(2,1)S(1)}, u32[]{:S(2)}, u32[]{:S(2)}) collective-permute-start(bf16[2,3,64,512]{3,2,1,0:T(8,128)(2,1)S(1)} %collective-permute-done.4.rest_5_), channel_id=1, source_target_pairs={{0,16},{1,9},{2,18},{3,11},{4,20},{5,13},{6,22},{7,15},{8,24},{9,1... | collective-permute-start | bytes 1179656 | tf_op jit(solution)/shard_map/ppermute | solution.py:39
  62.3 20.5 %collective-permute-start.15 = (bf16[4,3,64,512]{3,2,1,0:T(8,128)(2,1)S(1)}, bf16[4,3,64,512]{3,2,1,0:T(8,128)(2,1)S(1)}, u32[]{:S(2)}, u32[]{:S(2)}) collective-permute-start(bf16[4,3,64,512]{3,2,1,0:T(8,128)(2,1)S(1)} %collective-permute-done.11.rest_9_), channel_id=1, source_target_pairs={{0,16},{1,9},{2,18},{3,11},{4,20},{5,13},{6,22},{7,15},{8,24},{9,1... | collective-permute-start | bytes 2359304 | tf_op jit(solution)/shard_map/ppermute | solution.py:39
  64.7 18.1 %collective-permute-start.19 = (bf16[2,3,64,512]{3,2,1,0:T(8,128)(2,1)S(1)}, bf16[2,3,64,512]{3,2,1,0:T(8,128)(2,1)S(1)}, u32[]{:S(2)}, u32[]{:S(2)}) collective-permute-start(bf16[2,3,64,512]{3,2,1,0:T(8,128)(2,1)S(1)} %pad_maximum_fusion.3.rest_12_), channel_id=1, source_target_pairs={{0,16},{1,9},{2,18},{3,11},{4,20},{5,13},{6,22},{7,15},{8,24},{9,1... | collective-permute-start | bytes 1179656 | tf_op jit(solution)/shard_map/ppermute | solution.py:39
  84.7 23.9 %collective-permute-start.21 = (bf16[4,3,64,512]{3,2,1,0:T(8,128)(2,1)S(1)}, bf16[4,3,64,512]{3,2,1,0:T(8,128)(2,1)S(1)}, u32[]{:S(2)}, u32[]{:S(2)}) collective-permute-start(bf16[4,3,64,512]{3,2,1,0:T(8,128)(2,1)S(1)} %pad_maximum_fusion.1.rest_8_), channel_id=1, source_target_pairs={{0,8},{1,17},{2,10},{3,19},{4,12},{5,21},{6,14},{7,23},{8,0},{9,25... | collective-permute-start | bytes 2359304 | tf_op jit(solution)/shard_map/ppermute | solution.py:39
  85.1 23.5 %collective-permute-start.23 = (bf16[4,3,64,512]{3,2,1,0:T(8,128)(2,1)S(1)}, bf16[4,3,64,512]{3,2,1,0:T(8,128)(2,1)S(1)}, u32[]{:S(2)}, u32[]{:S(2)}) collective-permute-start(bf16[4,3,64,512]{3,2,1,0:T(8,128)(2,1)S(1)} %pad_maximum_fusion.1.rest_8_), channel_id=1, source_target_pairs={{0,16},{1,9},{2,18},{3,11},{4,20},{5,13},{6,22},{7,15},{8,24},{9,1... | collective-permute-start | bytes 2359304 | tf_op jit(solution)/shard_map/ppermute | solution.py:39
  85.6 19.9 %collective-permute-start.17 = (bf16[2,3,64,512]{3,2,1,0:T(8,128)(2,1)S(1)}, bf16[2,3,64,512]{3,2,1,0:T(8,128)(2,1)S(1)}, u32[]{:S(2)}, u32[]{:S(2)}) collective-permute-start(bf16[2,3,64,512]{3,2,1,0:T(8,128)(2,1)S(1)} %copy-done.56), channel_id=1, source_target_pairs={{0,4},{1,5},{2,6},{3,7},{4,0},{5,1},{6,2},{7,3},{8,12},{9,13},{10,... | collective-permute-start | bytes 1179656 | tf_op jit(solution)/shard_map/ppermute | solution.py:24
  87.8 20.7 %collective-permute-start.22 = (bf16[2,3,64,512]{3,2,1,0:T(8,128)(2,1)S(1)}, bf16[2,3,64,512]{3,2,1,0:T(8,128)(2,1)S(1)}, u32[]{:S(2)}, u32[]{:S(2)}) collective-permute-start(bf16[2,3,64,512]{3,2,1,0:T(8,128)(2,1)S(1)} %collective-permute-done.14.rest_13_), channel_id=1, source_target_pairs={{0,16},{1,9},{2,18},{3,11},{4,20},{5,13},{6,22},{7,15},{8,24},{9,1... | collective-permute-start | bytes 1179656 | tf_op jit(solution)/shard_map/ppermute | solution.py:39
  108.8 26.7 %collective-permute-start.25 = (bf16[4,3,64,512]{3,2,1,0:T(8,128)(2,1)S(1)}, bf16[4,3,64,512]{3,2,1,0:T(8,128)(2,1)S(1)}, u32[]{:S(2)}, u32[]{:S(2)}) collective-permute-start(bf16[4,3,64,512]{3,2,1,0:T(8,128)(2,1)S(1)} %collective-permute-done.21.rest_9_), channel_id=1, source_target_pairs={{0,16},{1,9},{2,18},{3,11},{4,20},{5,13},{6,22},{7,15},{8,24},{9,1... | collective-permute-start | bytes 2359304 | tf_op jit(solution)/shard_map/ppermute | solution.py:39
  110.5 25.0 %collective-permute-start.27 = (bf16[2,3,64,512]{3,2,1,0:T(8,128)(2,1)S(1)}, bf16[2,3,64,512]{3,2,1,0:T(8,128)(2,1)S(1)}, u32[]{:S(2)}, u32[]{:S(2)}) collective-permute-start(bf16[2,3,64,512]{3,2,1,0:T(8,128)(2,1)S(1)} %pad_maximum_fusion.5.rest_12_), channel_id=1, source_target_pairs={{0,16},{1,9},{2,18},{3,11},{4,20},{5,13},{6,22},{7,15},{8,24},{9,1... | collective-permute-start | bytes 1179656 | tf_op jit(solution)/shard_map/ppermute | solution.py:39
  137.6 26.3 %collective-permute-start.34 = (bf16[4,3,64,512]{3,2,1,0:T(8,128)(2,1)}, bf16[4,3,64,512]{3,2,1,0:T(8,128)(2,1)S(1)}, u32[]{:S(2)}, u32[]{:S(2)}) collective-permute-start(bf16[4,3,64,512]{3,2,1,0:T(8,128)(2,1)} %get-tuple-element.156), channel_id=1, source_target_pairs={{0,8},{1,17},{2,10},{3,19},{4,12},{5,21},{6,14},{7,23},{8,0},{9,25... | collective-permute-start | bytes 2359304 | tf_op jit(solution)/shard_map/ppermute | solution.py:39
  152.7 20.0 %collective-permute-start.32 = (bf16[4,3,64,512]{3,2,1,0:T(8,128)(2,1)S(1)}, bf16[4,3,64,512]{3,2,1,0:T(8,128)(2,1)S(1)}, u32[]{:S(2)}, u32[]{:S(2)}) collective-permute-start(bf16[4,3,64,512]{3,2,1,0:T(8,128)(2,1)S(1)} %copy-done.51), channel_id=1, source_target_pairs={{0,8},{1,17},{2,10},{3,19},{4,12},{5,21},{6,14},{7,23},{8,0},{9,25... | collective-permute-start | bytes 2359304 | tf_op jit(solution)/shard_map/ppermute | solution.py:39
  164.2 21.0 %collective-permute-start.36 = (bf16[4,3,64,512]{3,2,1,0:T(8,128)(2,1)S(1)}, bf16[4,3,64,512]{3,2,1,0:T(8,128)(2,1)S(1)}, u32[]{:S(2)}, u32[]{:S(2)}) collective-permute-start(bf16[4,3,64,512]{3,2,1,0:T(8,128)(2,1)S(1)} %add_convert_fusion.3), channel_id=1, source_target_pairs={{0,16},{1,9},{2,18},{3,11},{4,20},{5,13},{6,22},{7,15},{8,24},{9,1... | collective-permute-start | bytes 2359304 | tf_op jit(solution)/shard_map/ppermute | solution.py:39
  165.7 18.3 %collective-permute-start.38 = (bf16[2,3,64,512]{3,2,1,0:T(8,128)(2,1)S(1)}, bf16[2,3,64,512]{3,2,1,0:T(8,128)(2,1)S(1)}, u32[]{:S(2)}, u32[]{:S(2)}) collective-permute-start(bf16[2,3,64,512]{3,2,1,0:T(8,128)(2,1)S(1)} %add_convert_fusion.8), channel_id=1, source_target_pairs={{0,4},{1,5},{2,6},{3,7},{4,0},{5,1},{6,2},{7,3},{8,12},{9,13},{10,... | collective-permute-start | bytes 1179656 | tf_op jit(solution)/shard_map/ppermute | solution.py:24
  184.0 23.7 %collective-permute-start.41 = (bf16[4,3,64,512]{3,2,1,0:T(8,128)(2,1)S(1)}, bf16[4,3,64,512]{3,2,1,0:T(8,128)(2,1)S(1)}, u32[]{:S(2)}, u32[]{:S(2)}) collective-permute-start(bf16[4,3,64,512]{3,2,1,0:T(8,128)(2,1)S(1)} %copy-done.50), channel_id=1, source_target_pairs={{0,8},{1,17},{2,10},{3,19},{4,12},{5,21},{6,14},{7,23},{8,0},{9,25... | collective-permute-start | bytes 2359304 | tf_op jit(solution)/shard_map/ppermute | solution.py:39
  188.1 18.6 %collective-permute-start.44 = (bf16[2,3,64,512]{3,2,1,0:T(8,128)(2,1)S(1)}, bf16[2,3,64,512]{3,2,1,0:T(8,128)(2,1)S(1)}, u32[]{:S(2)}, u32[]{:S(2)}) collective-permute-start(bf16[2,3,64,512]{3,2,1,0:T(8,128)(2,1)S(1)} %get-tuple-element.173), channel_id=1, source_target_pairs={{0,2},{1,3},{2,0},{3,1},{4,6},{5,7},{6,4},{7,5},{8,10},{9,11},{10,... | collective-permute-start | bytes 1179656 | tf_op jit(solution)/shard_map/ppermute | solution.py:24
  188.2 19.8 %collective-permute-start.37 = (bf16[2,3,64,512]{3,2,1,0:T(8,128)(2,1)S(1)}, bf16[2,3,64,512]{3,2,1,0:T(8,128)(2,1)S(1)}, u32[]{:S(2)}, u32[]{:S(2)}) collective-permute-start(bf16[2,3,64,512]{3,2,1,0:T(8,128)(2,1)S(1)} %add_convert_fusion.10), channel_id=1, source_target_pairs={{0,16},{1,9},{2,18},{3,11},{4,20},{5,13},{6,22},{7,15},{8,24},{9,1... | collective-permute-start | bytes 1179656 | tf_op jit(solution)/shard_map/ppermute | solution.py:39
  206.7 23.6 %collective-permute-start.45 = (bf16[4,3,64,512]{3,2,1,0:T(8,128)(2,1)S(1)}, bf16[4,3,64,512]{3,2,1,0:T(8,128)(2,1)S(1)}, u32[]{:S(2)}, u32[]{:S(2)}) collective-permute-start(bf16[4,3,64,512]{3,2,1,0:T(8,128)(2,1)S(1)} %copy-done.49), channel_id=1, source_target_pairs={{0,8},{1,17},{2,10},{3,19},{4,12},{5,21},{6,14},{7,23},{8,0},{9,25... | collective-permute-start | bytes 2359304 | tf_op jit(solution)/shard_map/ppermute | solution.py:39
  208.0 24.4 %collective-permute-start.42 = (bf16[4,3,64,512]{3,2,1,0:T(8,128)(2,1)S(1)}, bf16[4,3,64,512]{3,2,1,0:T(8,128)(2,1)S(1)}, u32[]{:S(2)}, u32[]{:S(2)}) collective-permute-start(bf16[4,3,64,512]{3,2,1,0:T(8,128)(2,1)S(1)} %add_convert_fusion.1), channel_id=1, source_target_pairs={{0,16},{1,9},{2,18},{3,11},{4,20},{5,13},{6,22},{7,15},{8,24},{9,1... | collective-permute-start | bytes 2359304 | tf_op jit(solution)/shard_map/ppermute | solution.py:39
  210.0 20.3 %collective-permute-start.40 = (bf16[2,3,64,512]{3,2,1,0:T(8,128)(2,1)S(1)}, bf16[2,3,64,512]{3,2,1,0:T(8,128)(2,1)S(1)}, u32[]{:S(2)}, u32[]{:S(2)}) collective-permute-start(bf16[2,3,64,512]{3,2,1,0:T(8,128)(2,1)S(1)} %add_convert_fusion.9), channel_id=1, source_target_pairs={{0,4},{1,5},{2,6},{3,7},{4,0},{5,1},{6,2},{7,3},{8,12},{9,13},{10,... | collective-permute-start | bytes 1179656 | tf_op jit(solution)/shard_map/ppermute | solution.py:24
  210.6 20.7 %collective-permute-start.48 = (bf16[2,3,64,512]{3,2,1,0:T(8,128)(2,1)S(1)}, bf16[2,3,64,512]{3,2,1,0:T(8,128)(2,1)S(1)}, u32[]{:S(2)}, u32[]{:S(2)}) collective-permute-start(bf16[2,3,64,512]{3,2,1,0:T(8,128)(2,1)S(1)} %copy-done.54), channel_id=1, source_target_pairs={{0,8},{1,17},{2,10},{3,19},{4,12},{5,21},{6,14},{7,23},{8,0},{9,25... | collective-permute-start | bytes 1179656 | tf_op jit(solution)/shard_map/ppermute | solution.py:39
  235.7 18.0 %collective-permute-start.47 = (bf16[2,3,64,512]{3,2,1,0:T(8,128)(2,1)S(1)}, bf16[2,3,64,512]{3,2,1,0:T(8,128)(2,1)S(1)}, u32[]{:S(2)}, u32[]{:S(2)}) collective-permute-start(bf16[2,3,64,512]{3,2,1,0:T(8,128)(2,1)S(1)} %get-tuple-element.176), channel_id=1, source_target_pairs={{0,2},{1,3},{2,0},{3,1},{4,6},{5,7},{6,4},{7,5},{8,10},{9,11},{10,... | collective-permute-start | bytes 1179656 | tf_op jit(solution)/shard_map/ppermute | solution.py:24
  (97 other events, 1222.0 us)
